TPU v7x, 256 devices: a whole 4x4x8 slice. The times are simulated.
256 devices in a mesh: seq: 32 (over x_hi, z, core), head: 8 (over x_lo, y).
Axes of the slice: x: 4 (x_hi: 2, x_lo: 2; x = x_hi * 2 + x_lo), y: 4, z: 8, core: 2. Of those that a mesh axis runs over, the one named last changes fastest.
Arguments:
- queries: bfloat16 [64, 32, 4096], P('seq', None, 'head'), may hold values from -39 to 39
- new_kv: bfloat16 [64, 32, 2, 1024], P('seq', None, None, 'head'), may hold values from -6 to 6
- cache: bfloat16 [32, 4096, 2, 1024], P('seq', None, None, 'head'), may hold values from -6 to 6
- sinks: bfloat16 [32, 4, 2, 1024], P(None, None, None, 'head'), may hold values from -16 to 16
- lengths: int32 [32], replicated, may hold values from 6 to 32768, as said below
- offsets: int32 [32], replicated, may hold values from 0 to 4095
- order: int32 [32], replicated, may hold values from 0 to 31, as said below
- residual: bfloat16 [64, 32, 4096], P('seq', None, 'head'), may hold values from -16 to 16
- o_weight: bfloat16 [4096, 4096], P('head', 'seq'), may hold values from -0.1875 to 0.1875
- ffn_gain: float32 [4096], P('head'), may hold values from 0.1 to 1.9
- router: float32 [4096, 8], P('head'), may hold values from -0.09375 to 0.09375
- expert_ids: int32 [64, 32, 2], P('seq'), may hold values from 0 to 7, all different within a row; in each aligned block of 64 rows (0 to 63, 64 to 127, ..., all dimensions but the last counted through in order) at most 18 rows name the same one
- w_in: bfloat16 [8, 4096, 2, 8192], P('head', None, None, 'seq'), may hold values from -0.09375 to 0.09375
- w_out: bfloat16 [8, 8192, 4096], P('head', 'seq'), may hold values from -0.0625 to 0.0625
Outputs:
- layer_out: bfloat16 [64, 32, 4096], P('seq', None, 'head')
- cache_out: bfloat16 [32, 4096, 2, 1024], P('seq', None, None, 'head')
Inputs may be any that keep to these rules, and one draw needn't show every extreme that they name: `lengths`: one request has exactly 32768 cached tokens and one exactly 6; the others are spread below 1024, 4096 and 32768. `order`: a permutation. `expert_ids`: each row names two different experts; among the 64 rows of one index of seq (an aligned block of the flattened token grid of 64 x 32) no expert is named more than 18 times.
All inputs are finite; a program needn't handle non-finite values.
Results may differ from a plain program's by a relative error of at most 0.015.
Values may be sent and summed in bfloat16 or wider, within the bound.
No kernel may reach another device: no remote copies, remote signals or barrier semaphores. Data moves between devices by JAX's collectives and lax.ppermute only.
A program may use at most 64 MiB of HBM per device.

v0:
```python
import jax
import jax.numpy as jnp
from jax import lax
from jax.sharding import PartitionSpec as P

D = 4096
HD = 128
E = 8
CAP = 18


def split_pair(kv_rows, kv_local):
    row_count = kv_rows.shape[0]
    key_rows = kv_rows[:, 0].reshape(row_count, kv_local, HD).transpose(1, 0, 2)
    value_rows = kv_rows[:, 1].reshape(row_count, kv_local, HD).transpose(1, 0, 2)
    return (key_rows, value_rows)


def shards(
    queries,
    new_kv,
    cache,
    sinks,
    lengths,
    offsets,
    order,
    residual,
    o_weight,
    ffn_gain,
    router,
    expert_ids,
    w_in,
    w_out,
):
    seq_count = lax.axis_size("seq")
    seq_index = lax.axis_index("seq")
    part_rows, batch_slots, query_width = queries.shape
    kv_width = new_kv.shape[3]
    kv_local = kv_width // HD
    group_size = query_width // kv_width
    cycle_len = cache.shape[1]
    span_len = part_rows * seq_count
    sink_len = sinks.shape[1]
    score_scale = HD ** (-0.5)
    slot_iota = jnp.arange(batch_slots, dtype=jnp.int32)
    inverse = jnp.sum(jnp.where(order[None, :] == slot_iota[:, None], slot_iota[None, :], 0), 1)
    query_req = jnp.take(queries, inverse, axis=1)
    kv_req = jnp.take(new_kv, inverse, axis=1)
    query_block, span_block = (
        lax.all_to_all(query_req, "seq", split_axis=1, concat_axis=0, tiled=True),
        lax.all_to_all(kv_req, "seq", split_axis=1, concat_axis=0, tiled=True),
    )
    cycle_block = cache[0]
    length = lengths[seq_index]
    offset = offsets[seq_index]
    sink_rows = sinks[seq_index]
    span_rows = span_block[:, 0]
    query_mat = query_block.reshape(span_len, kv_local, group_size, HD).transpose(1, 0, 2, 3)
    query_mat = query_mat.reshape(kv_local, span_len * group_size, HD)
    token_pos = jnp.arange(span_len * group_size, dtype=jnp.int32) // group_size
    first_keys, first_values = split_pair(jnp.concatenate([sink_rows, span_rows], 0), kv_local)
    first_live = jnp.concatenate(
        [
            jnp.ones((token_pos.shape[0], sink_len), dtype=bool),
            jnp.arange(span_len, dtype=jnp.int32)[None, :] <= token_pos[:, None],
        ],
        1,
    )
    scores = (
        jnp.einsum("grd,gnd->grn", query_mat, first_keys, preferred_element_type=jnp.float32)
        * score_scale
    )
    scores = jnp.where(first_live[None], scores, -jnp.inf)
    row_max = jnp.max(scores, -1)
    expo = jnp.exp(scores - row_max[..., None])
    total = jnp.sum(expo, -1)
    accum = jnp.einsum(
        "grn,gnd->grd", expo.astype(jnp.bfloat16), first_values, preferred_element_type=jnp.float32
    )
    block_len = min(512, cycle_len)
    block_total = cycle_len // block_len

    def cycle_step(block_index, carry):
        first_slot = block_index * block_len
        cycle_rows = lax.dynamic_slice_in_dim(cycle_block, first_slot, block_len, 0)
        cycle_age = (first_slot + jnp.arange(block_len, dtype=jnp.int32) - offset) % cycle_len
        filled = cycle_age >= cycle_len - length + sink_len

        def attend(state):
            run_max, run_total, run_accum = state
            key_rows, value_rows = split_pair(cycle_rows, kv_local)
            block_scores = (
                jnp.einsum("grd,gnd->grn", query_mat, key_rows, preferred_element_type=jnp.float32)
                * score_scale
            )
            allowed = filled[None, :] & (cycle_age[None, :] > token_pos[:, None])
            block_scores = jnp.where(allowed[None], block_scores, -jnp.inf)
            new_max = jnp.maximum(run_max, jnp.max(block_scores, -1))
            factor = jnp.exp(run_max - new_max)
            block_expo = jnp.exp(block_scores - new_max[..., None])
            new_total = run_total * factor + jnp.sum(block_expo, -1)
            new_accum = run_accum * factor[..., None] + jnp.einsum(
                "grn,gnd->grd",
                block_expo.astype(jnp.bfloat16),
                value_rows,
                preferred_element_type=jnp.float32,
            )
            return (new_max, new_total, new_accum)

        def skip_block(state):
            return state

        return lax.cond(jnp.any(filled), attend, skip_block, carry)

    row_max, total, accum = lax.fori_loop(0, block_total, cycle_step, (row_max, total, accum))
    mixed = (
        (accum / total[..., None]).reshape(kv_local, span_len, group_size, HD).transpose(1, 0, 2, 3)
    )
    mixed = mixed.reshape(span_len, 1, query_width).astype(jnp.bfloat16)
    attn_rows = lax.all_to_all(mixed, "seq", split_axis=0, concat_axis=1, tiled=True)
    row_total = part_rows * batch_slots
    flat_attn = attn_rows.reshape(row_total, query_width)
    projected = jnp.dot(
        flat_attn,
        lax.all_gather(o_weight, "seq", axis=1, tiled=True),
        preferred_element_type=jnp.float32,
    )
    projected = lax.psum_scatter(projected, "head", scatter_dimension=1, tiled=True)
    model_part = projected.shape[1]
    residual_req = jnp.take(residual, inverse, axis=1)
    hidden_sum = residual_req.reshape(row_total, model_part).astype(jnp.float32) + projected
    gained = hidden_sum * ffn_gain
    square_part = jnp.sum(hidden_sum * hidden_sum, -1)
    square_total = lax.psum(square_part, "head")
    inv_rms = lax.rsqrt(square_total / D + 1e-05)
    scaled_part = jnp.dot(gained * inv_rms[:, None], router, precision=lax.Precision.HIGHEST)
    logits = lax.psum(scaled_part, "head")
    normed = (gained * inv_rms[:, None]).astype(jnp.bfloat16)
    picks = jnp.take(expert_ids, inverse, axis=1).reshape(row_total, 2)
    expert_iota = jnp.arange(E, dtype=jnp.int32)
    first_hot = picks[:, 0:1] == expert_iota[None, :]
    second_hot = picks[:, 1:2] == expert_iota[None, :]
    first_logit = jnp.sum(jnp.where(first_hot, logits, 0.0), -1)
    second_logit = jnp.sum(jnp.where(second_hot, logits, 0.0), -1)
    gate_one = jax.nn.sigmoid(first_logit - second_logit).astype(jnp.bfloat16)
    gate_two = jax.nn.sigmoid(second_logit - first_logit).astype(jnp.bfloat16)
    both_hot = (first_hot | second_hot).astype(jnp.int32)
    earlier = jnp.cumsum(both_hot, 0) - both_hot
    code_one = jnp.sum(jnp.where(first_hot, earlier, 0), -1) * E + picks[:, 0]
    code_two = jnp.sum(jnp.where(second_hot, earlier, 0), -1) * E + picks[:, 1]
    bucket_iota = jnp.arange(CAP * E, dtype=jnp.int32)
    codes = jnp.stack([code_one, code_two], 1)
    all_normed, all_codes = (
        lax.all_gather(normed, "seq", axis=0, tiled=True),
        lax.all_gather(codes, "seq", axis=0, tiled=True),
    )
    all_normed = all_normed.reshape(seq_count, row_total, model_part)
    all_codes = all_codes.reshape(seq_count, row_total, 2)
    spread = ((all_codes[:, :, 0:1] == bucket_iota) | (all_codes[:, :, 1:2] == bucket_iota)).astype(
        jnp.bfloat16
    )
    bucket = jnp.einsum(
        "nrb,nrd->nbd", spread, all_normed, preferred_element_type=jnp.float32
    ).astype(jnp.bfloat16)
    bucket = bucket.reshape(seq_count * CAP, E, model_part)
    expert_in = lax.all_to_all(bucket, "head", split_axis=1, concat_axis=2, tiled=True)
    gate_up = jnp.einsum("red,edkf->rekf", expert_in, w_in, preferred_element_type=jnp.float32)
    inner = (jax.nn.silu(gate_up[:, :, 0]) * gate_up[:, :, 1]).astype(jnp.bfloat16)
    summed = lax.psum_scatter(
        jnp.einsum("ref,efd->red", inner, w_out, preferred_element_type=jnp.float32).astype(
            jnp.bfloat16
        ),
        "seq",
        scatter_dimension=0,
        tiled=True,
    )
    returned = lax.all_to_all(summed, "head", split_axis=2, concat_axis=1, tiled=True)
    zero_gate = jnp.zeros((), jnp.bfloat16)
    weigh = jnp.where(code_one[:, None] == bucket_iota[None, :], gate_one[:, None], zero_gate)
    weigh = weigh + jnp.where(
        code_two[:, None] == bucket_iota[None, :], gate_two[:, None], zero_gate
    )
    mixture = jnp.dot(
        weigh, returned.reshape(CAP * E, model_part), preferred_element_type=jnp.float32
    )
    layer_out = (
        (hidden_sum + mixture).astype(jnp.bfloat16).reshape(part_rows, batch_slots, model_part)
    )
    token_of = (jnp.arange(cycle_len, dtype=jnp.int32) - offset) % cycle_len
    picked = jnp.take(span_rows, jnp.minimum(token_of, span_len - 1), axis=0)
    cache_out = jnp.where((token_of < span_len)[:, None, None], picked, cycle_block)[None]
    return (layer_out, cache_out)


def solution(mesh):
    return jax.shard_map(
        shards,
        mesh=mesh,
        in_specs=(
            P("seq", None, "head"),
            P("seq", None, None, "head"),
            P("seq", None, None, "head"),
            P(None, None, None, "head"),
            P(),
            P(),
            P(),
            P("seq", None, "head"),
            P("head", "seq"),
            P("head"),
            P("head", None),
            P("seq", None, None),
            P("head", None, None, "seq"),
            P("head", "seq", None),
        ),
        out_specs=(P("seq", None, "head"), P("seq", None, None, "head")),
        check_vma=False,
    )
```

profile of v0, /device:TPU:2, one launch (start us, length us, event | category | flops | bytes accessed | tf_op | source)
XLA Modules:
  0.0 578.6 jit_solution(15877360856352066303)
XLA Ops:
  8.7 1.4 gather_fusion
  10.8 10.4 %all-to-all-start.1 = ((bf16[2,32,2,128]{3,2,0,1:T(2,128)(2,1)}), bf16[2,32,2,128]{3,2,0,1:T(2,128)(2,1)S(1)}, u32[]{:S(2)}, u32[]{:S(2)}) async-start(bf16[2,32,2,128]{3,2,0,1:T(2,128)(2,1)} %fusion.46), calls=%async_computation.1 | async-start | bytes 65536 | tf_op jit(solution)/shard_map/all_to_all | solution.py:51
  21.3 1.6 gather_fusion.3
  22.9 1.6 gather_fusion.4
  25.4 6.0 %all-to-all-done.1 = bf16[2,32,2,128]{3,2,0,1:T(2,128)(2,1)S(1)} async-done(((bf16[2,32,2,128]{3,2,0,1:T(2,128)(2,1)}), bf16[2,32,2,128]{3,2,0,1:T(2,128)(2,1)S(1)}, u32[]{:S(2)}, u32[]{:S(2)}) %all-to-all-start.1) | async-done | bytes 32800 | tf_op jit(solution)/shard_map/all_to_all | solution.py:51
  31.4 3.9 all-to-all-start
  36.0 1.3 dynamic_slice.22
  37.3 1.2 dynamic_slice.23
  38.5 3.2 copy.98
  42.3 4.1 all-to-all-done
  47.0 36.4 %while.20 = (s32[]{:T(128)}, f32[1,256]{1,0:T(1,128)S(1)}, f32[1,256]{1,0:T(1,128)S(1)}, f32[1,256,128]{2,1,0:T(8,128)S(1)}, s32[]{:T(128)}, /*index=5*/s32[]{:T...) while((s32[]{:T(128)}, f32[1,256]{1,0:T(1,128)S(1)}, ...), condition=%wide.region_9.11_spmd.clone, body=%wide.region_3.10_spmd.clone.sunk | while | flops 68370944 | bytes 2192765 | solution.py:115
  47.0 1.3 fusion.78
  49.5 2.6 conditional.3
  50.9 1.2 fusion.5
  52.2 1.3 fusion.78
  54.7 2.6 conditional.3
  57.4 1.3 fusion.78
  59.9 2.6 conditional.3
  62.6 1.3 fusion.78
  65.2 2.6 conditional.3
  67.8 1.3 fusion.78
  70.4 1.3 fusion.78
  73.0 1.3 fusion.78
  75.6 2.6 conditional.3
  76.9 1.2 fusion.5
  78.2 1.3 fusion.78
  80.8 2.6 conditional.3
  82.2 1.2 fusion.5
  85.2 20.2 %all_to_all.63 = bf16[32,2,512]{2,1,0:T(2,128)(2,1)S(1)} all-to-all(bf16[32,2,512]{2,1,0:T(2,128)(2,1)S(1)} %reshape.378), channel_id=1, replica_groups=mesh['seq'=32,'head'=8] {'seq'}, dimensions={0} | all-to-all | bytes 131072 | tf_op jit(solution)/shard_map/all_to_all | solution.py:120
  106.0 4.0 fusion.69
  110.0 35.7 %reduce-scatter.5.cloned.1.call-done = f32[64,512]{1,0:T(8,128)} async-done(((f32[64,4096]{1,0:T(8,128)}), f32[64,512]{1,0:T(8,128)}) %reduce-scatter.5.cloned.1.call-update) | async-done | bytes 131088 | tf_op jit(solution)/shard_map/reduce_scatter | solution.py:128
  146.7 17.5 %psum.14 = f32[64]{0:T(128)S(1)} all-reduce(f32[64]{0:T(128)S(1)} %get-tuple-element.408), channel_id=1, replica_groups=mesh['seq'=32,'head'=8] {'head'}, use_global_device_ids=true, to_apply=%region_14.16 | all-reduce | flops 64 | bytes 512 | tf_op jit(solution)/shard_map/psum | solution.py:134
  166.3 41.2 %all-gather = s32[32,64,2]{1,2,0:T(2,128)S(1)} all-gather(s32[1,64,2]{1,2,0:T(2,128)S(1)} %add_bitcast_fusion), channel_id=1, replica_groups=mesh['seq'=32,'head'=8] {'seq'}, dimensions={0}, use_global_device_ids=true | all-gather | bytes 16896 | tf_op jit(solution)/shard_map/all_gather | solution.py:155
  207.5 36.1 %all-gather.6.cloned.1.call-done = bf16[2048,512]{1,0:T(8,128)(2,1)} async-done(((bf16[64,512]{1,0:T(8,128)(2,1)}), bf16[2048,512]{1,0:T(8,128)(2,1)}) %all-gather.6.cloned.1.call-update) | async-done | bytes 2097168 | tf_op jit(solution)/shard_map/all_gather | solution.py:154
  243.6 3.8 convolution_convert_fusion.1
  247.4 3.9 copy.73
  251.3 6.1 %all-to-all-start.3 = ((bf16[576,8,512]{2,0,1:T(8,128)(2,1)}), bf16[576,8,512]{2,0,1:T(8,128)(2,1)}, u32[]{:S(2)}, u32[]{:S(2)}) async-start(bf16[576,8,512]{2,0,1:T(8,128)(2,1)} %copy.73), calls=%async_computation.4 | async-start | bytes 9437184 | tf_op jit(solution)/shard_map/all_to_all | solution.py:166
  260.0 27.2 %gather_fusion.2 = bf16[4096,2,128]{2,1,0:T(2,128)(2,1)} fusion(bf16[64,2,128]{2,1,0:T(2,128)(2,1)S(1)} %bitcast.144, s32[4096]{0:T(1024)S(1)} %broadcast_clamp_fusion), kind=kCustom, calls=%fused_computation.4 | custom fusion | bytes 4210688 | tf_op jit(solution)/shard_map/jit(_take)/gather | solution.py:190
  287.2 24.6 %all-to-all-done.3 = bf16[576,8,512]{2,0,1:T(8,128)(2,1)} async-done(((bf16[576,8,512]{2,0,1:T(8,128)(2,1)}), bf16[576,8,512]{2,0,1:T(8,128)(2,1)}, u32[]{:S(2)}, u32[]{:S(2)}) %all-to-all-start.3) | async-done | bytes 4718624 | tf_op jit(solution)/shard_map/all_to_all | solution.py:166
  311.8 7.1 %copy.74 = bf16[576,8,512]{2,1,0:T(8,128)(2,1)} copy(bf16[576,8,512]{2,0,1:T(8,128)(2,1)} %all-to-all-done.3) | data formatting | bytes 9437184 | tf_op jit(solution)/shard_map/all_to_all | solution.py:166
  318.9 8.3 %reshape.372 = bf16[576,4096,1]{1,0,2:T(8,128)(2,1)} reshape(bf16[576,8,512]{2,1,0:T(8,128)(2,1)} %copy.74) | data formatting | bytes 9437184 | tf_op jit(solution)/shard_map/reshape.34
  327.2 5.9 %fusion.21 = f32[576,1,2,256]{3,0,2,1:T(8,128)S(1)} fusion(bf16[576,4096,1]{1,0,2:T(8,128)(2,1)} %reshape.372, bf16[4096,2,256]{2,1,0:T(2,128)(2,1)} %bitcast.168), kind=kOutput, calls=%fused_computation.42 | convolution fusion | flops 2415919104 | bytes 10092544 | tf_op jit(solution)/shard_map/red,edkf->rekf/dot_general | solution.py:167
  333.1 3.6 fusion.15
  336.6 81.4 %fusion.2 = bf16[24,4096]{1,0:T(8,128)(2,1)S(1)} fusion(bf16[576,1,4096]{2,0,1:T(8,128)(2,1)} %fusion.15), kind=kCustom, calls=%all-reduce-scatter | all-reduce-scatter fusion | flops 3145729 | bytes 4916224
  418.1 1.3 collective-permute-start
  419.4 1.3 collective-permute-start.1
  420.7 1.3 collective-permute-start.7
  422.0 21.1 %broadcast_select_fusion = bf16[1,4096,2,128]{3,2,1,0:T(2,128)(2,1)} fusion(bf16[1,4096,2,128]{3,2,1,0:T(2,128)(2,1)} %param.22, pred[4096]{0:T(1024)(128)(4,1)S(1)} %get-tuple-element.427, pred[4096]{0:T(1024)(128)(4,1)S(1)} %get-tuple-element.426, bf16[4096,2,128]{2,1,0:T(2,128)(2,1)} %gather_fusion.2), kind=kLoop, calls=%fused_computation.34 | loop fusion | flops 2097152 | bytes 6299648 | tf_op jit(solution)/shard_map/jit(_where)/select_n | solution.py:191
  443.1 2.5 collective-permute-start.2
  445.6 11.7 %collective-permute-start.3 = (bf16[24,4096]{1,0:T(8,128)(2,1)S(1)}, bf16[24,4096]{1,0:T(8,128)(2,1)S(1)}, u32[]{:S(2)}, u32[]{:S(2)}) collective-permute-start(bf16[24,4096]{1,0:T(8,128)(2,1)S(1)} %fusion.2), channel_id=1, source_target_pairs={{0,32},{8,40},{16,48},{24,56},{32,64},{40,72},{48,80},{56,88},{64,... | collective-permute-start | bytes 589832
  457.3 2.3 collective-permute-start.4
  459.7 2.7 collective-permute-start.5
  462.4 2.0 collective-permute-start.6
  464.7 18.2 %psum.15 = f32[64,8]{0,1:T(8,128)S(1)} all-reduce(f32[64,8]{0,1:T(8,128)S(1)} %fusion.32), channel_id=1, replica_groups=mesh['seq'=32,'head'=8] {'head'}, use_global_device_ids=true, to_apply=%region_15.17 | all-reduce | flops 512 | bytes 4096 | tf_op jit(solution)/shard_map/psum | solution.py:137
  483.0 2.6 collective-permute-done.5
  485.5 11.3 %collective-permute-done.6 = bf16[24,4096]{1,0:T(8,128)(2,1)} collective-permute-done((bf16[24,4096]{1,0:T(8,128)(2,1)S(1)}, bf16[24,4096]{1,0:T(8,128)(2,1)}, u32[]{:S(2)}, u32[]{:S(2)}) %collective-permute-start.6) | collective-permute-done | bytes 196640
  496.8 24.6 %concatenate.8 = bf16[210,4096]{1,0:T(8,128)(2,1)} concatenate(bf16[18,4096]{1,0:T(8,128)(2,1)S(1)} %collective-permute-done.7, bf16[24,4096]{1,0:T(8,128)(2,1)} %collective-permute-done.6, bf16[24,4096]{1,0:T(8,128)(2,1)} %collective-permute-done.5, bf16[24,4096]{1,0:T(8,128)(2,1)} %collective-permute-done.4, bf16[24,4096]{1,0:T(8,128)(2,1)S(1)} %collective-permute-done.3, ...), dimensions={0} | concatenate | bytes 3440640
  522.5 3.9 copy.76
  526.3 23.5 %reduce.12 = bf16[4096,18]{1,0:T(8,128)(2,1)S(1)} reduce(bf16[4096,1,18]{2,1,0:T(2,128)(2,1)} %bitcast.146, bf16[]{:T(256)} %broadcast.349), dimensions={1}, to_apply=%bitcast.126.reduce_sub_computation | reduce | bytes 294914
  549.8 2.6 reshape.380
  552.4 4.4 all-to-all-start.4
  556.9 5.3 all-to-all-done.4
  562.2 4.2 reshape.381
  566.4 4.6 copy.77
  (145 shorter events, 30.9 us)
Async XLA Ops:
  7.2 325.9 %copy-start = (bf16[1,256,4096]{2,1,0:T(8,128)(2,1)S(1)}, bf16[1,256,4096]{2,1,0:T(8,128)(2,1)}, u32[]{:S(2)}) copy-start(bf16[1,256,4096]{2,1,0:T(8,128)(2,1)} %param.33) | copy-start | bytes 6291460
  7.2 98.8 %all-gather.4.cloned.1.call-start = ((), (), s32[]{:S(2)}) async-start(), calls=%async_computation.6 | async-start | bytes 4325376 | tf_op jit(solution)/shard_map/all_gather | solution.py:125
  10.8 20.5 %all-to-all-start.1 = ((bf16[2,32,2,128]{3,2,0,1:T(2,128)(2,1)}), bf16[2,32,2,128]{3,2,0,1:T(2,128)(2,1)S(1)}, u32[]{:S(2)}, u32[]{:S(2)}) async-start(bf16[2,32,2,128]{3,2,0,1:T(2,128)(2,1)} %fusion.46), calls=%async_computation.1 | async-start | bytes 65536 | tf_op jit(solution)/shard_map/all_to_all | solution.py:51
  31.4 15.0 %all-to-all-start = ((bf16[2,32,512]{2,0,1:T(2,128)(2,1)}), bf16[2,32,512]{2,0,1:T(2,128)(2,1)S(1)}, u32[]{:S(2)}, u32[]{:S(2)}) async-start(bf16[2,32,512]{2,0,1:T(2,128)(2,1)} %copy.65), calls=%async_computation | async-start | bytes 131072 | tf_op jit(solution)/shard_map/all_to_all | solution.py:50
  35.2 110.5 %reduce-scatter.5.cloned.1.call-start = ((), (), s32[]{:S(2)}) async-start(), calls=%async_computation.7 | async-start | bytes 1179648 | tf_op jit(solution)/shard_map/reduce_scatter | solution.py:128
  105.9 58.3 %copy-start.2 = (f32[512]{0:T(512)S(1)}, f32[512]{0:T(512)}, u32[]{:S(2)}) copy-start(f32[512]{0:T(512)} %param.29) | copy-start | bytes 6148
  106.0 59.1 %copy-start.3 = (s32[2,32,2]{1,2,0:T(2,128)S(1)}, s32[2,32,2]{1,2,0:T(2,128)}, u32[]{:S(2)}) copy-start(s32[2,32,2]{1,2,0:T(2,128)} %param.31) | copy-start | bytes 1540
  110.0 133.6 %all-gather.6.cloned.1.call-start = ((), (), s32[]{:S(2)}) async-start(), calls=%async_computation.8 | async-start | bytes 2162688 | tf_op jit(solution)/shard_map/all_gather | solution.py:154
  251.3 6.1 %copy-start.4 = (u32[256]{0:T(256)S(1)}, u32[256]{0:T(256)}, u32[]{:S(2)}) copy-start(u32[256]{0:T(256)} %constant.224) | copy-start | bytes 3076
  251.3 60.5 %all-to-all-start.3 = ((bf16[576,8,512]{2,0,1:T(8,128)(2,1)}), bf16[576,8,512]{2,0,1:T(8,128)(2,1)}, u32[]{:S(2)}, u32[]{:S(2)}) async-start(bf16[576,8,512]{2,0,1:T(8,128)(2,1)} %copy.73), calls=%async_computation.4 | async-start | bytes 9437184 | tf_op jit(solution)/shard_map/all_to_all | solution.py:166
  418.1 41.6 %collective-permute-start = (bf16[24,4096]{1,0:T(8,128)(2,1)S(1)}, bf16[24,4096]{1,0:T(8,128)(2,1)S(1)}, u32[]{:S(2)}, u32[]{:S(2)}) collective-permute-start(bf16[24,4096]{1,0:T(8,128)(2,1)S(1)} %fusion.2), channel_id=1, source_target_pairs={{0,8},{8,16},{16,24},{24,32},{32,40},{40,48},{48,56},{56,64},{64,7... | collective-permute-start | bytes 589832
  419.4 43.0 %collective-permute-start.1 = (bf16[24,4096]{1,0:T(8,128)(2,1)S(1)}, bf16[24,4096]{1,0:T(8,128)(2,1)S(1)}, u32[]{:S(2)}, u32[]{:S(2)}) collective-permute-start(bf16[24,4096]{1,0:T(8,128)(2,1)S(1)} %fusion.2), channel_id=1, source_target_pairs={{0,16},{8,24},{16,32},{24,40},{32,48},{40,56},{48,64},{56,72},{64,... | collective-permute-start | bytes 589832
  420.7 36.6 %collective-permute-start.7 = (bf16[18,4096]{1,0:T(8,128)(2,1)S(1)}, bf16[18,4096]{1,0:T(8,128)(2,1)S(1)}, u32[]{:S(2)}, u32[]{:S(2)}) collective-permute-start(bf16[18,4096]{1,0:T(8,128)(2,1)S(1)} %slice.60), channel_id=1, source_target_pairs={{0,64},{8,72},{16,80},{24,88},{32,96},{40,104},{48,112},{56,120},{... | collective-permute-start | bytes 442376
  422.0 42.5 %copy-start.1 = (f32[512,8]{0,1:T(8,128)S(1)}, f32[512,8]{0,1:T(8,128)}, u32[]{:S(2)}) copy-start(f32[512,8]{0,1:T(8,128)} %param.30) | copy-start | bytes 49156
  443.1 39.9 %collective-permute-start.2 = (bf16[24,4096]{1,0:T(8,128)(2,1)S(1)}, bf16[24,4096]{1,0:T(8,128)(2,1)S(1)}, u32[]{:S(2)}, u32[]{:S(2)}) collective-permute-start(bf16[24,4096]{1,0:T(8,128)(2,1)S(1)} %fusion.2), channel_id=1, source_target_pairs={{0,24},{8,32},{16,40},{24,48},{32,56},{40,64},{48,72},{56,80},{64,... | collective-permute-start | bytes 589832
  445.6 37.3 %collective-permute-start.3 = (bf16[24,4096]{1,0:T(8,128)(2,1)S(1)}, bf16[24,4096]{1,0:T(8,128)(2,1)S(1)}, u32[]{:S(2)}, u32[]{:S(2)}) collective-permute-start(bf16[24,4096]{1,0:T(8,128)(2,1)S(1)} %fusion.2), channel_id=1, source_target_pairs={{0,32},{8,40},{16,48},{24,56},{32,64},{40,72},{48,80},{56,88},{64,... | collective-permute-start | bytes 589832
  457.3 25.6 %collective-permute-start.4 = (bf16[24,4096]{1,0:T(8,128)(2,1)S(1)}, bf16[24,4096]{1,0:T(8,128)(2,1)}, u32[]{:S(2)}, u32[]{:S(2)}) collective-permute-start(bf16[24,4096]{1,0:T(8,128)(2,1)S(1)} %fusion.2), channel_id=1, source_target_pairs={{0,40},{8,48},{16,56},{24,64},{32,72},{40,80},{48,88},{56,96},{64,... | collective-permute-start | bytes 589832
  459.7 25.9 %collective-permute-start.5 = (bf16[24,4096]{1,0:T(8,128)(2,1)S(1)}, bf16[24,4096]{1,0:T(8,128)(2,1)}, u32[]{:S(2)}, u32[]{:S(2)}) collective-permute-start(bf16[24,4096]{1,0:T(8,128)(2,1)S(1)} %fusion.2), channel_id=1, source_target_pairs={{0,48},{8,56},{16,64},{24,72},{32,80},{40,88},{48,96},{56,104},{64... | collective-permute-start | bytes 589832
  462.4 34.4 %collective-permute-start.6 = (bf16[24,4096]{1,0:T(8,128)(2,1)S(1)}, bf16[24,4096]{1,0:T(8,128)(2,1)}, u32[]{:S(2)}, u32[]{:S(2)}) collective-permute-start(bf16[24,4096]{1,0:T(8,128)(2,1)S(1)} %fusion.2), channel_id=1, source_target_pairs={{0,56},{8,64},{16,72},{24,80},{32,88},{40,96},{48,104},{56,112},{6... | collective-permute-start | bytes 589832
  552.4 9.7 %all-to-all-start.4 = ((bf16[8,2,4608]{2,1,0:T(2,128)(2,1)}), bf16[8,2,4608]{2,1,0:T(2,128)(2,1)S(1)}, u32[]{:S(2)}, u32[]{:S(2)}) async-start(bf16[8,2,4608]{2,1,0:T(2,128)(2,1)} %reshape.380), calls=%async_computation.5 | async-start | bytes 294912 | tf_op jit(solution)/shard_map/all_to_all | solution.py:177
Sparse Core Ops, SparseCore 0:
  10.6 89.2 all-gather.3
  110.1 35.5 reduce-scatter.4
  165.1 78.4 all-gather.5
where the time goes:
time: 589 us; the launch traced here: 579 us
  blocking collectives  178 us (30%)
  waiting for transfers between devices  126 us (21%)
  local copies, waits for them, and re-layouts  102 us (17%)
  other arithmetic  67.5 us (11%)
  starting transfers between devices  50.1 us (9%)
  matrix products  33.2 us (6%)
  between operations  15.4 us (3%)
    unnamed x1, blocking collectives  81.4 us
    all_gather x1, blocking collectives, shards(): lax.all_gather(codes, 'seq', axis=0, tiled=True)  41.2 us
    unnamed x20, local copies, waits for them, and re-layouts  36.6 us
    all_gather x1, waiting for transfers between devices, shards(): lax.all_gather(normed, 'seq', axis=0, tiled=True)  36.1 us
    reduce_scatter x1, waiting for transfers between devices, shards(): lax.psum_scatter(projected, 'head', scatter_dimension=1, tiled=True)  35.7 us
    gather x1, local copies, waits for them, and re-layouts, shards(): picked = jnp.take(span_rows, jnp.minimum(token_of, span_len - 1), axis=0)  27.2 us
    unnamed x8, starting transfers between devices  25.2 us
    all_to_all x1, waiting for transfers between devices, shards(): lax.all_to_all(bucket, 'head', split_axis=1, concat_axis=2, tiled=True)  24.6 us
  transfers between devices with their start and end apart: 15, of which 8 were waited for; matrix products, arithmetic and copies ran while one was open for 17% of the time, Pallas kernels for 0%

commit v1 on v0

v1 whole, which is shorter than its diff:
```python
import functools

import jax
import jax.numpy as jnp
from jax import lax
from jax.experimental import pallas as pl
from jax.experimental.pallas import tpu as pltpu
from jax.sharding import Mesh
from jax.sharding import PartitionSpec as P

D = 4096
HD = 128
E = 8
CAP = 18
SLOT = 24
NZ = 8
BF = jnp.bfloat16
F32 = jnp.float32
VMEM = pl.BlockSpec(memory_space=pltpu.VMEM)
SMEM = pl.BlockSpec(memory_space=pltpu.SMEM)
SEQ = ("xh", "z", "c")
HEAD = ("xl", "y")


def call(body, outs, name, n_in, scalars=0, flops=0, nbytes=0, limit=32, scratch=()):
    return pl.pallas_call(
        body,
        out_shape=outs,
        in_specs=[SMEM] * scalars + [VMEM] * (n_in - scalars),
        out_specs=jax.tree.map(lambda _: VMEM, outs),
        scratch_shapes=list(scratch),
        compiler_params=pltpu.CompilerParams(vmem_limit_bytes=limit << 20),
        cost_estimate=pl.CostEstimate(
            flops=flops, bytes_accessed=nbytes, transcendentals=0
        ),
        name=name,
    )


def shape(*dims, dtype=BF):
    return jax.ShapeDtypeStruct(dims, dtype)


def dot(a, b):
    return jnp.dot(a, b, preferred_element_type=F32)


def dot_t(a, b):
    return lax.dot_general(a, b, (((1,), (1,)), ((), ())), preferred_element_type=F32)


def slot_of_request(order_row):
    n = order_row.shape[1]
    return order_row == lax.broadcasted_iota(jnp.int32, (n, n), 0)


def permute_body(order_ref, q_ref, kv_ref, out_ref):
    hot = jnp.where(slot_of_request(order_ref[...]), 1.0, 0.0).astype(BF)
    for i in range(q_ref.shape[0]):
        out_ref[i, :, 0:512] = dot(hot, q_ref[i]).astype(BF)
        out_ref[i, :, 512:768] = dot(hot, kv_ref[i]).astype(BF)


def split_body(cache_ref, k_ref, v_ref, wide):
    rows = cache_ref.shape[0]
    wide[...] = cache_ref[...].astype(F32)
    k_ref[...] = wide[pl.ds(0, rows // 2, stride=2), :].astype(BF)
    v_ref[...] = wide[pl.ds(1, rows // 2, stride=2), :].astype(BF)


def split_cycle(cache_rows):
    rows, step = cache_rows.shape[0], 2048
    return pl.pallas_call(
        split_body,
        grid=(rows // step,),
        out_shape=[shape(rows // 2, HD)] * 2,
        in_specs=[pl.BlockSpec((step, HD), lambda n: (n, 0))],
        out_specs=[pl.BlockSpec((step // 2, HD), lambda n: (n, 0))] * 2,
        scratch_shapes=[pltpu.VMEM((step, HD), F32)],
        cost_estimate=pl.CostEstimate(
            flops=1 << 24, bytes_accessed=8 << 20, transcendentals=0
        ),
        name="split_cycle",
    )(cache_rows)


CHUNK = 512


def attend_body(
    seq_ref, len_ref, off_ref, rows_ref, k_ref, v_ref, sink_ref, out_ref, scores, wide
):
    seq = seq_ref[0]
    length, offset = len_ref[seq], off_ref[seq]
    span = rows_ref.shape[0]
    cycle = k_ref.shape[0]
    group = 4
    query = jnp.concatenate(
        [rows_ref[:, g * HD : (g + 1) * HD] for g in range(group)], 0
    )
    count = span * group
    scale = HD**-0.5
    token = lax.broadcasted_iota(jnp.int32, (count, 1), 0) % span
    oldest = jnp.maximum(token + 1, cycle - length + 4)
    wide[...] = sink_ref[seq].astype(F32)
    pad = jnp.zeros((span - 4, HD), F32)
    first_k = jnp.concatenate(
        [
            jnp.concatenate([wide[pl.ds(0, 4, stride=2), :], pad], 0).astype(BF),
            rows_ref[:, 4 * HD : 5 * HD],
        ],
        0,
    )
    first_v = jnp.concatenate(
        [
            jnp.concatenate([wide[pl.ds(1, 4, stride=2), :], pad], 0).astype(BF),
            rows_ref[:, 5 * HD : 6 * HD],
        ],
        0,
    )
    column = lax.broadcasted_iota(jnp.int32, (1, 2 * span), 1)
    live = (column < 4) | ((column >= span) & (column - span <= token))
    low = jnp.float32(-jnp.inf)
    first = jnp.where(live, dot_t(query, first_k), low)
    peak = first
    for n in range(cycle // CHUNK):
        part = dot_t(query, k_ref[n * CHUNK : (n + 1) * CHUNK, :])
        age = lax.broadcasted_iota(jnp.int32, (1, CHUNK), 1) + (n * CHUNK - offset)
        age = jnp.where(age < 0, age + cycle, age)
        part = jnp.where(age >= oldest, part, low)
        scores[:, n * CHUNK : (n + 1) * CHUNK] = part
        for m in range(CHUNK // HD):
            peak = jnp.maximum(peak, part[:, m * HD : (m + 1) * HD])
    top = jnp.max(peak, 1, keepdims=True)
    expo = jnp.exp((first - top) * scale)
    total = expo
    acc = dot(expo.astype(BF), first_v)
    for n in range(cycle // CHUNK):
        expo = jnp.exp((scores[:, n * CHUNK : (n + 1) * CHUNK] - top) * scale)
        for m in range(CHUNK // HD):
            total = total + expo[:, m * HD : (m + 1) * HD]
        acc = acc + dot(expo.astype(BF), v_ref[n * CHUNK : (n + 1) * CHUNK, :])
    mixed = acc / jnp.sum(total, 1, keepdims=True)
    for g in range(group):
        out_ref[:, g * HD : (g + 1) * HD] = mixed[g * span : (g + 1) * span].astype(BF)


def write_body(seq_ref, off_ref, rows_ref, cache_ref, out_ref):
    offset = off_ref[seq_ref[0]]
    step = cache_ref.shape[0]
    span = rows_ref.shape[0]
    cycle = step * pl.num_programs(0) // 2
    row = lax.broadcasted_iota(jnp.int32, (step, 1), 0) + pl.program_id(0) * step
    age = row // 2 - offset
    age = jnp.where(age < 0, age + cycle, age)
    column = lax.broadcasted_iota(jnp.int32, (1, 2 * span), 1)
    hot = jnp.where(age + (row % 2) * span == column, 1.0, 0.0)
    hot = jnp.where(age < span, hot, 0.0).astype(BF)
    new = jnp.concatenate(
        [rows_ref[:, 4 * HD : 5 * HD], rows_ref[:, 5 * HD : 6 * HD]], 0
    )
    fresh = dot(hot, new)
    out_ref[...] = jnp.where(age < span, fresh, cache_ref[...].astype(F32)).astype(BF)


def write_cycle(seq, offsets, rows, cache_rows):
    total, step = cache_rows.shape[0], 1024
    return pl.pallas_call(
        write_body,
        grid=(total // step,),
        out_shape=shape(total, HD),
        in_specs=[
            SMEM,
            SMEM,
            pl.BlockSpec(rows.shape, lambda n: (0, 0)),
            pl.BlockSpec((step, HD), lambda n: (n, 0)),
        ],
        out_specs=pl.BlockSpec((step, HD), lambda n: (n, 0)),
        cost_estimate=pl.CostEstimate(
            flops=1 << 28, bytes_accessed=8 << 20, transcendentals=0
        ),
        name="write_cycle",
    )(seq, offsets, rows, cache_rows)


def project_body(core_ref, own_ref, other_ref, w_ref, out_ref):
    first = core_ref[0] == 0
    own, other = own_ref[...], other_ref[...]
    rows = own.shape[0]
    own32, other32 = own.astype(F32), other.astype(F32)
    both = jnp.concatenate(
        [jnp.where(first, own32, other32), jnp.where(first, other32, own32)], 0
    ).astype(BF)
    weight = jnp.concatenate([w_ref[0, 0], w_ref[1, 0]], 1)
    result = dot(both, weight).astype(BF)
    out_ref[0, 0] = result[:rows]
    out_ref[1, 0] = result[rows:]


def project(core, own, other, weight):
    rows = own.shape[0]
    return pl.pallas_call(
        project_body,
        grid=(8,),
        out_shape=shape(2, 8, rows, 256),
        in_specs=[
            SMEM,
            pl.BlockSpec(own.shape, lambda h: (0, 0)),
            pl.BlockSpec(own.shape, lambda h: (0, 0)),
            pl.BlockSpec((2, 1, 512, 128), lambda h: (h % 4, h // 4, 0, 0)),
        ],
        out_specs=pl.BlockSpec((2, 1, rows, 256), lambda h: (0, h, 0, 0)),
        cost_estimate=pl.CostEstimate(
            flops=1 << 28, bytes_accessed=3 << 20, transcendentals=0
        ),
        name="project",
    )(core, own, other, weight)


def pieces(value):
    high = value.astype(BF).astype(F32)
    rest = value - high
    middle = rest.astype(BF).astype(F32)
    return high, middle, (rest - middle).astype(BF).astype(F32)


def dispatch_body(
    order_ref,
    part_ref,
    res_ref,
    gain_ref,
    router_ref,
    ids_ref,
    ids_t_ref,
    hidden_ref,
    code_ref,
    send_ref,
):
    hot = jnp.where(slot_of_request(order_ref[...]), 1.0, 0.0).astype(BF)
    resid = jnp.concatenate([dot(hot, res_ref[i]) for i in range(2)], 0)
    picks = jnp.concatenate(
        [dot(hot, ids_ref[i].astype(F32).astype(BF)) for i in range(2)], 0
    )
    picks_t = jnp.concatenate(
        [dot_t(ids_t_ref[i].astype(F32).astype(BF), hot) for i in range(2)], 1
    )
    sums = []
    for c in range(2):
        total = part_ref[c * 8].astype(F32)
        for h in range(1, 8):
            total = total + part_ref[c * 8 + h].astype(F32)
        sums.append(total)
    projected = jnp.concatenate(
        [sums[0][:, :HD], sums[1][:, :HD], sums[0][:, HD:], sums[1][:, HD:]], 1
    )
    hidden = resid + projected
    hidden_ref[...] = hidden
    gained = hidden * gain_ref[...]
    square = jnp.sum(hidden * hidden, 1, keepdims=True)
    share = jnp.dot(
        gained,
        router_ref[...],
        precision=lax.Precision.HIGHEST,
        preferred_element_type=F32,
    )
    rows = hidden.shape[0]
    one, two = picks[:, 0:1], picks[:, 1:2]
    expert = lax.broadcasted_iota(jnp.int32, (1, E), 1).astype(F32)
    first, second = one == expert, two == expert
    apart = jnp.sum(jnp.where(first, share, 0.0) - jnp.where(second, share, 0.0), 1, keepdims=True)
    before = lax.broadcasted_iota(jnp.int32, (rows, rows), 0)
    after = lax.broadcasted_iota(jnp.int32, (rows, rows), 1)
    lower = jnp.where(before > after, 1.0, 0.0).astype(BF)
    upper = jnp.where(before < after, 1.0, 0.0).astype(BF)
    earlier = dot(lower, jnp.where(first | second, 1.0, 0.0).astype(BF))
    slot_one = jnp.sum(jnp.where(first, earlier, 0.0), 1, keepdims=True)
    slot_two = jnp.sum(jnp.where(second, earlier, 0.0), 1, keepdims=True)
    lane = lax.broadcasted_iota(jnp.int32, (rows, HD), 1)
    code_ref[...] = jnp.where(
        lane == 0, one * SLOT + slot_one, two * SLOT + slot_two
    ).astype(jnp.int32)
    one_t, two_t = picks_t[0:1], picks_t[1:2]
    expert_t = lax.broadcasted_iota(jnp.int32, (E, 1), 0).astype(F32)
    first_t, second_t = one_t == expert_t, two_t == expert_t
    earlier_t = dot(jnp.where(first_t | second_t, 1.0, 0.0).astype(BF), upper)
    slot_one_t = jnp.sum(jnp.where(first_t, earlier_t, 0.0), 0, keepdims=True)
    slot_two_t = jnp.sum(jnp.where(second_t, earlier_t, 0.0), 0, keepdims=True)
    place = lax.broadcasted_iota(jnp.int32, (E * SLOT, 1), 0).astype(F32)
    is_one = jnp.where(place == one_t * SLOT + slot_one_t, 1.0, 0.0)
    is_two = jnp.where(place == two_t * SLOT + slot_two_t, 1.0, 0.0)
    plus, minus = (is_one + is_two).astype(BF), (is_one - is_two).astype(BF)
    bucket = dot(plus, gained.astype(BF)).astype(BF)
    norm_terms, gate_terms = jnp.zeros((rows, HD), F32), jnp.zeros((rows, HD), F32)
    for n, (s, a) in enumerate(zip(pieces(square), pieces(apart))):
        norm_terms = jnp.where(lane == n, s, norm_terms)
        gate_terms = jnp.where(lane == 3 + n, a, gate_terms)
    terms = (dot(plus, norm_terms.astype(BF)) + dot(minus, gate_terms.astype(BF))).astype(BF)
    for e in range(E):
        for x in range(2):
            send_ref[x * E + e, :, 0:512] = bucket[e * SLOT : e * SLOT + CAP]
            send_ref[x * E + e, :, 512:640] = terms[e * SLOT : e * SLOT + CAP]


def norm_body(got_ref, x_ref, gate_ref):
    target = lax.broadcasted_iota(jnp.int32, (2 * CAP, CAP), 0)
    source = lax.broadcasted_iota(jnp.int32, (2 * CAP, CAP), 1)
    put = [jnp.where(target == source + CAP * x, 1.0, 0.0).astype(BF) for x in range(2)]
    terms = jnp.zeros((2 * CAP, HD), F32)
    for h in range(8):
        for x in range(2):
            terms = terms + dot(put[x], got_ref[x * 8 + h, :, 512:640])
    lane = lax.broadcasted_iota(jnp.int32, (2 * CAP, HD), 1)
    square = jnp.sum(jnp.where(lane < 3, terms, 0.0), 1, keepdims=True)
    apart = jnp.sum(jnp.where((lane >= 3) & (lane < 6), terms, 0.0), 1, keepdims=True)
    inv_rms = lax.rsqrt(square / D + 1e-05)
    gate = 1.0 / (1.0 + jnp.exp(-(apart * inv_rms)))
    gate_ref[...] = jnp.broadcast_to(gate.astype(BF).astype(F32), gate_ref.shape)
    for h in range(8):
        part = dot(put[0], got_ref[h, :, 0:512]) + dot(put[1], got_ref[8 + h, :, 0:512])
        x_ref[:, h * 512 : (h + 1) * 512] = (part * inv_rms).astype(BF)


ROWS = 2 * CAP
PAD = 48


def expert_body(*refs):
    x_refs, refs = refs[:9], refs[9:]
    own_ref, other_ref, down_ref, other_down_ref = refs[:4]
    out_refs, (x, inner) = refs[4:13], refs[13:]
    step = pl.program_id(0)

    @pl.when(step == 0)
    def _():
        for n in range(7):
            x[n * PAD : n * PAD + ROWS, :] = x_refs[n][...]
        x[7 * PAD : 7 * PAD + ROWS, : D // 2] = x_refs[7][...]
        x[7 * PAD : 7 * PAD + ROWS, D // 2 :] = x_refs[8][...]

    for n, w_ref in ((0, own_ref), (1, other_ref)):

        @pl.when(step == n)
        def _(n=n, w_ref=w_ref):
            gate, up = dot(x[...], w_ref[0]), dot(x[...], w_ref[1])
            inner[:, n * 256 : (n + 1) * 256] = (
                gate / (1.0 + jnp.exp(-gate)) * up
            ).astype(BF)

    @pl.when(step >= 2)
    def _():
        result = dot(inner[:, :256], down_ref[...]) + dot(inner[:, 256:], other_down_ref[...])
        result = result.astype(BF)
        for n in range(7):
            out_refs[n][...] = result[n * PAD : n * PAD + ROWS]
        last = result[7 * PAD : 7 * PAD + ROWS]

        @pl.when(step < 4)
        def _():
            out_refs[7][...] = last

        @pl.when(step >= 4)
        def _():
            out_refs[8][...] = last


def expert(blocks, own, other, down, other_down):
    width = 1024
    column = lambda j: (0, jnp.maximum(j - 2, 0))
    left = lambda j: (0, jnp.clip(j - 2, 0, 1))
    right = lambda j: (0, jnp.maximum(j - 4, 0))
    whole = lambda a: pl.BlockSpec(a.shape, lambda j: (0,) * a.ndim)
    wide = pl.BlockSpec((ROWS, width), column)
    return pl.pallas_call(
        expert_body,
        grid=(6,),
        out_shape=[shape(ROWS, D)] * 7 + [shape(ROWS, D // 2)] * 2,
        in_specs=[whole(b) for b in blocks]
        + [whole(own), whole(other)]
        + [pl.BlockSpec((256, width), column)] * 2,
        out_specs=[wide] * 7
        + [pl.BlockSpec((ROWS, width), left), pl.BlockSpec((ROWS, width), right)],
        scratch_shapes=[pltpu.VMEM((8 * PAD, D), BF), pltpu.VMEM((8 * PAD, 512), BF)],
        compiler_params=pltpu.CompilerParams(vmem_limit_bytes=48 << 20),
        cost_estimate=pl.CostEstimate(
            flops=4 << 30, bytes_accessed=18 << 20, transcendentals=0
        ),
        name="expert",
    )(*blocks, own, other, down, other_down)


def gate_body(own_ref, right_ref, left_ref, gate_ref, send_ref):
    target = lax.broadcasted_iota(jnp.int32, (CAP, ROWS), 0)
    source = lax.broadcasted_iota(jnp.int32, (CAP, ROWS), 1)
    take = [jnp.where(target + CAP * x == source, 1.0, 0.0).astype(BF) for x in range(2)]
    for h in range(8):
        cut = slice(h * 512, (h + 1) * 512)
        total = own_ref[:, cut].astype(F32) + right_ref[:, cut].astype(F32)
        total = (total + left_ref[:, cut].astype(F32)) * gate_ref[:, 0:1]
        total = total.astype(BF)
        for x in range(2):
            send_ref[x * 8 + h] = dot(take[x], total).astype(BF)


def combine_body(hidden_ref, code_ref, got_ref, out_ref):
    total = hidden_ref[...]
    rows = total.shape[0]
    one, two = code_ref[:, 0:1], code_ref[:, 1:2]
    lane = lax.broadcasted_iota(jnp.int32, (rows, CAP), 1)
    for e in range(E):
        at = lane + e * SLOT
        hot = jnp.where((one == at) | (two == at), 1.0, 0.0).astype(BF)
        total = total + dot(hot, got_ref[e]) + dot(hot, got_ref[8 + e])
    out_ref[0] = total[: rows // 2].astype(BF)
    out_ref[1] = total[rows // 2 :].astype(BF)


def shards(
    queries,
    new_kv,
    cache,
    sinks,
    lengths,
    offsets,
    order,
    residual,
    o_weight,
    ffn_gain,
    router,
    expert_ids,
    w_in,
    w_out,
):
    seq = lax.axis_index(SEQ).astype(jnp.int32).reshape(1)
    core = lax.axis_index("c").astype(jnp.int32).reshape(1)
    swap = [(0, 1), (1, 0)]
    right = [(i, (i + 1) % NZ) for i in range(NZ)]
    left = [(i, (i - 1) % NZ) for i in range(NZ)]
    order_row = order.reshape(1, -1)

    o_other = lax.ppermute(o_weight, "xh", swap)
    low = lax.axis_index("xh") == 0
    o_pair = jnp.stack(
        [jnp.where(low, o_weight, o_other), jnp.where(low, o_other, o_weight)], 0
    )
    o_all = lax.all_gather(o_pair, "z", axis=0, tiled=False)

    kv = new_kv.reshape(2, 32, 256)
    asked = call(permute_body, shape(2, 32, 768), "permute", 3)(order_row, queries, kv)
    rows = lax.all_to_all(asked, SEQ, split_axis=1, concat_axis=0, tiled=True)
    rows = rows.reshape(64, 768)

    cache_rows = cache.reshape(8192, HD)
    keys, values = split_cycle(cache_rows)
    attended = call(
        attend_body,
        shape(64, 512),
        "attend",
        7,
        scalars=3,
        flops=1 << 30,
        nbytes=2 << 20,
        scratch=[pltpu.VMEM((256, 4096), F32), pltpu.VMEM((8, HD), F32)],
    )(seq, lengths, offsets, rows, keys, values, sinks.reshape(32, 8, HD))
    cache_out = write_cycle(seq, offsets, rows, cache_rows).reshape(cache.shape)

    w_in, w_out = w_in[0], w_out[0]
    w_in_other = lax.ppermute(w_in, "c", swap)
    w_out_other = lax.ppermute(w_out, "c", swap)
    w_own, w_other = w_in.transpose(1, 0, 2), w_in_other.transpose(1, 0, 2)

    owned = lax.all_to_all(
        attended.reshape(64, 1, 512), SEQ, split_axis=0, concat_axis=1, tiled=True
    )
    owned = owned.reshape(64, 512)
    owned_other = lax.ppermute(owned, "c", swap)
    share = project(core, owned, owned_other, o_all)
    share = lax.all_to_all(
        share.reshape(16, 64, 256), ("c",) + HEAD, split_axis=0, concat_axis=0, tiled=True
    )
    ids_t = expert_ids.transpose(0, 2, 1)
    hidden, codes, send = call(
        dispatch_body,
        [shape(64, 512, dtype=F32), shape(64, HD, dtype=jnp.int32), shape(16, CAP, 640)],
        "dispatch",
        7,
        flops=1 << 26,
        nbytes=2 << 20,
    )(order_row, share, residual, ffn_gain.reshape(1, -1), router, expert_ids, ids_t)
    got = lax.all_to_all(send, ("xh",) + HEAD, split_axis=0, concat_axis=0, tiled=True)
    x, gate = call(
        norm_body,
        [shape(ROWS, D), shape(ROWS, HD, dtype=F32)],
        "norm",
        1,
        flops=1 << 26,
        nbytes=1 << 20,
    )(got)

    from_left, from_right = [x], [x]
    for _ in range(3):
        from_left.append(lax.ppermute(from_left[-1], "z", right))
        from_right.append(lax.ppermute(from_right[-1], "z", left))
    far_left = lax.ppermute(from_left[3][:, : D // 2], "z", right)
    far_right = lax.ppermute(from_right[3][:, D // 2 :], "z", left)
    blocks = [x] + from_left[1:] + from_right[1:] + [far_left, far_right]
    parts = expert(blocks, w_own, w_other, w_out, w_out_other)
    own, at_left, at_right = parts[0], parts[1:4], parts[4:7]

    def add(a, b):
        return (a.astype(F32) + b.astype(F32)).astype(BF)

    half = D // 2
    to_right = lax.ppermute(parts[7], "z", right)
    to_left = lax.ppermute(parts[8], "z", left)
    to_right = jnp.concatenate(
        [add(at_right[2][:, :half], to_right), at_right[2][:, half:]], 1
    )
    to_left = jnp.concatenate(
        [at_left[2][:, :half], add(at_left[2][:, half:], to_left)], 1
    )
    for n in (1, 0):
        to_right = add(at_right[n], lax.ppermute(to_right, "z", right))
        to_left = add(at_left[n], lax.ppermute(to_left, "z", left))
    to_right = lax.ppermute(to_right, "z", right)
    to_left = lax.ppermute(to_left, "z", left)
    back = call(gate_body, shape(16, CAP, 512), "gate", 4, flops=1 << 26, nbytes=2 << 20)(
        own, to_right, to_left, gate
    )
    back = lax.all_to_all(back, ("xh",) + HEAD, split_axis=0, concat_axis=0, tiled=True)
    layer_out = call(
        combine_body, shape(2, 32, 512), "combine", 3, flops=1 << 26, nbytes=1 << 20
    )(hidden, codes, back)
    return (layer_out, cache_out)


def solution(mesh):
    fine = Mesh(mesh.devices.reshape(2, NZ, 2, 2, 4), SEQ + HEAD)
    return jax.shard_map(
        shards,
        mesh=fine,
        in_specs=(
            P(SEQ, None, HEAD),
            P(SEQ, None, None, HEAD),
            P(SEQ, None, None, HEAD),
            P(None, None, None, HEAD),
            P(),
            P(),
            P(),
            P(SEQ, None, HEAD),
            P(HEAD, SEQ),
            P(HEAD),
            P(HEAD, None),
            P(SEQ, None, None),
            P(HEAD, None, None, SEQ),
            P(HEAD, SEQ, None),
        ),
        out_specs=(P(SEQ, None, HEAD), P(SEQ, None, None, HEAD)),
        check_vma=False,
    )
```

time: 589 us -> 213 us (0.36); the launches traced: 579 us -> 212 us
  blocking collectives: 178 us -> 13 us
  local copies, waits for them, and re-layouts: 102 us -> 10.2 us
  other arithmetic: 67.5 us -> 3.14 us
  waiting for transfers between devices: 126 us -> 78 us
  Pallas kernels: 0 us -> 36 us
  matrix products: 33.2 us -> 0 us
  starting transfers between devices: 50.1 us -> 57.4 us
    unnamed x1 -> x0, blocking collectives: 81.4 us -> none
    ppermute x0 -> x20, waiting for transfers between devices: none -> 50.2 us  [the longest x3 16.8 us: shards(): from_left.append(lax.ppermute(from_left[-1], 'z', right))]
    all_gather x1 -> x0, blocking collectives: 41.2 us -> none  [shards(): lax.all_gather(codes, 'seq', axis=0, tiled=True)]
    all_gather x2 -> x1, waiting for transfers between devices: 36.1 us -> 0.01 us  [shards(): o_all = lax.all_gather(o_pair, 'z', axis=0, tiled=False)]
    pallas_call x0 -> x10, Pallas kernels: none -> 36 us  [the longest x1 11.4 us: expert(): pl.pallas_call(expert_body, grid=(6,), out_shape=[shape(ROWS, D)] * 7 + [...]
    psum x2 -> x0, blocking collectives: 35.7 us -> none  [the longest x1 18.2 us: shards(): logits = lax.psum(scaled_part, 'head')]
    reduce_scatter x1 -> x0, waiting for transfers between devices: 35.7 us -> none  [shards(): lax.psum_scatter(projected, 'head', scatter_dimension=1, tiled=True)]
    dot_general x20 -> x0, matrix products: 33.2 us -> none  [the longest x6 7.3 us: attend(): jnp.einsum('grn,gnd->grd', block_expo.astype(jnp.bfloat16), value_rows, p...]
  transfers between devices with their start and end apart: 15 -> 25, of which waited for: 8 -> 13; matrix products, arithmetic and copies ran while one was open for 17% -> 4% of each run, Pallas kernels for 0% -> 11%
where the time goes in v1:
time: 213 us; the launch traced here: 212 us
  waiting for transfers between devices  78 us (37%)
  starting transfers between devices  57.4 us (27%)
  Pallas kernels  36 us (17%)
  between operations  14.5 us (7%)
  blocking collectives  13 us (6%)
  local copies, waits for them, and re-layouts  10.2 us (5%)
  other arithmetic  3.14 us (1%)
    ppermute x3, waiting for transfers between devices, shards(): from_left.append(lax.ppermute(from_left[-1], 'z', right))  16.8 us
    ppermute x2, waiting for transfers between devices, shards(): to_right = add(at_right[n], lax.ppermute(to_right, 'z', right))  14.5 us
    all_to_all x1, blocking collectives, shards(): lax.all_to_all(send, ('xh',) + HEAD, split_axis=0, concat_axis=0, tiled=T...  13 us
    pallas_call x1, Pallas kernels, expert(): pl.pallas_call(expert_body, grid=(6,), out_shape=[shape(ROWS, D)] * 7 + [...  11.4 us
    all_to_all x1, starting transfers between devices, shards(): rows = lax.all_to_all(asked, SEQ, split_axis=1, concat_axis=0, tiled=True)  10.5 us
    all_to_all x1, waiting for transfers between devices, shards(): lax.all_to_all(attended.reshape(64, 1, 512), SEQ, split_axis=0, concat_ax...  10.1 us
    all_to_all x1, waiting for transfers between devices, shards(): lax.all_to_all(share.reshape(16, 64, 256), ('c',) + HEAD, split_axis=0, c...  9.59 us
    ppermute x3, starting transfers between devices, shards(): from_right.append(lax.ppermute(from_right[-1], 'z', left))  9.19 us
  transfers between devices with their start and end apart: 25, of which 13 were waited for; matrix products, arithmetic and copies ran while one was open for 4% of the time, Pallas kernels for 11%

profile of v1, /device:TPU:2, one launch (start us, length us, event | category | flops | bytes accessed | tf_op | source)
XLA Modules:
  0.0 212.3 jit_solution(16837685266222246185)
XLA Ops:
  7.2 0.0 all-gather.3.cloned.1.call-start
  7.2 2.2 %collective-permute-start.1 = (bf16[512,128]{1,0:T(8,128)(2,1)}, bf16[512,128]{1,0:T(8,128)(2,1)S(1)}, u32[]{:S(2)}, u32[]{:S(2)}) collective-permute-start(bf16[512,128]{1,0:T(8,128)(2,1)} %param.22), channel_id=1, source_target_pairs={{0,128},{128,0},{1,129},{129,1},{2,130},{130,2},{3,131},{131,3},{4... | collective-permute-start | bytes 393224 | tf_op jit(solution)/shard_map/ppermute | solution.py:440
  9.4 4.8 %collective-permute-done.1 = bf16[512,128]{1,0:T(8,128)(2,1)S(1)} collective-permute-done((bf16[512,128]{1,0:T(8,128)(2,1)}, bf16[512,128]{1,0:T(8,128)(2,1)S(1)}, u32[]{:S(2)}, u32[]{:S(2)}) %collective-permute-start.1) | collective-permute-done | bytes 131104 | tf_op jit(solution)/shard_map/ppermute | solution.py:440
  14.2 0.9 select_bitcast_fusion.1
  15.2 0.7 pad_maximum_fusion.2
  16.0 4.7 %copy.36 = bf16[1,4096,2,256]{3,1,2,0:T(8,128)(2,1)} copy(bf16[1,4096,2,256]{3,2,1,0:T(2,128)(2,1)} %param.26) | data formatting | bytes 8388608 | tf_op args[12]
  20.8 0.1 permute.1
  20.9 0.8 copy.27
  21.7 10.5 %all-to-all-start = ((bf16[2,32,768]{2,0,1:T(2,128)(2,1)}), bf16[2,32,768]{2,0,1:T(2,128)(2,1)S(1)}, u32[]{:S(2)}, u32[]{:S(2)}) async-start(bf16[2,32,768]{2,0,1:T(2,128)(2,1)} %copy.27), calls=%async_computation | async-start | bytes 196608 | tf_op jit(solution)/shard_map/all_to_all | solution.py:449
  32.2 4.0 %split_cycle.1 = (bf16[4096,128]{1,0:T(8,128)(2,1)}, bf16[4096,128]{1,0:T(8,128)(2,1)}) custom-call(bf16[8192,128]{1,0:T(8,128)(2,1)} %bitcast.36), custom_call_target="tpu_custom_call" | custom-call | flops 16777216 | bytes 8388608 | tf_op jit(solution)/shard_map/split_cycle/pallas_call | solution.py:73
  36.2 8.1 %all-to-all-done = bf16[2,32,768]{2,0,1:T(2,128)(2,1)S(1)} async-done(((bf16[2,32,768]{2,0,1:T(2,128)(2,1)}), bf16[2,32,768]{2,0,1:T(2,128)(2,1)S(1)}, u32[]{:S(2)}, u32[]{:S(2)}) %all-to-all-start) | async-done | bytes 98336 | tf_op jit(solution)/shard_map/all_to_all | solution.py:449
  44.4 1.2 copy-done.7
  45.6 1.2 copy-done.8
  46.8 2.8 %attend.1 = bf16[64,512]{1,0:T(8,128)(2,1)S(1)} custom-call(s32[1]{0:T(128)} %bitcast.2.seq_ref, s32[32]{0:T(128)S(1)} %copy-done.10, s32[32]{0:T(128)S(1)} %copy-done.6, bf16[64,768]{1,0:T(8,128)(2,1)S(1)} %reshape.46.rows_ref, bf16[4096,128]{1,0:T(8,128)(2,1)S(1)} %copy-done.7, bf16[4096,128]{1,0:T(8,128)(2,1)S(1)} %copy-done.8, ...), custom_call_target="tpu_custom_call" | custom-call | flops 1073741824 | bytes 2097152 | tf_op jit(solution)/shard_map/attend/pallas_call | solution.py:454
  49.6 0.5 broadcast.1
  50.1 0.7 reduce.1
  50.8 0.7 reshape.56
  51.4 3.9 %all-to-all-start.1 = ((bf16[32,2,512]{2,1,0:T(2,128)(2,1)}), bf16[32,2,512]{2,1,0:T(2,128)(2,1)S(1)}, u32[]{:S(2)}, u32[]{:S(2)}) async-start(bf16[32,2,512]{2,1,0:T(2,128)(2,1)} %reshape.56), calls=%async_computation.1 | async-start | bytes 131072 | tf_op jit(solution)/shard_map/all_to_all | solution.py:471
  55.3 0.2 collective-permute-start.11
  55.6 10.1 %all-to-all-done.1 = bf16[32,2,512]{2,1,0:T(2,128)(2,1)S(1)} async-done(((bf16[32,2,512]{2,1,0:T(2,128)(2,1)}), bf16[32,2,512]{2,1,0:T(2,128)(2,1)S(1)}, u32[]{:S(2)}, u32[]{:S(2)}) %all-to-all-start.1) | async-done | bytes 65568 | tf_op jit(solution)/shard_map/all_to_all | solution.py:471
  65.7 0.1 reshape.57
  65.7 0.4 reduce
  66.2 0.1 collective-permute-start
  66.3 1.2 collective-permute-done.other_ref
  67.6 0.6 copy-done.12
  68.2 6.0 %project.1 = bf16[2,8,64,256]{3,2,1,0:T(8,128)(2,1)} custom-call(s32[1]{0:T(128)} %bitcast.1.core_ref, bf16[64,512]{1,0:T(8,128)(2,1)} %bitcast.43, bf16[64,512]{1,0:T(8,128)(2,1)} %copy-done.12, bf16[8,2,512,128]{3,2,1,0:T(8,128)(2,1)} %bitcast.39), custom_call_target="tpu_custom_call" | custom-call | flops 268435456 | bytes 3145728 | tf_op jit(solution)/shard_map/project/pallas_call | solution.py:202
  74.2 6.1 %all-to-all-start.2 = ((bf16[16,64,256]{2,1,0:T(8,128)(2,1)}), bf16[16,64,256]{2,1,0:T(8,128)(2,1)S(1)}, u32[]{:S(2)}, u32[]{:S(2)}) async-start(bf16[16,64,256]{2,1,0:T(8,128)(2,1)} %bitcast.40), calls=%async_computation.2 | async-start | bytes 1048576 | tf_op jit(solution)/shard_map/all_to_all | solution.py:477
  80.2 0.1 copy.30.router_ref
  80.4 0.1 copy.31.ids_ref
  80.5 9.6 %all-to-all-done.2.part_ref = bf16[16,64,256]{2,1,0:T(8,128)(2,1)S(1)} async-done(((bf16[16,64,256]{2,1,0:T(8,128)(2,1)}), bf16[16,64,256]{2,1,0:T(8,128)(2,1)S(1)}, u32[]{:S(2)}, u32[]{:S(2)}) %all-to-all-start.2) | async-done | bytes 524320 | tf_op jit(solution)/shard_map/all_to_all | solution.py:477
  90.1 0.7 dispatch.1
  90.7 13.0 %all_to_all.45.got_ref = bf16[16,18,640]{2,1,0:T(8,128)(2,1)S(1)} all-to-all(bf16[16,18,640]{2,1,0:T(8,128)(2,1)S(1)} %get-tuple-element.22), channel_id=1, replica_groups=mesh['xh'=2,'z'=8,'c'=2,'xl'=2,'y'=4] {'xh','xl','y'}, dimensions={0} | all-to-all | bytes 737280 | tf_op jit(solution)/shard_map/all_to_all | solution.py:489
  103.8 0.5 norm.1
  104.2 0.7 collective-permute-start.2
  104.9 2.6 %collective-permute-start.5 = (bf16[36,4096]{1,0:T(8,128)(2,1)S(1)}, bf16[36,4096]{1,0:T(8,128)(2,1)S(1)}, u32[]{:S(2)}, u32[]{:S(2)}) collective-permute-start(bf16[36,4096]{1,0:T(8,128)(2,1)S(1)} %get-tuple-element.23.refs_0_), channel_id=1, source_target_pairs={{0,112},{16,0},{32,16},{48,32},{64,48},{80,64},{96,80},{112,96},{1... | collective-permute-start | bytes 884744 | tf_op jit(solution)/shard_map/ppermute | solution.py:502
  107.5 5.9 %collective-permute-done.2.refs_1_ = bf16[36,4096]{1,0:T(8,128)(2,1)S(1)} collective-permute-done((bf16[36,4096]{1,0:T(8,128)(2,1)S(1)}, bf16[36,4096]{1,0:T(8,128)(2,1)S(1)}, u32[]{:S(2)}, u32[]{:S(2)}) %collective-permute-start.2) | collective-permute-done | bytes 294944 | tf_op jit(solution)/shard_map/ppermute | solution.py:501
  113.5 3.2 %collective-permute-start.6 = (bf16[36,4096]{1,0:T(8,128)(2,1)S(1)}, bf16[36,4096]{1,0:T(8,128)(2,1)S(1)}, u32[]{:S(2)}, u32[]{:S(2)}) collective-permute-start(bf16[36,4096]{1,0:T(8,128)(2,1)S(1)} %collective-permute-done.5.refs_4_), channel_id=1, source_target_pairs={{0,112},{16,0},{32,16},{48,32},{64,48},{80,64},{96,80},{112,96},{1... | collective-permute-start | bytes 884744 | tf_op jit(solution)/shard_map/ppermute | solution.py:502
  116.7 5.0 %collective-permute-done.3.refs_2_ = bf16[36,4096]{1,0:T(8,128)(2,1)S(1)} collective-permute-done((bf16[36,4096]{1,0:T(8,128)(2,1)S(1)}, bf16[36,4096]{1,0:T(8,128)(2,1)S(1)}, u32[]{:S(2)}, u32[]{:S(2)}) %collective-permute-start.3) | collective-permute-done | bytes 294944 | tf_op jit(solution)/shard_map/ppermute | solution.py:501
  121.8 3.4 %collective-permute-start.7 = (bf16[36,4096]{1,0:T(8,128)(2,1)S(1)}, bf16[36,4096]{1,0:T(8,128)(2,1)S(1)}, u32[]{:S(2)}, u32[]{:S(2)}) collective-permute-start(bf16[36,4096]{1,0:T(8,128)(2,1)S(1)} %collective-permute-done.6.refs_5_), channel_id=1, source_target_pairs={{0,112},{16,0},{32,16},{48,32},{64,48},{80,64},{96,80},{112,96},{1... | collective-permute-start | bytes 884744 | tf_op jit(solution)/shard_map/ppermute | solution.py:502
  125.1 5.8 %collective-permute-done.4.refs_3_ = bf16[36,4096]{1,0:T(8,128)(2,1)S(1)} collective-permute-done((bf16[36,4096]{1,0:T(8,128)(2,1)S(1)}, bf16[36,4096]{1,0:T(8,128)(2,1)S(1)}, u32[]{:S(2)}, u32[]{:S(2)}) %collective-permute-start.4) | collective-permute-done | bytes 294944 | tf_op jit(solution)/shard_map/ppermute | solution.py:501
  131.0 0.1 collective-permute-start.8
  131.1 3.5 %collective-permute-start.9 = (bf16[36,2048]{1,0:T(8,128)(2,1)S(1)}, bf16[36,2048]{1,0:T(8,128)(2,1)S(1)}, u32[]{:S(2)}, u32[]{:S(2)}) collective-permute-start(bf16[36,2048]{1,0:T(8,128)(2,1)S(1)} %slice.25), channel_id=1, source_target_pairs={{0,112},{16,0},{32,16},{48,32},{64,48},{80,64},{96,80},{112,96},{1... | collective-permute-start | bytes 442376 | tf_op jit(solution)/shard_map/ppermute | solution.py:504
  134.6 2.9 %collective-permute-done.8.refs_7_ = bf16[36,2048]{1,0:T(8,128)(2,1)S(1)} collective-permute-done((bf16[36,2048]{1,0:T(8,128)(2,1)S(1)}, bf16[36,2048]{1,0:T(8,128)(2,1)S(1)}, u32[]{:S(2)}, u32[]{:S(2)}) %collective-permute-start.8) | collective-permute-done | bytes 147488 | tf_op jit(solution)/shard_map/ppermute | solution.py:503
  137.6 11.4 %expert.1 = (bf16[36,4096]{1,0:T(8,128)(2,1)S(1)}, bf16[36,4096]{1,0:T(8,128)(2,1)S(1)}, bf16[36,4096]{1,0:T(8,128)(2,1)S(1)}, bf16[36,4096]{1,0:T(8,128)(2,1)S(...) custom-call(bf16[36,4096]{1,0:T(8,128)(2,1)S(1)} %get-tuple-element., ...), custom_call_target="tpu_custom_call" | custom-call | flops 4294967296 | bytes 18874368 | tf_op jit(solution)/shard_map/expert/pallas_call | solution.py:373
  149.0 0.1 collective-permute-start.12
  149.1 3.6 %collective-permute-start.16 = (bf16[36,2048]{1,0:T(8,128)(2,1)S(1)}, bf16[36,2048]{1,0:T(8,128)(2,1)S(1)}, u32[]{:S(2)}, u32[]{:S(2)}) collective-permute-start(bf16[36,2048]{1,0:T(8,128)(2,1)S(1)} %get-tuple-element.32), channel_id=1, source_target_pairs={{0,112},{16,0},{32,16},{48,32},{64,48},{80,64},{96,80},{112,96},{1... | collective-permute-start | bytes 442376 | tf_op jit(solution)/shard_map/ppermute | solution.py:514
  152.8 5.0 %collective-permute-done.12 = bf16[36,2048]{1,0:T(8,128)(2,1)S(1)} collective-permute-done((bf16[36,2048]{1,0:T(8,128)(2,1)S(1)}, bf16[36,2048]{1,0:T(8,128)(2,1)S(1)}, u32[]{:S(2)}, u32[]{:S(2)}) %collective-permute-start.12) | collective-permute-done | bytes 147488 | tf_op jit(solution)/shard_map/ppermute | solution.py:513
  157.8 0.1 collective-permute-start.13
  158.0 3.3 %collective-permute-start.17 = (bf16[36,4096]{1,0:T(8,128)(2,1)S(1)}, bf16[36,4096]{1,0:T(8,128)(2,1)S(1)}, u32[]{:S(2)}, u32[]{:S(2)}) collective-permute-start(bf16[36,4096]{1,0:T(8,128)(2,1)S(1)} %pad_maximum_fusion.1), channel_id=1, source_target_pairs={{0,112},{16,0},{32,16},{48,32},{64,48},{80,64},{96,80},{112,96},{1... | collective-permute-start | bytes 884744 | tf_op jit(solution)/shard_map/ppermute | solution.py:523
  161.3 7.7 %collective-permute-done.13 = bf16[36,4096]{1,0:T(8,128)(2,1)S(1)} collective-permute-done((bf16[36,4096]{1,0:T(8,128)(2,1)S(1)}, bf16[36,4096]{1,0:T(8,128)(2,1)S(1)}, u32[]{:S(2)}, u32[]{:S(2)}) %collective-permute-start.13) | collective-permute-done | bytes 294944 | tf_op jit(solution)/shard_map/ppermute | solution.py:522
  169.0 0.1 add_convert_fusion.3
  169.0 0.1 collective-permute-start.14
  169.1 0.1 add_convert_fusion.1
  169.2 3.3 %collective-permute-start.18 = (bf16[36,4096]{1,0:T(8,128)(2,1)S(1)}, bf16[36,4096]{1,0:T(8,128)(2,1)S(1)}, u32[]{:S(2)}, u32[]{:S(2)}) collective-permute-start(bf16[36,4096]{1,0:T(8,128)(2,1)S(1)} %add_convert_fusion.1), channel_id=1, source_target_pairs={{0,112},{16,0},{32,16},{48,32},{64,48},{80,64},{96,80},{112,96},{1... | collective-permute-start | bytes 884744 | tf_op jit(solution)/shard_map/ppermute | solution.py:523
  172.5 6.8 %collective-permute-done.14 = bf16[36,4096]{1,0:T(8,128)(2,1)S(1)} collective-permute-done((bf16[36,4096]{1,0:T(8,128)(2,1)S(1)}, bf16[36,4096]{1,0:T(8,128)(2,1)S(1)}, u32[]{:S(2)}, u32[]{:S(2)}) %collective-permute-start.14) | collective-permute-done | bytes 294944 | tf_op jit(solution)/shard_map/ppermute | solution.py:522
  179.3 0.1 add_convert_fusion.2
  179.4 0.1 collective-permute-start.15
  179.5 0.1 add_convert_fusion
  179.6 3.3 %collective-permute-start.19 = (bf16[36,4096]{1,0:T(8,128)(2,1)S(1)}, bf16[36,4096]{1,0:T(8,128)(2,1)S(1)}, u32[]{:S(2)}, u32[]{:S(2)}) collective-permute-start(bf16[36,4096]{1,0:T(8,128)(2,1)S(1)} %add_convert_fusion), channel_id=1, source_target_pairs={{0,112},{16,0},{32,16},{48,32},{64,48},{80,64},{96,80},{112,96},{1... | collective-permute-start | bytes 884744 | tf_op jit(solution)/shard_map/ppermute | solution.py:525
  182.9 4.9 %collective-permute-done.15.right_ref = bf16[36,4096]{1,0:T(8,128)(2,1)S(1)} collective-permute-done((bf16[36,4096]{1,0:T(8,128)(2,1)S(1)}, bf16[36,4096]{1,0:T(8,128)(2,1)S(1)}, u32[]{:S(2)}, u32[]{:S(2)}) %collective-permute-start.15) | collective-permute-done | bytes 294944 | tf_op jit(solution)/shard_map/ppermute | solution.py:524
  187.8 1.1 gate.1
  188.9 7.0 %all-to-all-start.4 = ((bf16[16,18,512]{2,1,0:T(8,128)(2,1)}), bf16[16,18,512]{2,1,0:T(8,128)(2,1)S(1)}, u32[]{:S(2)}, u32[]{:S(2)}) async-start(bf16[16,18,512]{2,1,0:T(8,128)(2,1)} %gate.1), calls=%async_computation.4 | async-start | bytes 786432 | tf_op jit(solution)/shard_map/all_to_all | solution.py:529
  196.0 8.4 %write_cycle.1 = bf16[8192,128]{1,0:T(8,128)(2,1)} custom-call(s32[1]{0:T(128)} %bitcast.2.seq_ref, s32[32]{0:T(128)} %off_ref.3, bf16[64,768]{1,0:T(8,128)(2,1)} %copy-done, bf16[8192,128]{1,0:T(8,128)(2,1)} %bitcast.37), custom_call_target="tpu_custom_call" | custom-call | flops 268435456 | bytes 8388608 | tf_op jit(solution)/shard_map/write_cycle/pallas_call | solution.py:168
  204.4 1.1 combine.1
  (57 shorter events, 0.4 us)
Async XLA Ops:
  7.2 60.4 %all-gather.3.cloned.1.call-start = ((), (), s32[]{:S(2)}) async-start(), calls=%async_computation.5 | async-start | bytes 2359296 | tf_op jit(solution)/shard_map/all_gather | solution.py:445
  7.2 7.0 %collective-permute-start.1 = (bf16[512,128]{1,0:T(8,128)(2,1)}, bf16[512,128]{1,0:T(8,128)(2,1)S(1)}, u32[]{:S(2)}, u32[]{:S(2)}) collective-permute-start(bf16[512,128]{1,0:T(8,128)(2,1)} %param.22), channel_id=1, source_target_pairs={{0,128},{128,0},{1,129},{129,1},{2,130},{130,2},{3,131},{131,3},{4... | collective-permute-start | bytes 393224 | tf_op jit(solution)/shard_map/ppermute | solution.py:440
  15.9 4.8 %copy-start.13 = (bf16[2,32,2,128]{3,2,1,0:T(2,128)(2,1)S(1)}, bf16[2,32,2,128]{3,2,1,0:T(2,128)(2,1)}, u32[]{:S(2)}) copy-start(bf16[2,32,2,128]{3,2,1,0:T(2,128)(2,1)} %param.15) | copy-start | bytes 98308
  16.0 4.8 %copy-start.1 = (bf16[2,32,512]{2,1,0:T(8,128)(2,1)S(1)}, bf16[2,32,512]{2,1,0:T(8,128)(2,1)}, u32[]{:S(2)}) copy-start(bf16[2,32,512]{2,1,0:T(8,128)(2,1)} %q_ref.1) | copy-start | bytes 196612
  16.0 4.8 %copy-start.5 = (s32[32]{0:T(128)S(1)}, s32[32]{0:T(128)}, u32[]{:S(2)}) copy-start(s32[32]{0:T(128)} %param.20) | copy-start | bytes 388
  20.7 23.6 %copy-start.6 = (s32[32]{0:T(128)S(1)}, s32[32]{0:T(128)}, u32[]{:S(2)}) copy-start(s32[32]{0:T(128)} %off_ref.3) | copy-start | bytes 388
  20.7 23.6 %copy-start.9 = (bf16[32,4,2,128]{3,2,1,0:T(2,128)(2,1)S(1)}, bf16[32,4,2,128]{3,2,1,0:T(2,128)(2,1)}, u32[]{:S(2)}) copy-start(bf16[32,4,2,128]{3,2,1,0:T(2,128)(2,1)} %param.17) | copy-start | bytes 196612
  20.7 23.6 %copy-start.10 = (s32[32]{0:T(128)S(1)}, s32[32]{0:T(128)}, u32[]{:S(2)}) copy-start(s32[32]{0:T(128)} %len_ref.1) | copy-start | bytes 388
  20.7 113.9 %collective-permute-start.10 = (bf16[4096,2,256]{2,0,1:T(8,128)(2,1)}, bf16[4096,2,256]{2,0,1:T(8,128)(2,1)}, u32[]{:S(2)}, u32[]{:S(2)}) collective-permute-start(bf16[4096,2,256]{2,0,1:T(8,128)(2,1)} %bitcast.29), channel_id=1, source_target_pairs={{0,8},{8,0},{1,9},{9,1},{2,10},{10,2},{3,11},{11,3},{4,12},{12,4},... | collective-permute-start | bytes 12582920 | tf_op jit(solution)/shard_map/ppermute | solution.py:467
  21.7 22.6 %all-to-all-start = ((bf16[2,32,768]{2,0,1:T(2,128)(2,1)}), bf16[2,32,768]{2,0,1:T(2,128)(2,1)S(1)}, u32[]{:S(2)}, u32[]{:S(2)}) async-start(bf16[2,32,768]{2,0,1:T(2,128)(2,1)} %copy.27), calls=%async_computation | async-start | bytes 196608 | tf_op jit(solution)/shard_map/all_to_all | solution.py:449
  44.3 7.1 %copy-start = (bf16[64,768]{1,0:T(8,128)(2,1)}, bf16[64,768]{1,0:T(8,128)(2,1)S(1)}, u32[]{:S(2)}) copy-start(bf16[64,768]{1,0:T(8,128)(2,1)S(1)} %reshape.46.rows_ref) | copy-start | bytes 294916
  44.3 1.3 copy-start.7
  45.6 1.2 copy-start.8
  46.8 8.5 %copy-start.15 = (bf16[1,256,4096]{2,1,0:T(8,128)(2,1)S(1)}, bf16[1,256,4096]{2,1,0:T(8,128)(2,1)}, u32[]{:S(2)}) copy-start(bf16[1,256,4096]{2,1,0:T(8,128)(2,1)} %param.27) | copy-start | bytes 6291460
  51.4 14.2 %all-to-all-start.1 = ((bf16[32,2,512]{2,1,0:T(2,128)(2,1)}), bf16[32,2,512]{2,1,0:T(2,128)(2,1)S(1)}, u32[]{:S(2)}, u32[]{:S(2)}) async-start(bf16[32,2,512]{2,1,0:T(2,128)(2,1)} %reshape.56), calls=%async_computation.1 | async-start | bytes 131072 | tf_op jit(solution)/shard_map/all_to_all | solution.py:471
  55.3 79.3 %collective-permute-start.11 = (bf16[256,4096]{1,0:T(8,128)(2,1)S(1)}, bf16[256,4096]{1,0:T(8,128)(2,1)}, u32[]{:S(2)}, u32[]{:S(2)}) collective-permute-start(bf16[256,4096]{1,0:T(8,128)(2,1)S(1)} %bitcast.46), channel_id=1, source_target_pairs={{0,8},{8,0},{1,9},{9,1},{2,10},{10,2},{3,11},{11,3},{4,12},{12,4},... | collective-permute-start | bytes 6291464 | tf_op jit(solution)/shard_map/ppermute | solution.py:468
  65.7 14.5 %copy-start.14 = (f32[512,8]{0,1:T(8,128)S(1)}, f32[512,8]{0,1:T(8,128)}, u32[]{:S(2)}) copy-start(f32[512,8]{0,1:T(8,128)} %param.24) | copy-start | bytes 49156
  66.1 14.2 %copy-start.3 = (s32[2,32,2]{1,2,0:T(2,128)S(1)}, s32[2,32,2]{1,2,0:T(2,128)}, u32[]{:S(2)}) copy-start(s32[2,32,2]{1,2,0:T(2,128)} %param.25) | copy-start | bytes 1540
  66.2 23.9 %copy-start.2 = (bf16[2,32,512]{2,1,0:T(8,128)(2,1)S(1)}, bf16[2,32,512]{2,1,0:T(8,128)(2,1)}, u32[]{:S(2)}) copy-start(bf16[2,32,512]{2,1,0:T(8,128)(2,1)} %res_ref.1) | copy-start | bytes 196612
  66.2 23.9 %copy-start.4 = (f32[512]{0:T(512)S(1)}, f32[512]{0:T(512)}, u32[]{:S(2)}) copy-start(f32[512]{0:T(512)} %param.23) | copy-start | bytes 6148
  66.2 1.4 copy-start.11
  66.2 1.3 collective-permute-start
  67.6 0.6 copy-start.12
  74.2 15.9 %all-to-all-start.2 = ((bf16[16,64,256]{2,1,0:T(8,128)(2,1)}), bf16[16,64,256]{2,1,0:T(8,128)(2,1)S(1)}, u32[]{:S(2)}, u32[]{:S(2)}) async-start(bf16[16,64,256]{2,1,0:T(8,128)(2,1)} %bitcast.40), calls=%async_computation.2 | async-start | bytes 1048576 | tf_op jit(solution)/shard_map/all_to_all | solution.py:477
  104.2 9.3 %collective-permute-start.2 = (bf16[36,4096]{1,0:T(8,128)(2,1)S(1)}, bf16[36,4096]{1,0:T(8,128)(2,1)S(1)}, u32[]{:S(2)}, u32[]{:S(2)}) collective-permute-start(bf16[36,4096]{1,0:T(8,128)(2,1)S(1)} %get-tuple-element.23.refs_0_), channel_id=1, source_target_pairs={{0,16},{16,32},{32,48},{48,64},{64,80},{80,96},{96,112},{112,0},{1... | collective-permute-start | bytes 884744 | tf_op jit(solution)/shard_map/ppermute | solution.py:501
  104.9 8.6 %collective-permute-start.5 = (bf16[36,4096]{1,0:T(8,128)(2,1)S(1)}, bf16[36,4096]{1,0:T(8,128)(2,1)S(1)}, u32[]{:S(2)}, u32[]{:S(2)}) collective-permute-start(bf16[36,4096]{1,0:T(8,128)(2,1)S(1)} %get-tuple-element.23.refs_0_), channel_id=1, source_target_pairs={{0,112},{16,0},{32,16},{48,32},{64,48},{80,64},{96,80},{112,96},{1... | collective-permute-start | bytes 884744 | tf_op jit(solution)/shard_map/ppermute | solution.py:502
  113.5 8.3 %collective-permute-start.3 = (bf16[36,4096]{1,0:T(8,128)(2,1)S(1)}, bf16[36,4096]{1,0:T(8,128)(2,1)S(1)}, u32[]{:S(2)}, u32[]{:S(2)}) collective-permute-start(bf16[36,4096]{1,0:T(8,128)(2,1)S(1)} %collective-permute-done.2.refs_1_), channel_id=1, source_target_pairs={{0,16},{16,32},{32,48},{48,64},{64,80},{80,96},{96,112},{112,0},{1... | collective-permute-start | bytes 884744 | tf_op jit(solution)/shard_map/ppermute | solution.py:501
  113.5 8.3 %collective-permute-start.6 = (bf16[36,4096]{1,0:T(8,128)(2,1)S(1)}, bf16[36,4096]{1,0:T(8,128)(2,1)S(1)}, u32[]{:S(2)}, u32[]{:S(2)}) collective-permute-start(bf16[36,4096]{1,0:T(8,128)(2,1)S(1)} %collective-permute-done.5.refs_4_), channel_id=1, source_target_pairs={{0,112},{16,0},{32,16},{48,32},{64,48},{80,64},{96,80},{112,96},{1... | collective-permute-start | bytes 884744 | tf_op jit(solution)/shard_map/ppermute | solution.py:502
  121.8 9.2 %collective-permute-start.4 = (bf16[36,4096]{1,0:T(8,128)(2,1)S(1)}, bf16[36,4096]{1,0:T(8,128)(2,1)S(1)}, u32[]{:S(2)}, u32[]{:S(2)}) collective-permute-start(bf16[36,4096]{1,0:T(8,128)(2,1)S(1)} %collective-permute-done.3.refs_2_), channel_id=1, source_target_pairs={{0,16},{16,32},{32,48},{48,64},{64,80},{80,96},{96,112},{112,0},{1... | collective-permute-start | bytes 884744 | tf_op jit(solution)/shard_map/ppermute | solution.py:501
  121.8 9.3 %collective-permute-start.7 = (bf16[36,4096]{1,0:T(8,128)(2,1)S(1)}, bf16[36,4096]{1,0:T(8,128)(2,1)S(1)}, u32[]{:S(2)}, u32[]{:S(2)}) collective-permute-start(bf16[36,4096]{1,0:T(8,128)(2,1)S(1)} %collective-permute-done.6.refs_5_), channel_id=1, source_target_pairs={{0,112},{16,0},{32,16},{48,32},{64,48},{80,64},{96,80},{112,96},{1... | collective-permute-start | bytes 884744 | tf_op jit(solution)/shard_map/ppermute | solution.py:502
  131.0 6.6 %collective-permute-start.8 = (bf16[36,2048]{1,0:T(8,128)(2,1)S(1)}, bf16[36,2048]{1,0:T(8,128)(2,1)S(1)}, u32[]{:S(2)}, u32[]{:S(2)}) collective-permute-start(bf16[36,2048]{1,0:T(8,128)(2,1)S(1)} %slice.24), channel_id=1, source_target_pairs={{0,16},{16,32},{32,48},{48,64},{64,80},{80,96},{96,112},{112,0},{1... | collective-permute-start | bytes 442376 | tf_op jit(solution)/shard_map/ppermute | solution.py:503
  131.1 6.5 %collective-permute-start.9 = (bf16[36,2048]{1,0:T(8,128)(2,1)S(1)}, bf16[36,2048]{1,0:T(8,128)(2,1)S(1)}, u32[]{:S(2)}, u32[]{:S(2)}) collective-permute-start(bf16[36,2048]{1,0:T(8,128)(2,1)S(1)} %slice.25), channel_id=1, source_target_pairs={{0,112},{16,0},{32,16},{48,32},{64,48},{80,64},{96,80},{112,96},{1... | collective-permute-start | bytes 442376 | tf_op jit(solution)/shard_map/ppermute | solution.py:504
  149.0 8.7 %collective-permute-start.12 = (bf16[36,2048]{1,0:T(8,128)(2,1)S(1)}, bf16[36,2048]{1,0:T(8,128)(2,1)S(1)}, u32[]{:S(2)}, u32[]{:S(2)}) collective-permute-start(bf16[36,2048]{1,0:T(8,128)(2,1)S(1)} %get-tuple-element.28), channel_id=1, source_target_pairs={{0,16},{16,32},{32,48},{48,64},{64,80},{80,96},{96,112},{112,0},{1... | collective-permute-start | bytes 442376 | tf_op jit(solution)/shard_map/ppermute | solution.py:513
  149.1 8.8 %collective-permute-start.16 = (bf16[36,2048]{1,0:T(8,128)(2,1)S(1)}, bf16[36,2048]{1,0:T(8,128)(2,1)S(1)}, u32[]{:S(2)}, u32[]{:S(2)}) collective-permute-start(bf16[36,2048]{1,0:T(8,128)(2,1)S(1)} %get-tuple-element.32), channel_id=1, source_target_pairs={{0,112},{16,0},{32,16},{48,32},{64,48},{80,64},{96,80},{112,96},{1... | collective-permute-start | bytes 442376 | tf_op jit(solution)/shard_map/ppermute | solution.py:514
  157.8 11.1 %collective-permute-start.13 = (bf16[36,4096]{1,0:T(8,128)(2,1)S(1)}, bf16[36,4096]{1,0:T(8,128)(2,1)S(1)}, u32[]{:S(2)}, u32[]{:S(2)}) collective-permute-start(bf16[36,4096]{1,0:T(8,128)(2,1)S(1)} %pad_maximum_fusion), channel_id=1, source_target_pairs={{0,16},{16,32},{32,48},{48,64},{64,80},{80,96},{96,112},{112,0},{1... | collective-permute-start | bytes 884744 | tf_op jit(solution)/shard_map/ppermute | solution.py:522
  158.0 11.1 %collective-permute-start.17 = (bf16[36,4096]{1,0:T(8,128)(2,1)S(1)}, bf16[36,4096]{1,0:T(8,128)(2,1)S(1)}, u32[]{:S(2)}, u32[]{:S(2)}) collective-permute-start(bf16[36,4096]{1,0:T(8,128)(2,1)S(1)} %pad_maximum_fusion.1), channel_id=1, source_target_pairs={{0,112},{16,0},{32,16},{48,32},{64,48},{80,64},{96,80},{112,96},{1... | collective-permute-start | bytes 884744 | tf_op jit(solution)/shard_map/ppermute | solution.py:523
  169.0 10.3 %collective-permute-start.14 = (bf16[36,4096]{1,0:T(8,128)(2,1)S(1)}, bf16[36,4096]{1,0:T(8,128)(2,1)S(1)}, u32[]{:S(2)}, u32[]{:S(2)}) collective-permute-start(bf16[36,4096]{1,0:T(8,128)(2,1)S(1)} %add_convert_fusion.3), channel_id=1, source_target_pairs={{0,16},{16,32},{32,48},{48,64},{64,80},{80,96},{96,112},{112,0},{1... | collective-permute-start | bytes 884744 | tf_op jit(solution)/shard_map/ppermute | solution.py:522
  169.2 10.3 %collective-permute-start.18 = (bf16[36,4096]{1,0:T(8,128)(2,1)S(1)}, bf16[36,4096]{1,0:T(8,128)(2,1)S(1)}, u32[]{:S(2)}, u32[]{:S(2)}) collective-permute-start(bf16[36,4096]{1,0:T(8,128)(2,1)S(1)} %add_convert_fusion.1), channel_id=1, source_target_pairs={{0,112},{16,0},{32,16},{48,32},{64,48},{80,64},{96,80},{112,96},{1... | collective-permute-start | bytes 884744 | tf_op jit(solution)/shard_map/ppermute | solution.py:523
  179.4 8.4 %collective-permute-start.15 = (bf16[36,4096]{1,0:T(8,128)(2,1)S(1)}, bf16[36,4096]{1,0:T(8,128)(2,1)S(1)}, u32[]{:S(2)}, u32[]{:S(2)}) collective-permute-start(bf16[36,4096]{1,0:T(8,128)(2,1)S(1)} %add_convert_fusion.2), channel_id=1, source_target_pairs={{0,16},{16,32},{32,48},{48,64},{64,80},{80,96},{96,112},{112,0},{1... | collective-permute-start | bytes 884744 | tf_op jit(solution)/shard_map/ppermute | solution.py:524
  179.6 8.2 %collective-permute-start.19 = (bf16[36,4096]{1,0:T(8,128)(2,1)S(1)}, bf16[36,4096]{1,0:T(8,128)(2,1)S(1)}, u32[]{:S(2)}, u32[]{:S(2)}) collective-permute-start(bf16[36,4096]{1,0:T(8,128)(2,1)S(1)} %add_convert_fusion), channel_id=1, source_target_pairs={{0,112},{16,0},{32,16},{48,32},{64,48},{80,64},{96,80},{112,96},{1... | collective-permute-start | bytes 884744 | tf_op jit(solution)/shard_map/ppermute | solution.py:525
  188.9 15.4 %all-to-all-start.4 = ((bf16[16,18,512]{2,1,0:T(8,128)(2,1)}), bf16[16,18,512]{2,1,0:T(8,128)(2,1)S(1)}, u32[]{:S(2)}, u32[]{:S(2)}) async-start(bf16[16,18,512]{2,1,0:T(8,128)(2,1)} %gate.1), calls=%async_computation.4 | async-start | bytes 786432 | tf_op jit(solution)/shard_map/all_to_all | solution.py:529
Sparse Core Ops, SparseCore 0:
  16.1 45.8 all-gather.2

commit v2 on v1

v2 whole, which is shorter than its diff:
```python
import functools

import jax
import jax.numpy as jnp
from jax import lax
from jax.experimental import pallas as pl
from jax.experimental.pallas import tpu as pltpu
from jax.sharding import Mesh
from jax.sharding import PartitionSpec as P

D = 4096
HD = 128
E = 8
CAP = 18
SLOT = 24
NZ = 8
BF = jnp.bfloat16
F32 = jnp.float32
VMEM = pl.BlockSpec(memory_space=pltpu.VMEM)
ANY = pl.BlockSpec(memory_space=pl.ANY)
HBM = pl.BlockSpec(memory_space=pltpu.HBM)
SMEM = pl.BlockSpec(memory_space=pltpu.SMEM)
SEQ = ("xh", "z", "c")
HEAD = ("xl", "y")


def call(
    body, outs, name, n_in, scalars=0, after=0, flops=0, nbytes=0, limit=20, scratch=(), keep=False
):
    return pl.pallas_call(
        body,
        out_shape=outs,
        in_specs=[SMEM] * scalars
        + [VMEM] * (n_in - scalars)
        + [HBM if keep else ANY] * after,
        out_specs=[VMEM] * (len(outs) - 1) + [HBM]
        if keep
        else jax.tree.map(lambda _: VMEM, outs),
        input_output_aliases={n_in + after - 1: len(outs) - 1} if keep else {},
        scratch_shapes=list(scratch),
        compiler_params=pltpu.CompilerParams(vmem_limit_bytes=limit << 20),
        cost_estimate=pl.CostEstimate(
            flops=flops, bytes_accessed=nbytes, transcendentals=0
        ),
        name=name,
    )


def shape(*dims, dtype=BF):
    return jax.ShapeDtypeStruct(dims, dtype)


def dot(a, b):
    return jnp.dot(a, b, preferred_element_type=F32)


def dot_t(a, b):
    return lax.dot_general(a, b, (((1,), (1,)), ((), ())), preferred_element_type=F32)


def slot_of_request(order_row):
    n = order_row.shape[1]
    return order_row == lax.broadcasted_iota(jnp.int32, (n, n), 0)


ASK = 16


def permute_body(order_ref, q_ref, kv_ref, out_ref, wide):
    hot = jnp.where(slot_of_request(order_ref[...]), 1.0, 0.0).astype(BF)
    count = hot.shape[0]
    wide[...] = jnp.zeros_like(wide)
    for i in range(2):
        rows = jnp.concatenate([q_ref[i], kv_ref[i, :, 0, :], kv_ref[i, :, 1, :]], 1)
        rows = dot(hot, rows)
        for g in range(6):
            wide[pl.ds(i * 6 + g, count, stride=ASK), :] = rows[:, g * HD : (g + 1) * HD]
    out_ref[...] = wide[...].astype(BF)


def split_body(cache_ref, k_ref, v_ref, wide):
    rows = cache_ref.shape[0]
    wide[...] = cache_ref[...].astype(F32)
    k_ref[...] = wide[pl.ds(0, rows // 2, stride=2), :].astype(BF)
    v_ref[...] = wide[pl.ds(1, rows // 2, stride=2), :].astype(BF)


def split_cycle(cache_rows):
    rows = cache_rows.shape[0]
    return call(
        split_body,
        [shape(rows // 2, HD)] * 2,
        "split_cycle",
        1,
        flops=1 << 24,
        nbytes=8 << 20,
        scratch=[pltpu.VMEM((rows, HD), F32)],
    )(cache_rows)


CHUNK = 512


def attend_body(
    seq_ref,
    len_ref,
    off_ref,
    rows_ref,
    sink_ref,
    k_ref,
    v_ref,
    weight_ref,
    out_ref,
    new_ref,
    weight_out_ref,
    scores,
    wide,
    asked,
    mixed_rows,
):
    seq = seq_ref[0]
    length, offset = len_ref[seq], off_ref[seq]
    half = rows_ref.shape[0] // ASK
    span = 2 * half
    cycle = k_ref.shape[0]
    group = 4
    asked[...] = rows_ref[...].astype(F32)

    def piece(g):
        return jnp.concatenate(
            [asked[pl.ds(i * 6 + g, half, stride=ASK), :] for i in range(2)], 0
        )

    query = jnp.concatenate([piece(g) for g in range(group)], 0).astype(BF)
    new_k, new_v = piece(4), piece(5)
    new_ref[...] = jnp.concatenate([new_k, new_v], 0).astype(BF)
    count = span * group
    scale = HD**-0.5
    row = lax.broadcasted_iota(jnp.int32, (count, 1), 0) % span
    token = row % half * 2 + row // half
    oldest = jnp.maximum(token + 1, cycle - length + 4)
    wide[...] = sink_ref[seq].astype(F32)
    pad = jnp.zeros((span - 4, HD), F32)
    first_k = jnp.concatenate([wide[pl.ds(0, 4, stride=2), :], pad, new_k], 0).astype(BF)
    first_v = jnp.concatenate([wide[pl.ds(1, 4, stride=2), :], pad, new_v], 0).astype(BF)
    column = lax.broadcasted_iota(jnp.int32, (1, 2 * span), 1)
    at = column - span
    live = (column < 4) | ((at >= 0) & (at % half * 2 + at // half <= token))
    low = jnp.float32(-jnp.inf)
    first = jnp.where(live, dot_t(query, first_k), low)
    peak = first
    for n in range(cycle // CHUNK):
        part = dot_t(query, k_ref[n * CHUNK : (n + 1) * CHUNK, :])
        age = lax.broadcasted_iota(jnp.int32, (1, CHUNK), 1) + (n * CHUNK - offset)
        age = jnp.where(age < 0, age + cycle, age)
        part = jnp.where(age >= oldest, part, low)
        scores[:, n * CHUNK : (n + 1) * CHUNK] = part
        for m in range(CHUNK // HD):
            peak = jnp.maximum(peak, part[:, m * HD : (m + 1) * HD])
    top = jnp.max(peak, 1, keepdims=True)
    expo = jnp.exp((first - top) * scale)
    total = expo
    acc = dot(expo.astype(BF), first_v)
    for n in range(cycle // CHUNK):
        expo = jnp.exp((scores[:, n * CHUNK : (n + 1) * CHUNK] - top) * scale)
        for m in range(CHUNK // HD):
            total = total + expo[:, m * HD : (m + 1) * HD]
        acc = acc + dot(expo.astype(BF), v_ref[n * CHUNK : (n + 1) * CHUNK, :])
    mixed = acc / jnp.sum(total, 1, keepdims=True)
    for g in range(group):
        for i in range(2):
            first_row = g * span + i * half
            mixed_rows[pl.ds(i * 4 + g, half, stride=8), :] = mixed[
                first_row : first_row + half
            ]
    out_ref[...] = mixed_rows[...].astype(BF)


WINDOW = 144


def write_body(seq_ref, off_ref, new_ref, cache_ref, after_ref, out_ref, done_ref):
    done_ref[...] = jnp.zeros_like(done_ref)
    offset = off_ref[seq_ref[0]]
    step = cache_ref.shape[0]
    total = step * pl.num_programs(0)
    span = new_ref.shape[0] // 2
    half = span // 2
    out_ref[...] = cache_ref[...]
    for wrap in (0, 1):
        first = 2 * offset - wrap * total - pl.program_id(0) * step

        @pl.when((first > -2 * span) & (first < step))
        def _(first=first):
            start = jnp.clip(first, 0, step - WINDOW) // 16 * 16
            window = pl.ds(pl.multiple_of(start, 16), WINDOW)
            row = lax.broadcasted_iota(jnp.int32, (WINDOW, 1), 0) + start
            at = row - first
            column = lax.broadcasted_iota(jnp.int32, (1, 2 * span), 1)
            hot = at % 2 * span + at // 2 % 2 * half + at // 4 == column
            written = (at >= 0) & (at < 2 * span)
            hot = jnp.where(written & hot, 1.0, 0.0).astype(BF)
            fresh = dot(hot, new_ref[...])
            old = out_ref[window, :].astype(F32)
            out_ref[window, :] = jnp.where(written, fresh, old).astype(BF)


def write_cycle(seq, offsets, new, cache_rows, after):
    total, step = cache_rows.shape[0], 2048
    return pl.pallas_call(
        write_body,
        grid=(total // step,),
        out_shape=[shape(total, HD), shape(8, HD, dtype=F32)],
        in_specs=[
            SMEM,
            SMEM,
            pl.BlockSpec(new.shape, lambda n: (0, 0)),
            pl.BlockSpec((step, HD), lambda n: (n, 0)),
            ANY,
        ],
        out_specs=[
            pl.BlockSpec((step, HD), lambda n: (n, 0)),
            pl.BlockSpec((8, HD), lambda n: (0, 0)),
        ],
        cost_estimate=pl.CostEstimate(
            flops=1 << 24, bytes_accessed=16 << 20, transcendentals=0
        ),
        compiler_params=pltpu.CompilerParams(vmem_limit_bytes=16 << 20),
        name="write_cycle",
    )(seq, offsets, new, cache_rows, after)


def pair_body(xh_ref, own_ref, other_ref, after_ref, out_ref):
    xh = xh_ref[0]
    out_ref[xh] = own_ref[...]
    out_ref[1 - xh] = other_ref[...]


def unmix_body(w_ref, after_ref, out_ref):
    for k in range(2):
        out_ref[k] = w_ref[:, k, :]


def unmix(w_in, after):
    step = 512
    return pl.pallas_call(
        unmix_body,
        grid=(D // step,),
        out_shape=shape(2, D, 256),
        in_specs=[pl.BlockSpec((step, 2, 256), lambda n: (n, 0, 0)), ANY],
        out_specs=pl.BlockSpec((2, step, 256), lambda n: (0, n, 0)),
        cost_estimate=pl.CostEstimate(
            flops=1 << 20, bytes_accessed=16 << 20, transcendentals=0
        ),
        compiler_params=pltpu.CompilerParams(vmem_limit_bytes=16 << 20),
        name="unmix",
    )(w_in, after)


def project_body(core_ref, own_ref, other_ref, w_ref, out_ref, wide, both):
    half = own_ref.shape[0] // 8
    rows = 2 * half

    @pl.when(pl.program_id(0) == 0)
    def _():
        first = core_ref[0] == 0
        own, other = own_ref[...].astype(F32), other_ref[...].astype(F32)
        for c in range(2):
            wide[...] = jnp.where(first == (c == 0), own, other)
            for i in range(2):
                for g in range(4):
                    at = c * rows + i * half
                    both[at : at + half, g * HD : (g + 1) * HD] = wide[
                        pl.ds(i * 4 + g, half, stride=8), :
                    ].astype(BF)

    for n in range(2):
        weight = jnp.concatenate([w_ref[2 * n, 0], w_ref[2 * n + 1, 0]], 1)
        result = dot(both[...], weight).astype(BF)
        out_ref[0, n] = result[:rows]
        out_ref[1, n] = result[rows:]


def project(core, own, other, weight):
    rows = own.shape[0] // 4
    return pl.pallas_call(
        project_body,
        grid=(4,),
        out_shape=shape(2, 8, rows, 256),
        in_specs=[
            SMEM,
            pl.BlockSpec(own.shape, lambda n: (0, 0)),
            pl.BlockSpec(own.shape, lambda n: (0, 0)),
            pl.BlockSpec((4, 1, 512, 128), lambda n: (n % 2, n // 2, 0, 0)),
        ],
        out_specs=pl.BlockSpec((2, 2, rows, 256), lambda n: (0, n, 0, 0)),
        scratch_shapes=[pltpu.VMEM(own.shape, F32), pltpu.VMEM((2 * rows, 512), BF)],
        cost_estimate=pl.CostEstimate(
            flops=1 << 28, bytes_accessed=3 << 20, transcendentals=0
        ),
        compiler_params=pltpu.CompilerParams(vmem_limit_bytes=16 << 20),
        name="project",
    )(core, own, other, weight)


def pieces(value):
    high = value.astype(BF).astype(F32)
    rest = value - high
    middle = rest.astype(BF).astype(F32)
    return high, middle, (rest - middle).astype(BF).astype(F32)


def dispatch_body(
    order_ref,
    part_ref,
    res_ref,
    gain_ref,
    router_ref,
    ids_ref,
    ids_t_ref,
    hidden_ref,
    code_ref,
    send_ref,
):
    hot = jnp.where(slot_of_request(order_ref[...]), 1.0, 0.0).astype(BF)
    resid = jnp.concatenate([dot(hot, res_ref[i]) for i in range(2)], 0)
    picks = jnp.concatenate(
        [dot(hot, ids_ref[i].astype(F32).astype(BF)) for i in range(2)], 0
    )
    picks_t = jnp.concatenate(
        [dot_t(ids_t_ref[i].astype(F32).astype(BF), hot) for i in range(2)], 1
    )
    sums = []
    for c in range(2):
        total = part_ref[c * 8].astype(F32)
        for h in range(1, 8):
            total = total + part_ref[c * 8 + h].astype(F32)
        sums.append(total)
    projected = jnp.concatenate(
        [sums[0][:, :HD], sums[1][:, :HD], sums[0][:, HD:], sums[1][:, HD:]], 1
    )
    hidden = resid + projected
    hidden_ref[...] = hidden
    gained = hidden * gain_ref[...]
    square = jnp.sum(hidden * hidden, 1, keepdims=True)
    share = jnp.dot(
        gained,
        router_ref[...],
        precision=lax.Precision.HIGHEST,
        preferred_element_type=F32,
    )
    rows = hidden.shape[0]
    one, two = picks[:, 0:1], picks[:, 1:2]
    expert = lax.broadcasted_iota(jnp.int32, (1, E), 1).astype(F32)
    first, second = one == expert, two == expert
    apart = jnp.sum(jnp.where(first, share, 0.0) - jnp.where(second, share, 0.0), 1, keepdims=True)
    before = lax.broadcasted_iota(jnp.int32, (rows, rows), 0)
    after = lax.broadcasted_iota(jnp.int32, (rows, rows), 1)
    lower = jnp.where(before > after, 1.0, 0.0).astype(BF)
    upper = jnp.where(before < after, 1.0, 0.0).astype(BF)
    earlier = dot(lower, jnp.where(first | second, 1.0, 0.0).astype(BF))
    slot_one = jnp.sum(jnp.where(first, earlier, 0.0), 1, keepdims=True)
    slot_two = jnp.sum(jnp.where(second, earlier, 0.0), 1, keepdims=True)
    lane = lax.broadcasted_iota(jnp.int32, (rows, HD), 1)
    code_ref[...] = jnp.where(
        lane == 0, one * SLOT + slot_one, two * SLOT + slot_two
    ).astype(jnp.int32)
    one_t, two_t = picks_t[0:1], picks_t[1:2]
    expert_t = lax.broadcasted_iota(jnp.int32, (E, 1), 0).astype(F32)
    first_t, second_t = one_t == expert_t, two_t == expert_t
    earlier_t = dot(jnp.where(first_t | second_t, 1.0, 0.0).astype(BF), upper)
    slot_one_t = jnp.sum(jnp.where(first_t, earlier_t, 0.0), 0, keepdims=True)
    slot_two_t = jnp.sum(jnp.where(second_t, earlier_t, 0.0), 0, keepdims=True)
    place = lax.broadcasted_iota(jnp.int32, (E * SLOT, 1), 0).astype(F32)
    is_one = jnp.where(place == one_t * SLOT + slot_one_t, 1.0, 0.0)
    is_two = jnp.where(place == two_t * SLOT + slot_two_t, 1.0, 0.0)
    plus, minus = (is_one + is_two).astype(BF), (is_one - is_two).astype(BF)
    bucket = dot(plus, gained.astype(BF)).astype(BF)
    norm_terms, gate_terms = jnp.zeros((rows, HD), F32), jnp.zeros((rows, HD), F32)
    for n, (s, a) in enumerate(zip(pieces(square), pieces(apart))):
        norm_terms = jnp.where(lane == n, s, norm_terms)
        gate_terms = jnp.where(lane == 3 + n, a, gate_terms)
    terms = (dot(plus, norm_terms.astype(BF)) + dot(minus, gate_terms.astype(BF))).astype(BF)
    for e in range(E):
        for x in range(2):
            send_ref[x * E + e, :, 0:512] = bucket[e * SLOT : e * SLOT + CAP]
            send_ref[x * E + e, :, 512:640] = terms[e * SLOT : e * SLOT + CAP]


QUARTER = D // 4
BLOCK = 8 * CAP


def norm_body(got_ref, after_ref, x_ref, gate_ref):
    target = lax.broadcasted_iota(jnp.int32, (BLOCK, CAP), 0)
    source = lax.broadcasted_iota(jnp.int32, (BLOCK, CAP), 1)
    lane = lax.broadcasted_iota(jnp.int32, (CAP, HD), 1)
    parts, gates = [0.0, 0.0], 0.0
    for x in range(2):
        terms = got_ref[x * 8, :, 512:640].astype(F32)
        for h in range(1, 8):
            terms = terms + got_ref[x * 8 + h, :, 512:640].astype(F32)
        square = jnp.sum(jnp.where(lane < 3, terms, 0.0), 1, keepdims=True)
        apart = jnp.sum(jnp.where((lane >= 3) & (lane < 6), terms, 0.0), 1, keepdims=True)
        inv_rms = lax.rsqrt(square / D + 1e-05)
        gate = 1.0 / (1.0 + jnp.exp(-(apart * inv_rms)))
        gate = jnp.broadcast_to(gate, (CAP, HD)).astype(BF)
        for q in range(4):
            put = jnp.where(target == source + CAP * (4 * x + q), 1.0, 0.0).astype(BF)
            gates = gates + dot(put, gate)
            for n in range(2):
                rows = got_ref[x * 8 + 2 * q + n, :, 0:512].astype(F32) * inv_rms
                parts[n] = parts[n] + dot(put, rows.astype(BF))
    gate_ref[...] = gates
    for n in range(2):
        x_ref[:, n * 512 : (n + 1) * 512] = parts[n].astype(BF)


def expert_body(*refs):
    x_refs, refs = refs[:9], refs[9:]
    w_refs, down_refs = refs[0:2], refs[2:4]
    out_refs, (x, sums, inner) = refs[4:12], refs[12:]
    half = QUARTER // 2
    step = pl.program_id(0)
    for q in range(4):

        @pl.when(step == q)
        def _(q=q):
            for n in range(8):
                for b in range(2):
                    to = slice((2 * n + b) * CAP, (2 * n + b + 1) * CAP)
                    at = slice((4 * b + q) * CAP, (4 * b + q + 1) * CAP)
                    if n < 7:
                        x[to, :] = x_refs[n][at, :]
                    else:
                        x[to, :half] = x_refs[7][at, :]
                        x[to, half:] = x_refs[8][at, :]
            rows = x[...]
            for m in range(4):
                cut = slice(m * 256, (m + 1) * 256)
                part = dot(rows, w_refs[m // 2][m % 2])
                sums[:, cut] = part if q == 0 else sums[:, cut] + part

        @pl.when(step == 4 + q)
        def _(q=q):
            if q == 0:
                for c in range(2):
                    gate, up = (sums[:, (2 * c + k) * 256 : (2 * c + k + 1) * 256] for k in range(2))
                    inner[:, c * 256 : (c + 1) * 256] = (
                        gate / (1.0 + jnp.exp(-gate)) * up
                    ).astype(BF)
            result = dot(inner[:, :256], down_refs[0][...])
            result = result + dot(inner[:, 256:], down_refs[1][...])
            for n in range(8):
                for b in range(2):
                    at = (2 * n + b) * CAP
                    to = slice((4 * b + q) * CAP, (4 * b + q + 1) * CAP)
                    out_refs[n][to, :] = result[at : at + CAP].astype(BF)


def expert(blocks, own, other, down, other_down):
    rows = 16 * CAP
    block = pl.BlockSpec((BLOCK, QUARTER), lambda j: (0, 0))
    part = pl.BlockSpec((BLOCK, QUARTER // 2), lambda j: (0, 0))
    wide = pl.BlockSpec((2, QUARTER, 256), lambda j: (0, jnp.minimum(j, 3), 0))
    narrow = pl.BlockSpec((256, QUARTER), lambda j: (0, jnp.maximum(j - 4, 0)))
    return pl.pallas_call(
        expert_body,
        grid=(8,),
        out_shape=[shape(BLOCK, QUARTER)] * 8,
        in_specs=[block] * 7 + [part] * 2 + [wide] * 2 + [narrow] * 2,
        out_specs=[block] * 8,
        scratch_shapes=[
            pltpu.VMEM((rows, QUARTER), BF),
            pltpu.VMEM((rows, QUARTER), F32),
            pltpu.VMEM((rows, 512), BF),
        ],
        compiler_params=pltpu.CompilerParams(vmem_limit_bytes=40 << 20),
        cost_estimate=pl.CostEstimate(
            flops=4 << 30, bytes_accessed=14 << 20, transcendentals=0
        ),
        name="expert",
    )(*blocks, own, other, down, other_down)


def gate_body(own_ref, right_ref, left_ref, gate_ref, send_ref):
    target = lax.broadcasted_iota(jnp.int32, (CAP, BLOCK // 2), 0)
    source = lax.broadcasted_iota(jnp.int32, (CAP, BLOCK // 2), 1)
    take = [jnp.where(target + CAP * q == source, 1.0, 0.0).astype(BF) for q in range(4)]
    for x in range(2):
        rows = slice(x * BLOCK // 2, (x + 1) * BLOCK // 2)
        total = own_ref[rows, :].astype(F32) + right_ref[rows, :].astype(F32)
        total = total + left_ref[rows, :].astype(F32)
        total = (total * gate_ref[rows, 0:1]).astype(BF)
        for h in range(8):
            cut = slice(h % 2 * 512, h % 2 * 512 + 512)
            send_ref[x * 8 + h] = dot(take[h // 2], total[:, cut]).astype(BF)


def combine_body(hidden_ref, code_ref, got_ref, out_ref):
    total = hidden_ref[...]
    rows = total.shape[0]
    one, two = code_ref[:, 0:1], code_ref[:, 1:2]
    lane = lax.broadcasted_iota(jnp.int32, (rows, CAP), 1)
    for e in range(E):
        at = lane + e * SLOT
        hot = jnp.where((one == at) | (two == at), 1.0, 0.0).astype(BF)
        total = total + dot(hot, got_ref[e]) + dot(hot, got_ref[8 + e])
    out_ref[0] = total[: rows // 2].astype(BF)
    out_ref[1] = total[rows // 2 :].astype(BF)


def shards(
    queries,
    new_kv,
    cache,
    sinks,
    lengths,
    offsets,
    order,
    residual,
    o_weight,
    ffn_gain,
    router,
    expert_ids,
    w_in,
    w_out,
):
    seq = lax.axis_index(SEQ).astype(jnp.int32).reshape(1)
    core = lax.axis_index("c").astype(jnp.int32).reshape(1)
    swap = [(0, 1), (1, 0)]
    right = [(i, (i + 1) % NZ) for i in range(NZ)]
    left = [(i, (i - 1) % NZ) for i in range(NZ)]
    order_row = order.reshape(1, -1)

    asked = call(
        permute_body,
        shape(32 * ASK, HD),
        "permute",
        3,
        scratch=[pltpu.VMEM((32 * ASK, HD), F32)],
    )(order_row, queries, new_kv)
    w_in, w_out = w_in[0], w_out[0]
    rows = lax.all_to_all(asked, SEQ, split_axis=0, concat_axis=0, tiled=True)

    o_other = lax.ppermute(o_weight, "xh", swap)
    xh = lax.axis_index("xh").astype(jnp.int32).reshape(1)
    o_pair = call(
        pair_body, shape(2, *o_weight.shape), "pair", 3, scalars=1, after=1, nbytes=1 << 19
    )(xh, o_weight, o_other, asked)
    o_all = lax.all_gather(o_pair, "z", axis=0, tiled=False)

    cache_rows = cache.reshape(8192, HD)
    keys, values = split_cycle(cache_rows)
    w_own = unmix(w_in, asked)
    attended, new, w_own = call(
        attend_body,
        [shape(256, HD), shape(128, HD), shape(2, D, 256)],
        "attend",
        7,
        scalars=3,
        after=1,
        keep=True,
        flops=1 << 30,
        nbytes=2 << 20,
        scratch=[
            pltpu.VMEM((256, 4096), F32),
            pltpu.VMEM((8, HD), F32),
            pltpu.VMEM((32 * ASK, HD), F32),
            pltpu.VMEM((256, HD), F32),
        ],
    )(seq, lengths, offsets, rows, sinks.reshape(32, 8, HD), keys, values, w_own)

    owned = lax.all_to_all(attended, SEQ, split_axis=0, concat_axis=0, tiled=True)
    owned_other = lax.ppermute(owned, "c", swap)
    w_other = lax.ppermute(w_own, "c", swap)
    w_out_other = lax.ppermute(w_out, "c", swap)
    share = project(core, owned, owned_other, o_all)
    share = lax.all_to_all(
        share.reshape(16, 64, 256), ("c",) + HEAD, split_axis=0, concat_axis=0, tiled=True
    )
    ids_t = expert_ids.transpose(0, 2, 1)
    hidden, codes, send = call(
        dispatch_body,
        [shape(64, 512, dtype=F32), shape(64, HD, dtype=jnp.int32), shape(16, CAP, 640)],
        "dispatch",
        7,
        flops=1 << 26,
        nbytes=2 << 20,
    )(order_row, share, residual, ffn_gain.reshape(1, -1), router, expert_ids, ids_t)
    cache_out, written = write_cycle(seq, offsets, new, cache_rows, send)
    got = lax.all_to_all(send, ("xh",) + HEAD, split_axis=0, concat_axis=0, tiled=True)
    x, gate = call(
        norm_body,
        [shape(BLOCK, QUARTER), shape(BLOCK, HD, dtype=F32)],
        "norm",
        1,
        after=1,
        flops=1 << 26,
        nbytes=1 << 20,
    )(got, written)

    half = QUARTER // 2
    from_left, from_right = [x], [x]
    for _ in range(3):
        from_left.append(lax.ppermute(from_left[-1], "z", right))
        from_right.append(lax.ppermute(from_right[-1], "z", left))
    far_left = lax.ppermute(from_left[3][:, :half], "z", right)
    far_right = lax.ppermute(from_right[3][:, half:], "z", left)
    blocks = [x] + from_left[1:] + from_right[1:] + [far_left, far_right]
    weights = [
        pltpu.with_memory_space_constraint(w, pltpu.HBM)
        for w in (w_own, w_other, w_out, w_out_other)
    ]
    parts = expert(blocks, *weights)
    own, at_left, at_right, far = parts[0], parts[1:4], parts[4:7], parts[7]

    def add(a, b):
        return (a.astype(F32) + b.astype(F32)).astype(BF)

    to_right = lax.ppermute(far[:, :half], "z", right)
    to_left = lax.ppermute(far[:, half:], "z", left)
    to_right = jnp.concatenate(
        [add(at_right[2][:, :half], to_right), at_right[2][:, half:]], 1
    )
    to_left = jnp.concatenate([at_left[2][:, :half], add(at_left[2][:, half:], to_left)], 1)
    for n in (1, 0):
        to_right = add(at_right[n], lax.ppermute(to_right, "z", right))
        to_left = add(at_left[n], lax.ppermute(to_left, "z", left))
    to_right = lax.ppermute(to_right, "z", right)
    to_left = lax.ppermute(to_left, "z", left)
    back = call(
        gate_body, shape(16, CAP, 512), "gate", 4, flops=1 << 26, nbytes=2 << 20
    )(own, to_right, to_left, gate)
    back = lax.all_to_all(back, ("xh",) + HEAD, split_axis=0, concat_axis=0, tiled=True)
    layer_out = call(
        combine_body, shape(2, 32, 512), "combine", 3, flops=1 << 26, nbytes=1 << 20
    )(hidden, codes, back)
    return (layer_out, cache_out.reshape(cache.shape))


def solution(mesh):
    fine = Mesh(mesh.devices.reshape(2, NZ, 2, 2, 4), SEQ + HEAD)
    return jax.shard_map(
        shards,
        mesh=fine,
        in_specs=(
            P(SEQ, None, HEAD),
            P(SEQ, None, None, HEAD),
            P(SEQ, None, None, HEAD),
            P(None, None, None, HEAD),
            P(),
            P(),
            P(),
            P(SEQ, None, HEAD),
            P(HEAD, SEQ),
            P(HEAD),
            P(HEAD, None),
            P(SEQ, None, None),
            P(HEAD, None, None, SEQ),
            P(HEAD, SEQ, None),
        ),
        out_specs=(P(SEQ, None, HEAD), P(SEQ, None, None, HEAD)),
        check_vma=False,
    )
```

time: 213 us -> 206 us (0.967)
  waiting for transfers between devices: 78 us -> 74.3 us
  other arithmetic: 3.14 us -> 0.43 us
  Pallas kernels: 36 us -> 33.8 us
    ppermute x3, waiting for transfers between devices: 16.8 us -> 0.01 us  [shards(): from_left.append(lax.ppermute(from_left[-1], 'z', right))]
    ppermute x3, waiting for transfers between devices: 0.01 us -> 15.5 us  [shards(): from_right.append(lax.ppermute(from_right[-1], 'z', left))]
    ppermute x3, starting transfers between devices: 9.19 us -> 4.52 us  [shards(): from_right.append(lax.ppermute(from_right[-1], 'z', left))]
    all_to_all x3, starting transfers between devices: 21.4 us -> 24.6 us  [the longest x1 10.4 us: shards(): rows = lax.all_to_all(asked, SEQ, split_axis=0, concat_axis=0, tiled=True)]
    ppermute x1, waiting for transfers between devices: 4.83 us -> 1.68 us  [shards(): o_other = lax.ppermute(o_weight, 'xh', swap)]
    ppermute x5, waiting for transfers between devices: 7.92 us -> 10.9 us  [the longest x1 4.55 us: shards(): to_right = lax.ppermute(far[:, :half], 'z', right)]
    pallas_call x7 -> x9, Pallas kernels: 33.1 us -> 30.8 us  [the longest x1 9.67 us: unmix(): pl.pallas_call(unmix_body, grid=(D // step,), out_shape=shape(2, D, 256),...]
    unnamed x37 -> x36, local copies, waits for them, and re-layouts: 8.81 us -> 9.37 us
  transfers between devices with their start and end apart: 25 -> 25, of which waited for: 13 -> 14; matrix products, arithmetic and copies ran while one was open for 4% -> 0% of each run, Pallas kernels for 11% -> 11%
where the time goes in v2:
time: 206 us; the launch traced here: 204 us
  waiting for transfers between devices  74.3 us (36%)
  starting transfers between devices  57.7 us (28%)
  Pallas kernels  33.8 us (16%)
  between operations  14.3 us (7%)
  blocking collectives  13.9 us (7%)
  local copies, waits for them, and re-layouts  9.43 us (5%)
    ppermute x3, waiting for transfers between devices, shards(): from_right.append(lax.ppermute(from_right[-1], 'z', left))  15.5 us
    all_to_all x1, blocking collectives, shards(): lax.all_to_all(back, ('xh',) + HEAD, split_axis=0, concat_axis=0, tiled=T...  13.9 us
    ppermute x2, waiting for transfers between devices, shards(): to_right = add(at_right[n], lax.ppermute(to_right, 'z', right))  13.8 us
    all_to_all x1, starting transfers between devices, shards(): rows = lax.all_to_all(asked, SEQ, split_axis=0, concat_axis=0, tiled=True)  10.4 us
    all_to_all x1, waiting for transfers between devices, shards(): lax.all_to_all(attended, SEQ, split_axis=0, concat_axis=0, tiled=True)  10.1 us
    all_to_all x1, starting transfers between devices, shards(): lax.all_to_all(attended, SEQ, split_axis=0, concat_axis=0, tiled=True)  9.81 us
    pallas_call x1, Pallas kernels, unmix(): pl.pallas_call(unmix_body, grid=(D // step,), out_shape=shape(2, D, 256),...  9.67 us
    all_to_all x1, waiting for transfers between devices, shards(): lax.all_to_all(share.reshape(16, 64, 256), ('c',) + HEAD, split_axis=0, c...  9.6 us
  transfers between devices with their start and end apart: 25, of which 14 were waited for; matrix products, arithmetic and copies ran while one was open for 0% of the time, Pallas kernels for 11%

profile of v2, /device:TPU:2, one launch (start us, length us, event | category | flops | bytes accessed | tf_op | source)
XLA Modules:
  0.0 204.0 jit_solution(16807777165199112177)
XLA Ops:
  7.2 0.0 all-gather.3.cloned.1.call-start
  7.2 2.2 %collective-permute-start.1 = (bf16[512,128]{1,0:T(8,128)(2,1)}, bf16[512,128]{1,0:T(8,128)(2,1)S(1)}, u32[]{:S(2)}, u32[]{:S(2)}) collective-permute-start(bf16[512,128]{1,0:T(8,128)(2,1)} %own_ref.1), channel_id=1, source_target_pairs={{0,128},{128,0},{1,129},{129,1},{2,130},{130,2},{3,131},{131,3},{4... | collective-permute-start | bytes 393224 | tf_op jit(solution)/shard_map/ppermute | solution.py:546
  9.4 0.8 copy-done.7
  10.3 0.8 copy-done.9
  11.0 0.7 copy-done.12
  11.7 0.9 permute.1.after_ref
  12.6 1.7 collective-permute-done.1.other_ref
  14.2 0.9 copy-done.5
  15.2 0.7 pair.1
  15.9 10.4 %all-to-all-start = ((bf16[32,16,128]{2,1,0:T(8,128)(2,1)}), bf16[32,16,128]{2,1,0:T(8,128)(2,1)S(1)}, u32[]{:S(2)}, u32[]{:S(2)}) async-start(bf16[32,16,128]{2,1,0:T(8,128)(2,1)} %bitcast.3), calls=%async_computation | async-start | bytes 262144 | tf_op jit(solution)/shard_map/all_to_all | solution.py:544
  26.4 2.2 %copy-done.1 = bf16[1,4096,2,256]{3,2,1,0:T(2,128)(2,1)S(1)} copy-done((bf16[1,4096,2,256]{3,2,1,0:T(2,128)(2,1)S(1)}, bf16[1,4096,2,256]{3,2,1,0:T(2,128)(2,1)}, u32[]{:S(2)}) %copy-start.1) | copy-done | bytes 4194328
  28.5 9.7 %unmix.1.weight_ref = bf16[2,4096,256]{2,1,0:T(8,128)(2,1)} custom-call(bf16[4096,2,256]{2,1,0:T(2,128)(2,1)S(1)} %bitcast.19, bf16[512,128]{1,0:T(8,128)(2,1)} %permute.1.after_ref), custom_call_target="tpu_custom_call" | custom-call | flops 1048576 | bytes 16777216 | tf_op jit(solution)/shard_map/unmix/pallas_call | solution.py:246
  38.2 0.5 split_cycle.1
  38.8 1.0 copy-done.3
  39.8 1.2 copy-done.4
  41.0 3.5 %attend.1 = (bf16[256,128]{1,0:T(8,128)(2,1)}, bf16[128,128]{1,0:T(8,128)(2,1)S(1)}, bf16[2,4096,256]{2,1,0:T(8,128)(2,1)}) custom-call(s32[1]{0:T(128)} %bitcast.2.seq_ref, s32[32]{0:T(128)S(1)} %copy-done.15, s32[32]{0:T(128)S(1)} %copy-done.14, bf16[512,128]{1,0:T(8,128)(2,1)S(1)} %bitcast.21, ...), custom_call_target="tpu_custom_call", output_to_operand_aliasing={{2}: (7, {})} | custom-call | flops 1073741824 | bytes 2097152 | tf_op jit(solution)/shard_map/attend/pallas_call | solution.py:556
  44.5 0.3 collective-permute-start.10
  44.8 9.8 %all-to-all-start.1 = ((bf16[32,8,128]{2,1,0:T(8,128)(2,1)}), bf16[32,8,128]{2,1,0:T(8,128)(2,1)S(1)}, u32[]{:S(2)}, u32[]{:S(2)}) async-start(bf16[32,8,128]{2,1,0:T(8,128)(2,1)} %bitcast.8), calls=%async_computation.1 | async-start | bytes 131072 | tf_op jit(solution)/shard_map/all_to_all | solution.py:574
  54.6 0.4 collective-permute-start.11
  55.0 10.1 %all-to-all-done.1 = bf16[32,8,128]{2,1,0:T(8,128)(2,1)S(1)} async-done(((bf16[32,8,128]{2,1,0:T(8,128)(2,1)}), bf16[32,8,128]{2,1,0:T(8,128)(2,1)S(1)}, u32[]{:S(2)}, u32[]{:S(2)}) %all-to-all-start.1) | async-done | bytes 65568 | tf_op jit(solution)/shard_map/all_to_all | solution.py:574
  65.0 1.3 collective-permute-done.other_ref
  66.3 1.6 copy-done.2
  67.9 2.3 %project.1 = bf16[2,8,64,256]{3,2,1,0:T(8,128)(2,1)} custom-call(s32[1]{0:T(128)} %bitcast.1.core_ref, bf16[256,128]{1,0:T(8,128)(2,1)S(1)} %bitcast.23, bf16[256,128]{1,0:T(8,128)(2,1)S(1)} %collective-permute-done.other_ref, bf16[8,2,512,128]{3,2,1,0:T(8,128)(2,1)S(1)} %bitcast.20), custom_call_target="tpu_custom_call" | custom-call | flops 268435456 | bytes 3145728 | tf_op jit(solution)/shard_map/project/pallas_call | solution.py:286
  70.2 5.9 %all-to-all-start.2 = ((bf16[16,64,256]{2,1,0:T(8,128)(2,1)}), bf16[16,64,256]{2,1,0:T(8,128)(2,1)S(1)}, u32[]{:S(2)}, u32[]{:S(2)}) async-start(bf16[16,64,256]{2,1,0:T(8,128)(2,1)} %bitcast.12), calls=%async_computation.2 | async-start | bytes 1048576 | tf_op jit(solution)/shard_map/all_to_all | solution.py:579
  76.1 0.1 copy.20.ids_ref
  76.2 0.1 copy.19.router_ref
  76.3 9.6 %all-to-all-done.2.part_ref = bf16[16,64,256]{2,1,0:T(8,128)(2,1)S(1)} async-done(((bf16[16,64,256]{2,1,0:T(8,128)(2,1)}), bf16[16,64,256]{2,1,0:T(8,128)(2,1)S(1)}, u32[]{:S(2)}, u32[]{:S(2)}) %all-to-all-start.2) | async-done | bytes 524320 | tf_op jit(solution)/shard_map/all_to_all | solution.py:579
  86.0 1.5 dispatch.1
  87.4 4.3 %all-to-all-start.3 = ((bf16[16,18,640]{2,1,0:T(8,128)(2,1)}), bf16[16,18,640]{2,1,0:T(8,128)(2,1)S(1)}, u32[]{:S(2)}, u32[]{:S(2)}) async-start(bf16[16,18,640]{2,1,0:T(8,128)(2,1)} %get-tuple-element.27.after_ref), calls=%async_computation.3 | async-start | bytes 983040 | tf_op jit(solution)/shard_map/all_to_all | solution.py:592
  91.7 2.7 %write_cycle.1 = (bf16[8192,128]{1,0:T(8,128)(2,1)}, f32[8,128]{1,0:T(8,128)S(1)}) custom-call(s32[1]{0:T(128)} %bitcast.2.seq_ref, s32[32]{0:T(128)S(1)} %copy-done.14, bf16[128,128]{1,0:T(8,128)(2,1)S(1)} %get-tuple-element.28.new_ref, bf16[8192,128]{1,0:T(8,128)(2,1)S(1)} %bitcast.18, bf16[16,18,640]{2,1,0:T(8,128)(2,1)} %get-tuple-element.27.after_ref), custom_call_target="tpu_custom_call" | custom-call | flops 16777216 | bytes 16777216 | tf_op jit(solution)/shard_map/write_cycle/pallas_call | solution.py:210
  94.4 7.0 %all-to-all-done.3.got_ref = bf16[16,18,640]{2,1,0:T(8,128)(2,1)S(1)} async-done(((bf16[16,18,640]{2,1,0:T(8,128)(2,1)}), bf16[16,18,640]{2,1,0:T(8,128)(2,1)S(1)}, u32[]{:S(2)}, u32[]{:S(2)}) %all-to-all-start.3) | async-done | bytes 368672 | tf_op jit(solution)/shard_map/all_to_all | solution.py:592
  101.4 1.0 norm.1
  102.4 0.3 collective-permute-start.5
  102.6 1.9 collective-permute-start.2
  104.5 6.0 %collective-permute-done.5.refs_4_ = bf16[144,1024]{1,0:T(8,128)(2,1)S(1)} collective-permute-done((bf16[144,1024]{1,0:T(8,128)(2,1)S(1)}, bf16[144,1024]{1,0:T(8,128)(2,1)S(1)}, u32[]{:S(2)}, u32[]{:S(2)}) %collective-permute-start.5) | collective-permute-done | bytes 294944 | tf_op jit(solution)/shard_map/ppermute | solution.py:607
  110.5 1.5 collective-permute-start.6
  112.0 0.5 collective-permute-start.3
  112.5 5.1 %collective-permute-done.6.refs_5_ = bf16[144,1024]{1,0:T(8,128)(2,1)S(1)} collective-permute-done((bf16[144,1024]{1,0:T(8,128)(2,1)S(1)}, bf16[144,1024]{1,0:T(8,128)(2,1)S(1)}, u32[]{:S(2)}, u32[]{:S(2)}) %collective-permute-start.6) | collective-permute-done | bytes 294944 | tf_op jit(solution)/shard_map/ppermute | solution.py:607
  117.7 2.8 %collective-permute-start.7 = (bf16[144,1024]{1,0:T(8,128)(2,1)S(1)}, bf16[144,1024]{1,0:T(8,128)(2,1)S(1)}, u32[]{:S(2)}, u32[]{:S(2)}) collective-permute-start(bf16[144,1024]{1,0:T(8,128)(2,1)S(1)} %collective-permute-done.6.refs_5_), channel_id=1, source_target_pairs={{0,112},{16,0},{32,16},{48,32},{64,48},{80,64},{96,80},{112,96},{1... | collective-permute-start | bytes 884744 | tf_op jit(solution)/shard_map/ppermute | solution.py:607
  120.4 4.4 %collective-permute-done.7.refs_6_ = bf16[144,1024]{1,0:T(8,128)(2,1)S(1)} collective-permute-done((bf16[144,1024]{1,0:T(8,128)(2,1)S(1)}, bf16[144,1024]{1,0:T(8,128)(2,1)S(1)}, u32[]{:S(2)}, u32[]{:S(2)}) %collective-permute-start.7) | collective-permute-done | bytes 294944 | tf_op jit(solution)/shard_map/ppermute | solution.py:607
  124.8 3.6 %collective-permute-start.9 = (bf16[144,512]{1,0:T(8,128)(2,1)S(1)}, bf16[144,512]{1,0:T(8,128)(2,1)S(1)}, u32[]{:S(2)}, u32[]{:S(2)}) collective-permute-start(bf16[144,512]{1,0:T(8,128)(2,1)S(1)} %slice.33), channel_id=1, source_target_pairs={{0,112},{16,0},{32,16},{48,32},{64,48},{80,64},{96,80},{112,96},{1... | collective-permute-start | bytes 442376 | tf_op jit(solution)/shard_map/ppermute | solution.py:609
  128.5 0.1 collective-permute-start.8
  128.6 2.5 %collective-permute-done.9.refs_8_ = bf16[144,512]{1,0:T(8,128)(2,1)S(1)} collective-permute-done((bf16[144,512]{1,0:T(8,128)(2,1)S(1)}, bf16[144,512]{1,0:T(8,128)(2,1)S(1)}, u32[]{:S(2)}, u32[]{:S(2)}) %collective-permute-start.9) | collective-permute-done | bytes 147488 | tf_op jit(solution)/shard_map/ppermute | solution.py:609
  131.1 3.8 %collective-permute-done.8.refs_7_ = bf16[144,512]{1,0:T(8,128)(2,1)S(1)} collective-permute-done((bf16[144,512]{1,0:T(8,128)(2,1)S(1)}, bf16[144,512]{1,0:T(8,128)(2,1)S(1)}, u32[]{:S(2)}, u32[]{:S(2)}) %collective-permute-start.8) | collective-permute-done | bytes 147488 | tf_op jit(solution)/shard_map/ppermute | solution.py:608
  134.9 9.5 %expert.1 = (bf16[144,1024]{1,0:T(8,128)(2,1)S(1)}, bf16[144,1024]{1,0:T(8,128)(2,1)S(1)}, bf16[144,1024]{1,0:T(8,128)(2,1)S(1)}, bf16[144,1024]{1,0:T(8,128)(2,...) custom-call(bf16[144,1024]{1,0:T(8,128)(2,1)S(1)} %get-tuple-element, ...), custom_call_target="tpu_custom_call" | custom-call | flops 4294967296 | bytes 14680064 | tf_op jit(solution)/shard_map/expert/pallas_call | solution.py:467
  144.5 0.1 collective-permute-start.12
  144.6 3.3 %collective-permute-start.16 = (bf16[144,512]{1,0:T(8,128)(2,1)S(1)}, bf16[144,512]{1,0:T(8,128)(2,1)S(1)}, u32[]{:S(2)}, u32[]{:S(2)}) collective-permute-start(bf16[144,512]{1,0:T(8,128)(2,1)S(1)} %get-tuple-element.42), channel_id=1, source_target_pairs={{0,112},{16,0},{32,16},{48,32},{64,48},{80,64},{96,80},{112,96},{1... | collective-permute-start | bytes 442376 | tf_op jit(solution)/shard_map/ppermute | solution.py:622
  147.9 4.5 %collective-permute-done.12 = bf16[144,512]{1,0:T(8,128)(2,1)S(1)} collective-permute-done((bf16[144,512]{1,0:T(8,128)(2,1)S(1)}, bf16[144,512]{1,0:T(8,128)(2,1)S(1)}, u32[]{:S(2)}, u32[]{:S(2)}) %collective-permute-start.12) | collective-permute-done | bytes 147488 | tf_op jit(solution)/shard_map/ppermute | solution.py:621
  152.5 0.1 collective-permute-start.13
  152.7 3.3 %collective-permute-start.17 = (bf16[144,1024]{1,0:T(8,128)(2,1)S(1)}, bf16[144,1024]{1,0:T(8,128)(2,1)S(1)}, u32[]{:S(2)}, u32[]{:S(2)}) collective-permute-start(bf16[144,1024]{1,0:T(8,128)(2,1)S(1)} %pad_maximum_fusion.1), channel_id=1, source_target_pairs={{0,112},{16,0},{32,16},{48,32},{64,48},{80,64},{96,80},{112,96},{1... | collective-permute-start | bytes 884744 | tf_op jit(solution)/shard_map/ppermute | solution.py:629
  156.0 7.4 %collective-permute-done.13 = bf16[144,1024]{1,0:T(8,128)(2,1)S(1)} collective-permute-done((bf16[144,1024]{1,0:T(8,128)(2,1)S(1)}, bf16[144,1024]{1,0:T(8,128)(2,1)S(1)}, u32[]{:S(2)}, u32[]{:S(2)}) %collective-permute-start.13) | collective-permute-done | bytes 294944 | tf_op jit(solution)/shard_map/ppermute | solution.py:628
  163.5 0.1 add_convert_fusion.3
  163.5 0.1 collective-permute-start.14
  163.6 0.1 add_convert_fusion.1
  163.7 3.5 %collective-permute-start.18 = (bf16[144,1024]{1,0:T(8,128)(2,1)S(1)}, bf16[144,1024]{1,0:T(8,128)(2,1)S(1)}, u32[]{:S(2)}, u32[]{:S(2)}) collective-permute-start(bf16[144,1024]{1,0:T(8,128)(2,1)S(1)} %add_convert_fusion.1), channel_id=1, source_target_pairs={{0,112},{16,0},{32,16},{48,32},{64,48},{80,64},{96,80},{112,96},{1... | collective-permute-start | bytes 884744 | tf_op jit(solution)/shard_map/ppermute | solution.py:629
  167.2 6.4 %collective-permute-done.14 = bf16[144,1024]{1,0:T(8,128)(2,1)S(1)} collective-permute-done((bf16[144,1024]{1,0:T(8,128)(2,1)S(1)}, bf16[144,1024]{1,0:T(8,128)(2,1)S(1)}, u32[]{:S(2)}, u32[]{:S(2)}) %collective-permute-start.14) | collective-permute-done | bytes 294944 | tf_op jit(solution)/shard_map/ppermute | solution.py:628
  173.6 0.1 add_convert_fusion.2
  173.7 0.1 collective-permute-start.15
  173.8 0.1 add_convert_fusion
  173.9 3.3 %collective-permute-start.19 = (bf16[144,1024]{1,0:T(8,128)(2,1)S(1)}, bf16[144,1024]{1,0:T(8,128)(2,1)S(1)}, u32[]{:S(2)}, u32[]{:S(2)}) collective-permute-start(bf16[144,1024]{1,0:T(8,128)(2,1)S(1)} %add_convert_fusion), channel_id=1, source_target_pairs={{0,112},{16,0},{32,16},{48,32},{64,48},{80,64},{96,80},{112,96},{1... | collective-permute-start | bytes 884744 | tf_op jit(solution)/shard_map/ppermute | solution.py:631
  177.1 4.5 %collective-permute-done.15.right_ref = bf16[144,1024]{1,0:T(8,128)(2,1)S(1)} collective-permute-done((bf16[144,1024]{1,0:T(8,128)(2,1)S(1)}, bf16[144,1024]{1,0:T(8,128)(2,1)S(1)}, u32[]{:S(2)}, u32[]{:S(2)}) %collective-permute-start.15) | collective-permute-done | bytes 294944 | tf_op jit(solution)/shard_map/ppermute | solution.py:630
  181.7 0.4 gate.1
  182.1 13.9 %all_to_all.37.got_ref = bf16[16,18,512]{2,1,0:T(8,128)(2,1)S(1)} all-to-all(bf16[16,18,512]{2,1,0:T(8,128)(2,1)S(1)} %gate.1), channel_id=1, replica_groups=mesh['xh'=2,'z'=8,'c'=2,'xl'=2,'y'=4] {'xh','xl','y'}, dimensions={0} | all-to-all | bytes 589824 | tf_op jit(solution)/shard_map/all_to_all | solution.py:635
  196.0 1.1 combine.1
  (49 shorter events, 0.3 us)
Async XLA Ops:
  7.2 59.1 %all-gather.3.cloned.1.call-start = ((), (), s32[]{:S(2)}) async-start(), calls=%async_computation.5 | async-start | bytes 2359296 | tf_op jit(solution)/shard_map/all_gather | solution.py:551
  7.2 7.0 %collective-permute-start.1 = (bf16[512,128]{1,0:T(8,128)(2,1)}, bf16[512,128]{1,0:T(8,128)(2,1)S(1)}, u32[]{:S(2)}, u32[]{:S(2)}) collective-permute-start(bf16[512,128]{1,0:T(8,128)(2,1)} %own_ref.1), channel_id=1, source_target_pairs={{0,128},{128,0},{1,129},{129,1},{2,130},{130,2},{3,131},{131,3},{4... | collective-permute-start | bytes 393224 | tf_op jit(solution)/shard_map/ppermute | solution.py:546
  9.4 0.8 copy-start.7
  10.3 0.8 copy-start.9
  11.0 0.7 copy-start.12
  14.2 0.9 copy-start.5
  15.9 23.8 %all-to-all-start = ((bf16[32,16,128]{2,1,0:T(8,128)(2,1)}), bf16[32,16,128]{2,1,0:T(8,128)(2,1)S(1)}, u32[]{:S(2)}, u32[]{:S(2)}) async-start(bf16[32,16,128]{2,1,0:T(8,128)(2,1)} %bitcast.3), calls=%async_computation | async-start | bytes 262144 | tf_op jit(solution)/shard_map/all_to_all | solution.py:544
  26.4 2.2 %copy-start.1 = (bf16[1,4096,2,256]{3,2,1,0:T(2,128)(2,1)S(1)}, bf16[1,4096,2,256]{3,2,1,0:T(2,128)(2,1)}, u32[]{:S(2)}) copy-start(bf16[1,4096,2,256]{3,2,1,0:T(2,128)(2,1)} %param.26) | copy-start | bytes 12582916
  28.5 9.7 %copy-start = (bf16[1,4096,2,128]{3,2,1,0:T(2,128)(2,1)S(1)}, bf16[1,4096,2,128]{3,2,1,0:T(2,128)(2,1)}, u32[]{:S(2)}) copy-start(bf16[1,4096,2,128]{3,2,1,0:T(2,128)(2,1)} %param.16) | copy-start | bytes 6291460
  38.2 1.5 copy-start.6
  38.2 1.5 copy-start.14
  38.2 1.5 copy-start.15
  38.8 1.0 copy-start.3
  39.8 1.2 copy-start.4
  44.5 31.6 %copy-start.10 = (s32[2,32,2]{1,2,0:T(2,128)S(1)}, s32[2,32,2]{1,2,0:T(2,128)}, u32[]{:S(2)}) copy-start(s32[2,32,2]{1,2,0:T(2,128)} %param.25) | copy-start | bytes 1540
  44.5 31.7 %copy-start.16 = (f32[512,8]{0,1:T(8,128)S(1)}, f32[512,8]{0,1:T(8,128)}, u32[]{:S(2)}) copy-start(f32[512,8]{0,1:T(8,128)} %param.24) | copy-start | bytes 49156
  44.5 84.1 %collective-permute-start.10 = (bf16[2,4096,256]{2,1,0:T(8,128)(2,1)}, bf16[2,4096,256]{2,1,0:T(8,128)(2,1)}, u32[]{:S(2)}, u32[]{:S(2)}) collective-permute-start(bf16[2,4096,256]{2,1,0:T(8,128)(2,1)} %get-tuple-element.31.refs_9_), channel_id=1, source_target_pairs={{0,8},{8,0},{1,9},{9,1},{2,10},{10,2},{3,11},{11,3},{4,12},{12,4},... | collective-permute-start | bytes 12582920 | tf_op jit(solution)/shard_map/ppermute | solution.py:576
  44.8 41.2 %copy-start.8 = (bf16[2,32,512]{2,1,0:T(8,128)(2,1)S(1)}, bf16[2,32,512]{2,1,0:T(8,128)(2,1)}, u32[]{:S(2)}) copy-start(bf16[2,32,512]{2,1,0:T(8,128)(2,1)} %res_ref.1) | copy-start | bytes 196612
  44.8 41.2 %copy-start.11 = (f32[512]{0:T(512)S(1)}, f32[512]{0:T(512)}, u32[]{:S(2)}) copy-start(f32[512]{0:T(512)} %param.23) | copy-start | bytes 6148
  44.8 41.2 %copy-start.13 = (s32[32]{0:T(128)S(1)}, s32[32]{0:T(128)}, u32[]{:S(2)}) copy-start(s32[32]{0:T(128)} %param.20) | copy-start | bytes 388
  44.8 20.2 %all-to-all-start.1 = ((bf16[32,8,128]{2,1,0:T(8,128)(2,1)}), bf16[32,8,128]{2,1,0:T(8,128)(2,1)S(1)}, u32[]{:S(2)}, u32[]{:S(2)}) async-start(bf16[32,8,128]{2,1,0:T(8,128)(2,1)} %bitcast.8), calls=%async_computation.1 | async-start | bytes 131072 | tf_op jit(solution)/shard_map/all_to_all | solution.py:574
  54.6 74.0 %collective-permute-start.11 = (bf16[256,4096]{1,0:T(8,128)(2,1)}, bf16[256,4096]{1,0:T(8,128)(2,1)}, u32[]{:S(2)}, u32[]{:S(2)}) collective-permute-start(bf16[256,4096]{1,0:T(8,128)(2,1)} %bitcast.29), channel_id=1, source_target_pairs={{0,8},{8,0},{1,9},{9,1},{2,10},{10,2},{3,11},{11,3},{4,12},{12,4},... | collective-permute-start | bytes 6291464 | tf_op jit(solution)/shard_map/ppermute | solution.py:577
  65.0 1.3 collective-permute-start
  66.3 1.6 copy-start.2
  70.2 15.8 %all-to-all-start.2 = ((bf16[16,64,256]{2,1,0:T(8,128)(2,1)}), bf16[16,64,256]{2,1,0:T(8,128)(2,1)S(1)}, u32[]{:S(2)}, u32[]{:S(2)}) async-start(bf16[16,64,256]{2,1,0:T(8,128)(2,1)} %bitcast.12), calls=%async_computation.2 | async-start | bytes 1048576 | tf_op jit(solution)/shard_map/all_to_all | solution.py:579
  87.4 14.0 %all-to-all-start.3 = ((bf16[16,18,640]{2,1,0:T(8,128)(2,1)}), bf16[16,18,640]{2,1,0:T(8,128)(2,1)S(1)}, u32[]{:S(2)}, u32[]{:S(2)}) async-start(bf16[16,18,640]{2,1,0:T(8,128)(2,1)} %get-tuple-element.27.after_ref), calls=%async_computation.3 | async-start | bytes 983040 | tf_op jit(solution)/shard_map/all_to_all | solution.py:592
  102.4 8.1 %collective-permute-start.5 = (bf16[144,1024]{1,0:T(8,128)(2,1)S(1)}, bf16[144,1024]{1,0:T(8,128)(2,1)S(1)}, u32[]{:S(2)}, u32[]{:S(2)}) collective-permute-start(bf16[144,1024]{1,0:T(8,128)(2,1)S(1)} %get-tuple-element.30.refs_0_), channel_id=1, source_target_pairs={{0,112},{16,0},{32,16},{48,32},{64,48},{80,64},{96,80},{112,96},{1... | collective-permute-start | bytes 884744 | tf_op jit(solution)/shard_map/ppermute | solution.py:607
  102.6 9.4 %collective-permute-start.2 = (bf16[144,1024]{1,0:T(8,128)(2,1)S(1)}, bf16[144,1024]{1,0:T(8,128)(2,1)S(1)}, u32[]{:S(2)}, u32[]{:S(2)}) collective-permute-start(bf16[144,1024]{1,0:T(8,128)(2,1)S(1)} %get-tuple-element.30.refs_0_), channel_id=1, source_target_pairs={{0,16},{16,32},{32,48},{48,64},{64,80},{80,96},{96,112},{112,0},{1... | collective-permute-start | bytes 884744 | tf_op jit(solution)/shard_map/ppermute | solution.py:606
  110.5 7.2 %collective-permute-start.6 = (bf16[144,1024]{1,0:T(8,128)(2,1)S(1)}, bf16[144,1024]{1,0:T(8,128)(2,1)S(1)}, u32[]{:S(2)}, u32[]{:S(2)}) collective-permute-start(bf16[144,1024]{1,0:T(8,128)(2,1)S(1)} %collective-permute-done.5.refs_4_), channel_id=1, source_target_pairs={{0,112},{16,0},{32,16},{48,32},{64,48},{80,64},{96,80},{112,96},{1... | collective-permute-start | bytes 884744 | tf_op jit(solution)/shard_map/ppermute | solution.py:607
  112.0 8.4 %collective-permute-start.3 = (bf16[144,1024]{1,0:T(8,128)(2,1)S(1)}, bf16[144,1024]{1,0:T(8,128)(2,1)S(1)}, u32[]{:S(2)}, u32[]{:S(2)}) collective-permute-start(bf16[144,1024]{1,0:T(8,128)(2,1)S(1)} %collective-permute-done.2.refs_1_), channel_id=1, source_target_pairs={{0,16},{16,32},{32,48},{48,64},{64,80},{80,96},{96,112},{112,0},{1... | collective-permute-start | bytes 884744 | tf_op jit(solution)/shard_map/ppermute | solution.py:606
  117.7 7.1 %collective-permute-start.7 = (bf16[144,1024]{1,0:T(8,128)(2,1)S(1)}, bf16[144,1024]{1,0:T(8,128)(2,1)S(1)}, u32[]{:S(2)}, u32[]{:S(2)}) collective-permute-start(bf16[144,1024]{1,0:T(8,128)(2,1)S(1)} %collective-permute-done.6.refs_5_), channel_id=1, source_target_pairs={{0,112},{16,0},{32,16},{48,32},{64,48},{80,64},{96,80},{112,96},{1... | collective-permute-start | bytes 884744 | tf_op jit(solution)/shard_map/ppermute | solution.py:607
  120.4 8.0 %collective-permute-start.4 = (bf16[144,1024]{1,0:T(8,128)(2,1)S(1)}, bf16[144,1024]{1,0:T(8,128)(2,1)S(1)}, u32[]{:S(2)}, u32[]{:S(2)}) collective-permute-start(bf16[144,1024]{1,0:T(8,128)(2,1)S(1)} %collective-permute-done.3.refs_2_), channel_id=1, source_target_pairs={{0,16},{16,32},{32,48},{48,64},{64,80},{80,96},{96,112},{112,0},{1... | collective-permute-start | bytes 884744 | tf_op jit(solution)/shard_map/ppermute | solution.py:606
  124.8 6.3 %collective-permute-start.9 = (bf16[144,512]{1,0:T(8,128)(2,1)S(1)}, bf16[144,512]{1,0:T(8,128)(2,1)S(1)}, u32[]{:S(2)}, u32[]{:S(2)}) collective-permute-start(bf16[144,512]{1,0:T(8,128)(2,1)S(1)} %slice.33), channel_id=1, source_target_pairs={{0,112},{16,0},{32,16},{48,32},{64,48},{80,64},{96,80},{112,96},{1... | collective-permute-start | bytes 442376 | tf_op jit(solution)/shard_map/ppermute | solution.py:609
  128.5 6.4 %collective-permute-start.8 = (bf16[144,512]{1,0:T(8,128)(2,1)S(1)}, bf16[144,512]{1,0:T(8,128)(2,1)S(1)}, u32[]{:S(2)}, u32[]{:S(2)}) collective-permute-start(bf16[144,512]{1,0:T(8,128)(2,1)S(1)} %slice.32), channel_id=1, source_target_pairs={{0,16},{16,32},{32,48},{48,64},{64,80},{80,96},{96,112},{112,0},{1... | collective-permute-start | bytes 442376 | tf_op jit(solution)/shard_map/ppermute | solution.py:608
  144.5 8.0 %collective-permute-start.12 = (bf16[144,512]{1,0:T(8,128)(2,1)S(1)}, bf16[144,512]{1,0:T(8,128)(2,1)S(1)}, u32[]{:S(2)}, u32[]{:S(2)}) collective-permute-start(bf16[144,512]{1,0:T(8,128)(2,1)S(1)} %get-tuple-element.43), channel_id=1, source_target_pairs={{0,16},{16,32},{32,48},{48,64},{64,80},{80,96},{96,112},{112,0},{1... | collective-permute-start | bytes 442376 | tf_op jit(solution)/shard_map/ppermute | solution.py:621
  144.6 8.0 %collective-permute-start.16 = (bf16[144,512]{1,0:T(8,128)(2,1)S(1)}, bf16[144,512]{1,0:T(8,128)(2,1)S(1)}, u32[]{:S(2)}, u32[]{:S(2)}) collective-permute-start(bf16[144,512]{1,0:T(8,128)(2,1)S(1)} %get-tuple-element.42), channel_id=1, source_target_pairs={{0,112},{16,0},{32,16},{48,32},{64,48},{80,64},{96,80},{112,96},{1... | collective-permute-start | bytes 442376 | tf_op jit(solution)/shard_map/ppermute | solution.py:622
  152.5 10.9 %collective-permute-start.13 = (bf16[144,1024]{1,0:T(8,128)(2,1)S(1)}, bf16[144,1024]{1,0:T(8,128)(2,1)S(1)}, u32[]{:S(2)}, u32[]{:S(2)}) collective-permute-start(bf16[144,1024]{1,0:T(8,128)(2,1)S(1)} %pad_maximum_fusion), channel_id=1, source_target_pairs={{0,16},{16,32},{32,48},{48,64},{64,80},{80,96},{96,112},{112,0},{1... | collective-permute-start | bytes 884744 | tf_op jit(solution)/shard_map/ppermute | solution.py:628
  152.7 10.9 %collective-permute-start.17 = (bf16[144,1024]{1,0:T(8,128)(2,1)S(1)}, bf16[144,1024]{1,0:T(8,128)(2,1)S(1)}, u32[]{:S(2)}, u32[]{:S(2)}) collective-permute-start(bf16[144,1024]{1,0:T(8,128)(2,1)S(1)} %pad_maximum_fusion.1), channel_id=1, source_target_pairs={{0,112},{16,0},{32,16},{48,32},{64,48},{80,64},{96,80},{112,96},{1... | collective-permute-start | bytes 884744 | tf_op jit(solution)/shard_map/ppermute | solution.py:629
  163.5 10.1 %collective-permute-start.14 = (bf16[144,1024]{1,0:T(8,128)(2,1)S(1)}, bf16[144,1024]{1,0:T(8,128)(2,1)S(1)}, u32[]{:S(2)}, u32[]{:S(2)}) collective-permute-start(bf16[144,1024]{1,0:T(8,128)(2,1)S(1)} %add_convert_fusion.3), channel_id=1, source_target_pairs={{0,16},{16,32},{32,48},{48,64},{64,80},{80,96},{96,112},{112,0},{1... | collective-permute-start | bytes 884744 | tf_op jit(solution)/shard_map/ppermute | solution.py:628
  163.7 10.0 %collective-permute-start.18 = (bf16[144,1024]{1,0:T(8,128)(2,1)S(1)}, bf16[144,1024]{1,0:T(8,128)(2,1)S(1)}, u32[]{:S(2)}, u32[]{:S(2)}) collective-permute-start(bf16[144,1024]{1,0:T(8,128)(2,1)S(1)} %add_convert_fusion.1), channel_id=1, source_target_pairs={{0,112},{16,0},{32,16},{48,32},{64,48},{80,64},{96,80},{112,96},{1... | collective-permute-start | bytes 884744 | tf_op jit(solution)/shard_map/ppermute | solution.py:629
  173.7 8.0 %collective-permute-start.15 = (bf16[144,1024]{1,0:T(8,128)(2,1)S(1)}, bf16[144,1024]{1,0:T(8,128)(2,1)S(1)}, u32[]{:S(2)}, u32[]{:S(2)}) collective-permute-start(bf16[144,1024]{1,0:T(8,128)(2,1)S(1)} %add_convert_fusion.2), channel_id=1, source_target_pairs={{0,16},{16,32},{32,48},{48,64},{64,80},{80,96},{96,112},{112,0},{1... | collective-permute-start | bytes 884744 | tf_op jit(solution)/shard_map/ppermute | solution.py:630
  173.9 7.8 %collective-permute-start.19 = (bf16[144,1024]{1,0:T(8,128)(2,1)S(1)}, bf16[144,1024]{1,0:T(8,128)(2,1)S(1)}, u32[]{:S(2)}, u32[]{:S(2)}) collective-permute-start(bf16[144,1024]{1,0:T(8,128)(2,1)S(1)} %add_convert_fusion), channel_id=1, source_target_pairs={{0,112},{16,0},{32,16},{48,32},{64,48},{80,64},{96,80},{112,96},{1... | collective-permute-start | bytes 884744 | tf_op jit(solution)/shard_map/ppermute | solution.py:631
Sparse Core Ops, SparseCore 0:
  16.0 44.9 all-gather.2

commit v3 on v2

--- a/solution.py
+++ b/solution.py
@@ -236,6 +236,10 @@
     out_ref[1 - xh] = other_ref[...]
 
 
+def pass_body(first_ref, weight_ref, out_ref, weight_out_ref):
+    out_ref[...] = first_ref[0:8, :]
+
+
 def unmix_body(w_ref, after_ref, out_ref):
     for k in range(2):
         out_ref[k] = w_ref[:, k, :]
@@ -573,8 +577,11 @@
 
     owned = lax.all_to_all(attended, SEQ, split_axis=0, concat_axis=0, tiled=True)
     owned_other = lax.ppermute(owned, "c", swap)
+    w_out_other = lax.ppermute(w_out, "c", swap)
+    _, w_own = call(
+        pass_body, [shape(8, HD), shape(2, D, 256)], "pass_on", 1, after=1, keep=True
+    )(owned_other.reshape(-1, HD), w_own)
     w_other = lax.ppermute(w_own, "c", swap)
-    w_out_other = lax.ppermute(w_out, "c", swap)
     share = project(core, owned, owned_other, o_all)
     share = lax.all_to_all(
         share.reshape(16, 64, 256), ("c",) + HEAD, split_axis=0, concat_axis=0, tiled=True

time: 206 us -> 206 us (level)
  blocking collectives: 13.9 us -> 34.1 us
  waiting for transfers between devices: 74.3 us -> 64.4 us
  starting transfers between devices: 57.7 us -> 48.1 us
    all_to_all x0 -> x1, blocking collectives: none -> 20.4 us  [shards(): lax.all_to_all(attended, SEQ, split_axis=0, concat_axis=0, tiled=True)]
    all_to_all x1 -> x0, waiting for transfers between devices: 10.1 us -> none  [shards(): lax.all_to_all(attended, SEQ, split_axis=0, concat_axis=0, tiled=True)]
    all_to_all x1 -> x0, starting transfers between devices: 9.81 us -> none  [shards(): lax.all_to_all(attended, SEQ, split_axis=0, concat_axis=0, tiled=True)]
  transfers between devices with their start and end apart: 25 -> 24, of which waited for: 14 -> 13; matrix products, arithmetic and copies ran while one was open for 0% -> 0% of each run, Pallas kernels for 11% -> 11%
where the time goes in v3:
time: 206 us; the launch traced here: 204 us
  waiting for transfers between devices  64.4 us (31%)
  starting transfers between devices  48.1 us (23%)
  blocking collectives  34.1 us (17%)
  Pallas kernels  33.7 us (16%)
  between operations  14.3 us (7%)
  local copies, waits for them, and re-layouts  9.44 us (5%)
    all_to_all x1, blocking collectives, shards(): lax.all_to_all(attended, SEQ, split_axis=0, concat_axis=0, tiled=True)  20.4 us
    ppermute x3, waiting for transfers between devices, shards(): from_right.append(lax.ppermute(from_right[-1], 'z', left))  15.4 us
    ppermute x2, waiting for transfers between devices, shards(): to_right = add(at_right[n], lax.ppermute(to_right, 'z', right))  14 us
    all_to_all x1, blocking collectives, shards(): lax.all_to_all(back, ('xh',) + HEAD, split_axis=0, concat_axis=0, tiled=T...  13.7 us
    all_to_all x1, starting transfers between devices, shards(): rows = lax.all_to_all(asked, SEQ, split_axis=0, concat_axis=0, tiled=True)  10.4 us
    pallas_call x1, Pallas kernels, unmix(): pl.pallas_call(unmix_body, grid=(D // step,), out_shape=shape(2, D, 256),...  9.71 us
    all_to_all x1, waiting for transfers between devices, shards(): lax.all_to_all(share.reshape(16, 64, 256), ('c',) + HEAD, split_axis=0, c...  9.6 us
    pallas_call x1, Pallas kernels, expert(): pl.pallas_call(expert_body, grid=(8,), out_shape=[shape(BLOCK, QUARTER)]...  9.52 us
  transfers between devices with their start and end apart: 24, of which 13 were waited for; matrix products, arithmetic and copies ran while one was open for 0% of the time, Pallas kernels for 11%

profile of v3, /device:TPU:2, one launch (start us, length us, event | category | flops | bytes accessed | tf_op | source)
XLA Modules:
  0.0 204.5 jit_solution(9877671455940407774)
XLA Ops:
  7.2 0.0 all-gather.3.cloned.1.call-start
  7.2 2.2 %collective-permute-start.1 = (bf16[512,128]{1,0:T(8,128)(2,1)}, bf16[512,128]{1,0:T(8,128)(2,1)S(1)}, u32[]{:S(2)}, u32[]{:S(2)}) collective-permute-start(bf16[512,128]{1,0:T(8,128)(2,1)} %own_ref.1), channel_id=1, source_target_pairs={{0,128},{128,0},{1,129},{129,1},{2,130},{130,2},{3,131},{131,3},{4... | collective-permute-start | bytes 393224 | tf_op jit(solution)/shard_map/ppermute | solution.py:550
  9.4 0.8 copy-done.7
  10.3 0.8 copy-done.9
  11.0 0.7 copy-done.12
  11.7 0.9 permute.1.after_ref
  12.6 1.7 collective-permute-done.1.other_ref
  14.2 0.9 copy-done.5
  15.2 0.7 pair.1
  15.9 10.4 %all-to-all-start = ((bf16[32,16,128]{2,1,0:T(8,128)(2,1)}), bf16[32,16,128]{2,1,0:T(8,128)(2,1)S(1)}, u32[]{:S(2)}, u32[]{:S(2)}) async-start(bf16[32,16,128]{2,1,0:T(8,128)(2,1)} %bitcast.3), calls=%async_computation | async-start | bytes 262144 | tf_op jit(solution)/shard_map/all_to_all | solution.py:548
  26.4 2.2 %copy-done.1 = bf16[1,4096,2,256]{3,2,1,0:T(2,128)(2,1)S(1)} copy-done((bf16[1,4096,2,256]{3,2,1,0:T(2,128)(2,1)S(1)}, bf16[1,4096,2,256]{3,2,1,0:T(2,128)(2,1)}, u32[]{:S(2)}) %copy-start.1) | copy-done | bytes 4194328
  28.6 9.7 %unmix.1.weight_ref = bf16[2,4096,256]{2,1,0:T(8,128)(2,1)} custom-call(bf16[4096,2,256]{2,1,0:T(2,128)(2,1)S(1)} %bitcast.19, bf16[512,128]{1,0:T(8,128)(2,1)} %permute.1.after_ref), custom_call_target="tpu_custom_call" | custom-call | flops 1048576 | bytes 16777216 | tf_op jit(solution)/shard_map/unmix/pallas_call | solution.py:250
  38.3 0.5 split_cycle.1
  38.8 1.0 copy-done.3
  39.8 1.2 copy-done.4
  41.0 2.9 %attend.1 = (bf16[256,128]{1,0:T(8,128)(2,1)S(1)}, bf16[128,128]{1,0:T(8,128)(2,1)S(1)}, bf16[2,4096,256]{2,1,0:T(8,128)(2,1)}) custom-call(s32[1]{0:T(128)} %bitcast.2.seq_ref, s32[32]{0:T(128)S(1)} %copy-done.15, s32[32]{0:T(128)S(1)} %copy-done.14, bf16[512,128]{1,0:T(8,128)(2,1)S(1)} %bitcast.21, ...), custom_call_target="tpu_custom_call", output_to_operand_aliasing={{2}: (7, {})} | custom-call | flops 1073741824 | bytes 2097152 | tf_op jit(solution)/shard_map/attend/pallas_call | solution.py:560
  43.9 20.4 %all_to_all.37 = bf16[32,8,128]{2,1,0:T(8,128)(2,1)S(1)} all-to-all(bf16[32,8,128]{2,1,0:T(8,128)(2,1)S(1)} %bitcast.25), channel_id=1, replica_groups=mesh['xh'=2,'z'=8,'c'=2,'xl'=2,'y'=4] {'xh','z','c'}, dimensions={0} | all-to-all | bytes 131072 | tf_op jit(solution)/shard_map/all_to_all | solution.py:578
  64.3 1.3 collective-permute-done.other_ref.first_ref
  65.5 0.6 pass_on.1
  66.1 0.2 collective-permute-start.10
  66.3 0.4 collective-permute-start.11
  66.6 1.6 copy-done.2
  68.2 2.3 %project.1 = bf16[2,8,64,256]{3,2,1,0:T(8,128)(2,1)} custom-call(s32[1]{0:T(128)} %bitcast.1.core_ref, bf16[256,128]{1,0:T(8,128)(2,1)S(1)} %bitcast.23, bf16[256,128]{1,0:T(8,128)(2,1)S(1)} %collective-permute-done.other_ref.first_ref, bf16[8,2,512,128]{3,2,1,0:T(8,128)(2,1)S(1)} %bitcast.20), custom_call_target="tpu_custom_call" | custom-call | flops 268435456 | bytes 3145728 | tf_op jit(solution)/shard_map/project/pallas_call | solution.py:290
  70.5 5.9 %all-to-all-start.2 = ((bf16[16,64,256]{2,1,0:T(8,128)(2,1)}), bf16[16,64,256]{2,1,0:T(8,128)(2,1)S(1)}, u32[]{:S(2)}, u32[]{:S(2)}) async-start(bf16[16,64,256]{2,1,0:T(8,128)(2,1)} %bitcast.12), calls=%async_computation.2 | async-start | bytes 1048576 | tf_op jit(solution)/shard_map/all_to_all | solution.py:586
  76.4 0.1 copy.21.ids_ref
  76.5 0.1 copy.20.router_ref
  76.7 9.6 %all-to-all-done.2.part_ref = bf16[16,64,256]{2,1,0:T(8,128)(2,1)S(1)} async-done(((bf16[16,64,256]{2,1,0:T(8,128)(2,1)}), bf16[16,64,256]{2,1,0:T(8,128)(2,1)S(1)}, u32[]{:S(2)}, u32[]{:S(2)}) %all-to-all-start.2) | async-done | bytes 524320 | tf_op jit(solution)/shard_map/all_to_all | solution.py:586
  86.3 1.5 dispatch.1
  87.7 4.3 %all-to-all-start.3 = ((bf16[16,18,640]{2,1,0:T(8,128)(2,1)}), bf16[16,18,640]{2,1,0:T(8,128)(2,1)S(1)}, u32[]{:S(2)}, u32[]{:S(2)}) async-start(bf16[16,18,640]{2,1,0:T(8,128)(2,1)} %get-tuple-element.28.after_ref), calls=%async_computation.3 | async-start | bytes 983040 | tf_op jit(solution)/shard_map/all_to_all | solution.py:599
  92.1 2.7 %write_cycle.1 = (bf16[8192,128]{1,0:T(8,128)(2,1)}, f32[8,128]{1,0:T(8,128)S(1)}) custom-call(s32[1]{0:T(128)} %bitcast.2.seq_ref, s32[32]{0:T(128)S(1)} %copy-done.14, bf16[128,128]{1,0:T(8,128)(2,1)S(1)} %get-tuple-element.29.new_ref, bf16[8192,128]{1,0:T(8,128)(2,1)S(1)} %bitcast.18, bf16[16,18,640]{2,1,0:T(8,128)(2,1)} %get-tuple-element.28.after_ref), custom_call_target="tpu_custom_call" | custom-call | flops 16777216 | bytes 16777216 | tf_op jit(solution)/shard_map/write_cycle/pallas_call | solution.py:210
  94.7 7.0 %all-to-all-done.3.got_ref = bf16[16,18,640]{2,1,0:T(8,128)(2,1)S(1)} async-done(((bf16[16,18,640]{2,1,0:T(8,128)(2,1)}), bf16[16,18,640]{2,1,0:T(8,128)(2,1)S(1)}, u32[]{:S(2)}, u32[]{:S(2)}) %all-to-all-start.3) | async-done | bytes 368672 | tf_op jit(solution)/shard_map/all_to_all | solution.py:599
  101.7 1.0 norm.1
  102.7 0.1 collective-permute-start.5
  102.8 2.0 collective-permute-start.2
  104.8 6.0 %collective-permute-done.5.refs_4_ = bf16[144,1024]{1,0:T(8,128)(2,1)S(1)} collective-permute-done((bf16[144,1024]{1,0:T(8,128)(2,1)S(1)}, bf16[144,1024]{1,0:T(8,128)(2,1)S(1)}, u32[]{:S(2)}, u32[]{:S(2)}) %collective-permute-start.5) | collective-permute-done | bytes 294944 | tf_op jit(solution)/shard_map/ppermute | solution.py:614
  110.8 1.5 collective-permute-start.6
  112.3 0.5 collective-permute-start.3
  112.9 5.1 %collective-permute-done.6.refs_5_ = bf16[144,1024]{1,0:T(8,128)(2,1)S(1)} collective-permute-done((bf16[144,1024]{1,0:T(8,128)(2,1)S(1)}, bf16[144,1024]{1,0:T(8,128)(2,1)S(1)}, u32[]{:S(2)}, u32[]{:S(2)}) %collective-permute-start.6) | collective-permute-done | bytes 294944 | tf_op jit(solution)/shard_map/ppermute | solution.py:614
  118.0 2.9 %collective-permute-start.7 = (bf16[144,1024]{1,0:T(8,128)(2,1)S(1)}, bf16[144,1024]{1,0:T(8,128)(2,1)S(1)}, u32[]{:S(2)}, u32[]{:S(2)}) collective-permute-start(bf16[144,1024]{1,0:T(8,128)(2,1)S(1)} %collective-permute-done.6.refs_5_), channel_id=1, source_target_pairs={{0,112},{16,0},{32,16},{48,32},{64,48},{80,64},{96,80},{112,96},{1... | collective-permute-start | bytes 884744 | tf_op jit(solution)/shard_map/ppermute | solution.py:614
  121.0 4.2 %collective-permute-done.7.refs_6_ = bf16[144,1024]{1,0:T(8,128)(2,1)S(1)} collective-permute-done((bf16[144,1024]{1,0:T(8,128)(2,1)S(1)}, bf16[144,1024]{1,0:T(8,128)(2,1)S(1)}, u32[]{:S(2)}, u32[]{:S(2)}) %collective-permute-start.7) | collective-permute-done | bytes 294944 | tf_op jit(solution)/shard_map/ppermute | solution.py:614
  125.2 3.8 %collective-permute-start.9 = (bf16[144,512]{1,0:T(8,128)(2,1)S(1)}, bf16[144,512]{1,0:T(8,128)(2,1)S(1)}, u32[]{:S(2)}, u32[]{:S(2)}) collective-permute-start(bf16[144,512]{1,0:T(8,128)(2,1)S(1)} %slice.33), channel_id=1, source_target_pairs={{0,112},{16,0},{32,16},{48,32},{64,48},{80,64},{96,80},{112,96},{1... | collective-permute-start | bytes 442376 | tf_op jit(solution)/shard_map/ppermute | solution.py:616
  129.0 0.1 collective-permute-start.8
  129.1 2.5 %collective-permute-done.9.refs_8_ = bf16[144,512]{1,0:T(8,128)(2,1)S(1)} collective-permute-done((bf16[144,512]{1,0:T(8,128)(2,1)S(1)}, bf16[144,512]{1,0:T(8,128)(2,1)S(1)}, u32[]{:S(2)}, u32[]{:S(2)}) %collective-permute-start.9) | collective-permute-done | bytes 147488 | tf_op jit(solution)/shard_map/ppermute | solution.py:616
  131.6 3.8 %collective-permute-done.8.refs_7_ = bf16[144,512]{1,0:T(8,128)(2,1)S(1)} collective-permute-done((bf16[144,512]{1,0:T(8,128)(2,1)S(1)}, bf16[144,512]{1,0:T(8,128)(2,1)S(1)}, u32[]{:S(2)}, u32[]{:S(2)}) %collective-permute-start.8) | collective-permute-done | bytes 147488 | tf_op jit(solution)/shard_map/ppermute | solution.py:615
  135.4 9.5 %expert.1 = (bf16[144,1024]{1,0:T(8,128)(2,1)S(1)}, bf16[144,1024]{1,0:T(8,128)(2,1)S(1)}, bf16[144,1024]{1,0:T(8,128)(2,1)S(1)}, bf16[144,1024]{1,0:T(8,128)(2,...) custom-call(bf16[144,1024]{1,0:T(8,128)(2,1)S(1)} %get-tuple-element, ...), custom_call_target="tpu_custom_call" | custom-call | flops 4294967296 | bytes 14680064 | tf_op jit(solution)/shard_map/expert/pallas_call | solution.py:471
  145.0 0.1 collective-permute-start.12
  145.1 3.3 %collective-permute-start.16 = (bf16[144,512]{1,0:T(8,128)(2,1)S(1)}, bf16[144,512]{1,0:T(8,128)(2,1)S(1)}, u32[]{:S(2)}, u32[]{:S(2)}) collective-permute-start(bf16[144,512]{1,0:T(8,128)(2,1)S(1)} %get-tuple-element.44), channel_id=1, source_target_pairs={{0,112},{16,0},{32,16},{48,32},{64,48},{80,64},{96,80},{112,96},{1... | collective-permute-start | bytes 442376 | tf_op jit(solution)/shard_map/ppermute | solution.py:629
  148.4 4.5 %collective-permute-done.12 = bf16[144,512]{1,0:T(8,128)(2,1)S(1)} collective-permute-done((bf16[144,512]{1,0:T(8,128)(2,1)S(1)}, bf16[144,512]{1,0:T(8,128)(2,1)S(1)}, u32[]{:S(2)}, u32[]{:S(2)}) %collective-permute-start.12) | collective-permute-done | bytes 147488 | tf_op jit(solution)/shard_map/ppermute | solution.py:628
  153.0 0.1 collective-permute-start.13
  153.2 3.3 %collective-permute-start.17 = (bf16[144,1024]{1,0:T(8,128)(2,1)S(1)}, bf16[144,1024]{1,0:T(8,128)(2,1)S(1)}, u32[]{:S(2)}, u32[]{:S(2)}) collective-permute-start(bf16[144,1024]{1,0:T(8,128)(2,1)S(1)} %pad_maximum_fusion.1), channel_id=1, source_target_pairs={{0,112},{16,0},{32,16},{48,32},{64,48},{80,64},{96,80},{112,96},{1... | collective-permute-start | bytes 884744 | tf_op jit(solution)/shard_map/ppermute | solution.py:636
  156.5 7.6 %collective-permute-done.13 = bf16[144,1024]{1,0:T(8,128)(2,1)S(1)} collective-permute-done((bf16[144,1024]{1,0:T(8,128)(2,1)S(1)}, bf16[144,1024]{1,0:T(8,128)(2,1)S(1)}, u32[]{:S(2)}, u32[]{:S(2)}) %collective-permute-start.13) | collective-permute-done | bytes 294944 | tf_op jit(solution)/shard_map/ppermute | solution.py:635
  164.1 0.1 add_convert_fusion.3
  164.1 0.1 collective-permute-start.14
  164.2 0.1 add_convert_fusion.1
  164.3 3.5 %collective-permute-start.18 = (bf16[144,1024]{1,0:T(8,128)(2,1)S(1)}, bf16[144,1024]{1,0:T(8,128)(2,1)S(1)}, u32[]{:S(2)}, u32[]{:S(2)}) collective-permute-start(bf16[144,1024]{1,0:T(8,128)(2,1)S(1)} %add_convert_fusion.1), channel_id=1, source_target_pairs={{0,112},{16,0},{32,16},{48,32},{64,48},{80,64},{96,80},{112,96},{1... | collective-permute-start | bytes 884744 | tf_op jit(solution)/shard_map/ppermute | solution.py:636
  167.8 6.5 %collective-permute-done.14 = bf16[144,1024]{1,0:T(8,128)(2,1)S(1)} collective-permute-done((bf16[144,1024]{1,0:T(8,128)(2,1)S(1)}, bf16[144,1024]{1,0:T(8,128)(2,1)S(1)}, u32[]{:S(2)}, u32[]{:S(2)}) %collective-permute-start.14) | collective-permute-done | bytes 294944 | tf_op jit(solution)/shard_map/ppermute | solution.py:635
  174.3 0.1 add_convert_fusion.2
  174.4 0.1 collective-permute-start.15
  174.5 0.1 add_convert_fusion
  174.6 3.3 %collective-permute-start.19 = (bf16[144,1024]{1,0:T(8,128)(2,1)S(1)}, bf16[144,1024]{1,0:T(8,128)(2,1)S(1)}, u32[]{:S(2)}, u32[]{:S(2)}) collective-permute-start(bf16[144,1024]{1,0:T(8,128)(2,1)S(1)} %add_convert_fusion), channel_id=1, source_target_pairs={{0,112},{16,0},{32,16},{48,32},{64,48},{80,64},{96,80},{112,96},{1... | collective-permute-start | bytes 884744 | tf_op jit(solution)/shard_map/ppermute | solution.py:638
  177.9 4.5 %collective-permute-done.15.right_ref = bf16[144,1024]{1,0:T(8,128)(2,1)S(1)} collective-permute-done((bf16[144,1024]{1,0:T(8,128)(2,1)S(1)}, bf16[144,1024]{1,0:T(8,128)(2,1)S(1)}, u32[]{:S(2)}, u32[]{:S(2)}) %collective-permute-start.15) | collective-permute-done | bytes 294944 | tf_op jit(solution)/shard_map/ppermute | solution.py:637
  182.4 0.4 gate.1
  182.8 13.7 %all_to_all.38.got_ref = bf16[16,18,512]{2,1,0:T(8,128)(2,1)S(1)} all-to-all(bf16[16,18,512]{2,1,0:T(8,128)(2,1)S(1)} %gate.1), channel_id=1, replica_groups=mesh['xh'=2,'z'=8,'c'=2,'xl'=2,'y'=4] {'xh','xl','y'}, dimensions={0} | all-to-all | bytes 589824 | tf_op jit(solution)/shard_map/all_to_all | solution.py:642
  196.5 1.1 combine.1
  (49 shorter events, 0.3 us)
Async XLA Ops:
  7.2 59.5 %all-gather.3.cloned.1.call-start = ((), (), s32[]{:S(2)}) async-start(), calls=%async_computation.5 | async-start | bytes 2359296 | tf_op jit(solution)/shard_map/all_gather | solution.py:555
  7.2 7.0 %collective-permute-start.1 = (bf16[512,128]{1,0:T(8,128)(2,1)}, bf16[512,128]{1,0:T(8,128)(2,1)S(1)}, u32[]{:S(2)}, u32[]{:S(2)}) collective-permute-start(bf16[512,128]{1,0:T(8,128)(2,1)} %own_ref.1), channel_id=1, source_target_pairs={{0,128},{128,0},{1,129},{129,1},{2,130},{130,2},{3,131},{131,3},{4... | collective-permute-start | bytes 393224 | tf_op jit(solution)/shard_map/ppermute | solution.py:550
  9.4 0.8 copy-start.7
  10.3 0.8 copy-start.9
  11.0 0.7 copy-start.12
  14.2 0.9 copy-start.5
  15.9 23.9 %all-to-all-start = ((bf16[32,16,128]{2,1,0:T(8,128)(2,1)}), bf16[32,16,128]{2,1,0:T(8,128)(2,1)S(1)}, u32[]{:S(2)}, u32[]{:S(2)}) async-start(bf16[32,16,128]{2,1,0:T(8,128)(2,1)} %bitcast.3), calls=%async_computation | async-start | bytes 262144 | tf_op jit(solution)/shard_map/all_to_all | solution.py:548
  26.4 2.2 %copy-start.1 = (bf16[1,4096,2,256]{3,2,1,0:T(2,128)(2,1)S(1)}, bf16[1,4096,2,256]{3,2,1,0:T(2,128)(2,1)}, u32[]{:S(2)}) copy-start(bf16[1,4096,2,256]{3,2,1,0:T(2,128)(2,1)} %param.26) | copy-start | bytes 12582916
  28.5 9.7 %copy-start = (bf16[1,4096,2,128]{3,2,1,0:T(2,128)(2,1)S(1)}, bf16[1,4096,2,128]{3,2,1,0:T(2,128)(2,1)}, u32[]{:S(2)}) copy-start(bf16[1,4096,2,128]{3,2,1,0:T(2,128)(2,1)} %param.16) | copy-start | bytes 6291460
  28.6 11.2 %copy-start.6 = (bf16[32,4,2,128]{3,2,1,0:T(2,128)(2,1)S(1)}, bf16[32,4,2,128]{3,2,1,0:T(2,128)(2,1)}, u32[]{:S(2)}) copy-start(bf16[32,4,2,128]{3,2,1,0:T(2,128)(2,1)} %param.17) | copy-start | bytes 196612
  28.6 11.2 %copy-start.14 = (s32[32]{0:T(128)S(1)}, s32[32]{0:T(128)}, u32[]{:S(2)}) copy-start(s32[32]{0:T(128)} %off_ref.3) | copy-start | bytes 388
  28.6 11.2 %copy-start.15 = (s32[32]{0:T(128)S(1)}, s32[32]{0:T(128)}, u32[]{:S(2)}) copy-start(s32[32]{0:T(128)} %len_ref.1) | copy-start | bytes 388
  38.8 1.0 copy-start.3
  39.8 1.2 copy-start.4
  43.9 32.6 %copy-start.10 = (s32[2,32,2]{1,2,0:T(2,128)S(1)}, s32[2,32,2]{1,2,0:T(2,128)}, u32[]{:S(2)}) copy-start(s32[2,32,2]{1,2,0:T(2,128)} %param.25) | copy-start | bytes 1540
  43.9 32.6 %copy-start.16 = (f32[512,8]{0,1:T(8,128)S(1)}, f32[512,8]{0,1:T(8,128)}, u32[]{:S(2)}) copy-start(f32[512,8]{0,1:T(8,128)} %param.24) | copy-start | bytes 49156
  64.3 1.3 collective-permute-start
  65.5 20.7 %copy-start.8 = (bf16[2,32,512]{2,1,0:T(8,128)(2,1)S(1)}, bf16[2,32,512]{2,1,0:T(8,128)(2,1)}, u32[]{:S(2)}) copy-start(bf16[2,32,512]{2,1,0:T(8,128)(2,1)} %res_ref.1) | copy-start | bytes 196612
  65.5 20.7 %copy-start.11 = (f32[512]{0:T(512)S(1)}, f32[512]{0:T(512)}, u32[]{:S(2)}) copy-start(f32[512]{0:T(512)} %param.23) | copy-start | bytes 6148
  65.5 20.7 %copy-start.13 = (s32[32]{0:T(128)S(1)}, s32[32]{0:T(128)}, u32[]{:S(2)}) copy-start(s32[32]{0:T(128)} %param.20) | copy-start | bytes 388
  66.1 63.0 %collective-permute-start.10 = (bf16[2,4096,256]{2,1,0:T(8,128)(2,1)}, bf16[2,4096,256]{2,1,0:T(8,128)(2,1)}, u32[]{:S(2)}, u32[]{:S(2)}) collective-permute-start(bf16[2,4096,256]{2,1,0:T(8,128)(2,1)} %get-tuple-element.33.refs_9_), channel_id=1, source_target_pairs={{0,8},{8,0},{1,9},{9,1},{2,10},{10,2},{3,11},{11,3},{4,12},{12,4},... | collective-permute-start | bytes 12582920 | tf_op jit(solution)/shard_map/ppermute | solution.py:584
  66.3 62.8 %collective-permute-start.11 = (bf16[256,4096]{1,0:T(8,128)(2,1)}, bf16[256,4096]{1,0:T(8,128)(2,1)}, u32[]{:S(2)}, u32[]{:S(2)}) collective-permute-start(bf16[256,4096]{1,0:T(8,128)(2,1)} %bitcast.15.refs_11_), channel_id=1, source_target_pairs={{0,8},{8,0},{1,9},{9,1},{2,10},{10,2},{3,11},{11,3},{4,12},{12,4},... | collective-permute-start | bytes 6291464 | tf_op jit(solution)/shard_map/ppermute | solution.py:580
  66.6 1.6 copy-start.2
  70.5 15.8 %all-to-all-start.2 = ((bf16[16,64,256]{2,1,0:T(8,128)(2,1)}), bf16[16,64,256]{2,1,0:T(8,128)(2,1)S(1)}, u32[]{:S(2)}, u32[]{:S(2)}) async-start(bf16[16,64,256]{2,1,0:T(8,128)(2,1)} %bitcast.12), calls=%async_computation.2 | async-start | bytes 1048576 | tf_op jit(solution)/shard_map/all_to_all | solution.py:586
  87.7 14.0 %all-to-all-start.3 = ((bf16[16,18,640]{2,1,0:T(8,128)(2,1)}), bf16[16,18,640]{2,1,0:T(8,128)(2,1)S(1)}, u32[]{:S(2)}, u32[]{:S(2)}) async-start(bf16[16,18,640]{2,1,0:T(8,128)(2,1)} %get-tuple-element.28.after_ref), calls=%async_computation.3 | async-start | bytes 983040 | tf_op jit(solution)/shard_map/all_to_all | solution.py:599
  102.7 8.1 %collective-permute-start.5 = (bf16[144,1024]{1,0:T(8,128)(2,1)S(1)}, bf16[144,1024]{1,0:T(8,128)(2,1)S(1)}, u32[]{:S(2)}, u32[]{:S(2)}) collective-permute-start(bf16[144,1024]{1,0:T(8,128)(2,1)S(1)} %get-tuple-element.31.refs_0_), channel_id=1, source_target_pairs={{0,112},{16,0},{32,16},{48,32},{64,48},{80,64},{96,80},{112,96},{1... | collective-permute-start | bytes 884744 | tf_op jit(solution)/shard_map/ppermute | solution.py:614
  102.8 9.5 %collective-permute-start.2 = (bf16[144,1024]{1,0:T(8,128)(2,1)S(1)}, bf16[144,1024]{1,0:T(8,128)(2,1)S(1)}, u32[]{:S(2)}, u32[]{:S(2)}) collective-permute-start(bf16[144,1024]{1,0:T(8,128)(2,1)S(1)} %get-tuple-element.31.refs_0_), channel_id=1, source_target_pairs={{0,16},{16,32},{32,48},{48,64},{64,80},{80,96},{96,112},{112,0},{1... | collective-permute-start | bytes 884744 | tf_op jit(solution)/shard_map/ppermute | solution.py:613
  110.8 7.2 %collective-permute-start.6 = (bf16[144,1024]{1,0:T(8,128)(2,1)S(1)}, bf16[144,1024]{1,0:T(8,128)(2,1)S(1)}, u32[]{:S(2)}, u32[]{:S(2)}) collective-permute-start(bf16[144,1024]{1,0:T(8,128)(2,1)S(1)} %collective-permute-done.5.refs_4_), channel_id=1, source_target_pairs={{0,112},{16,0},{32,16},{48,32},{64,48},{80,64},{96,80},{112,96},{1... | collective-permute-start | bytes 884744 | tf_op jit(solution)/shard_map/ppermute | solution.py:614
  112.3 8.6 %collective-permute-start.3 = (bf16[144,1024]{1,0:T(8,128)(2,1)S(1)}, bf16[144,1024]{1,0:T(8,128)(2,1)S(1)}, u32[]{:S(2)}, u32[]{:S(2)}) collective-permute-start(bf16[144,1024]{1,0:T(8,128)(2,1)S(1)} %collective-permute-done.2.refs_1_), channel_id=1, source_target_pairs={{0,16},{16,32},{32,48},{48,64},{64,80},{80,96},{96,112},{112,0},{1... | collective-permute-start | bytes 884744 | tf_op jit(solution)/shard_map/ppermute | solution.py:613
  118.0 7.2 %collective-permute-start.7 = (bf16[144,1024]{1,0:T(8,128)(2,1)S(1)}, bf16[144,1024]{1,0:T(8,128)(2,1)S(1)}, u32[]{:S(2)}, u32[]{:S(2)}) collective-permute-start(bf16[144,1024]{1,0:T(8,128)(2,1)S(1)} %collective-permute-done.6.refs_5_), channel_id=1, source_target_pairs={{0,112},{16,0},{32,16},{48,32},{64,48},{80,64},{96,80},{112,96},{1... | collective-permute-start | bytes 884744 | tf_op jit(solution)/shard_map/ppermute | solution.py:614
  120.9 8.0 %collective-permute-start.4 = (bf16[144,1024]{1,0:T(8,128)(2,1)S(1)}, bf16[144,1024]{1,0:T(8,128)(2,1)S(1)}, u32[]{:S(2)}, u32[]{:S(2)}) collective-permute-start(bf16[144,1024]{1,0:T(8,128)(2,1)S(1)} %collective-permute-done.3.refs_2_), channel_id=1, source_target_pairs={{0,16},{16,32},{32,48},{48,64},{64,80},{80,96},{96,112},{112,0},{1... | collective-permute-start | bytes 884744 | tf_op jit(solution)/shard_map/ppermute | solution.py:613
  125.2 6.4 %collective-permute-start.9 = (bf16[144,512]{1,0:T(8,128)(2,1)S(1)}, bf16[144,512]{1,0:T(8,128)(2,1)S(1)}, u32[]{:S(2)}, u32[]{:S(2)}) collective-permute-start(bf16[144,512]{1,0:T(8,128)(2,1)S(1)} %slice.33), channel_id=1, source_target_pairs={{0,112},{16,0},{32,16},{48,32},{64,48},{80,64},{96,80},{112,96},{1... | collective-permute-start | bytes 442376 | tf_op jit(solution)/shard_map/ppermute | solution.py:616
  129.0 6.4 %collective-permute-start.8 = (bf16[144,512]{1,0:T(8,128)(2,1)S(1)}, bf16[144,512]{1,0:T(8,128)(2,1)S(1)}, u32[]{:S(2)}, u32[]{:S(2)}) collective-permute-start(bf16[144,512]{1,0:T(8,128)(2,1)S(1)} %slice.32), channel_id=1, source_target_pairs={{0,16},{16,32},{32,48},{48,64},{64,80},{80,96},{96,112},{112,0},{1... | collective-permute-start | bytes 442376 | tf_op jit(solution)/shard_map/ppermute | solution.py:615
  145.0 8.0 %collective-permute-start.12 = (bf16[144,512]{1,0:T(8,128)(2,1)S(1)}, bf16[144,512]{1,0:T(8,128)(2,1)S(1)}, u32[]{:S(2)}, u32[]{:S(2)}) collective-permute-start(bf16[144,512]{1,0:T(8,128)(2,1)S(1)} %get-tuple-element.45), channel_id=1, source_target_pairs={{0,16},{16,32},{32,48},{48,64},{64,80},{80,96},{96,112},{112,0},{1... | collective-permute-start | bytes 442376 | tf_op jit(solution)/shard_map/ppermute | solution.py:628
  145.1 8.0 %collective-permute-start.16 = (bf16[144,512]{1,0:T(8,128)(2,1)S(1)}, bf16[144,512]{1,0:T(8,128)(2,1)S(1)}, u32[]{:S(2)}, u32[]{:S(2)}) collective-permute-start(bf16[144,512]{1,0:T(8,128)(2,1)S(1)} %get-tuple-element.44), channel_id=1, source_target_pairs={{0,112},{16,0},{32,16},{48,32},{64,48},{80,64},{96,80},{112,96},{1... | collective-permute-start | bytes 442376 | tf_op jit(solution)/shard_map/ppermute | solution.py:629
  153.0 11.0 %collective-permute-start.13 = (bf16[144,1024]{1,0:T(8,128)(2,1)S(1)}, bf16[144,1024]{1,0:T(8,128)(2,1)S(1)}, u32[]{:S(2)}, u32[]{:S(2)}) collective-permute-start(bf16[144,1024]{1,0:T(8,128)(2,1)S(1)} %pad_maximum_fusion), channel_id=1, source_target_pairs={{0,16},{16,32},{32,48},{48,64},{64,80},{80,96},{96,112},{112,0},{1... | collective-permute-start | bytes 884744 | tf_op jit(solution)/shard_map/ppermute | solution.py:635
  153.2 11.0 %collective-permute-start.17 = (bf16[144,1024]{1,0:T(8,128)(2,1)S(1)}, bf16[144,1024]{1,0:T(8,128)(2,1)S(1)}, u32[]{:S(2)}, u32[]{:S(2)}) collective-permute-start(bf16[144,1024]{1,0:T(8,128)(2,1)S(1)} %pad_maximum_fusion.1), channel_id=1, source_target_pairs={{0,112},{16,0},{32,16},{48,32},{64,48},{80,64},{96,80},{112,96},{1... | collective-permute-start | bytes 884744 | tf_op jit(solution)/shard_map/ppermute | solution.py:636
  164.1 10.2 %collective-permute-start.14 = (bf16[144,1024]{1,0:T(8,128)(2,1)S(1)}, bf16[144,1024]{1,0:T(8,128)(2,1)S(1)}, u32[]{:S(2)}, u32[]{:S(2)}) collective-permute-start(bf16[144,1024]{1,0:T(8,128)(2,1)S(1)} %add_convert_fusion.3), channel_id=1, source_target_pairs={{0,16},{16,32},{32,48},{48,64},{64,80},{80,96},{96,112},{112,0},{1... | collective-permute-start | bytes 884744 | tf_op jit(solution)/shard_map/ppermute | solution.py:635
  164.3 10.2 %collective-permute-start.18 = (bf16[144,1024]{1,0:T(8,128)(2,1)S(1)}, bf16[144,1024]{1,0:T(8,128)(2,1)S(1)}, u32[]{:S(2)}, u32[]{:S(2)}) collective-permute-start(bf16[144,1024]{1,0:T(8,128)(2,1)S(1)} %add_convert_fusion.1), channel_id=1, source_target_pairs={{0,112},{16,0},{32,16},{48,32},{64,48},{80,64},{96,80},{112,96},{1... | collective-permute-start | bytes 884744 | tf_op jit(solution)/shard_map/ppermute | solution.py:636
  174.4 8.0 %collective-permute-start.15 = (bf16[144,1024]{1,0:T(8,128)(2,1)S(1)}, bf16[144,1024]{1,0:T(8,128)(2,1)S(1)}, u32[]{:S(2)}, u32[]{:S(2)}) collective-permute-start(bf16[144,1024]{1,0:T(8,128)(2,1)S(1)} %add_convert_fusion.2), channel_id=1, source_target_pairs={{0,16},{16,32},{32,48},{48,64},{64,80},{80,96},{96,112},{112,0},{1... | collective-permute-start | bytes 884744 | tf_op jit(solution)/shard_map/ppermute | solution.py:637
  174.6 7.8 %collective-permute-start.19 = (bf16[144,1024]{1,0:T(8,128)(2,1)S(1)}, bf16[144,1024]{1,0:T(8,128)(2,1)S(1)}, u32[]{:S(2)}, u32[]{:S(2)}) collective-permute-start(bf16[144,1024]{1,0:T(8,128)(2,1)S(1)} %add_convert_fusion), channel_id=1, source_target_pairs={{0,112},{16,0},{32,16},{48,32},{64,48},{80,64},{96,80},{112,96},{1... | collective-permute-start | bytes 884744 | tf_op jit(solution)/shard_map/ppermute | solution.py:638
Sparse Core Ops, SparseCore 0:
  16.0 44.6 all-gather.2
